TPU v7x, 256 devices: a whole 4x4x8 slice. The times are simulated.
256 devices in a mesh: section: 16 (over x, z_hi), head: 16 (over y, z_lo, core).
Axes of the slice: x: 4, y: 4, z: 8 (z_hi: 4, z_lo: 2; z = z_hi * 2 + z_lo), core: 2. Of those that a mesh axis runs over, the one named last changes fastest.
Arguments:
- qkv: bfloat16 [16, 288, 3, 6144], P('section', 'head'), may hold values from -160 to 160
- stale_kv: bfloat16 [16, 4608, 2, 6144], P('section', None, None, 'head'), may hold values from -6 to 6
- out_weight: bfloat16 [16, 6144, 6144], P('section', 'head'), may hold values from -0.3125 to 0.3125
- residual: bfloat16 [16, 288, 6144], P('section', 'head'), may hold values from -6 to 6
- gate: float32 [16, 6144], P('section'), may hold values from 0.5 to 2
- patch_of_section: int32 [16], P('section'), may hold values from 0 to 15, each once
Outputs:
- handed: bfloat16 [16, 288, 6144], P('section', 'head')
All inputs are finite; a program needn't handle non-finite values.
Results may differ from a plain program's by a relative error of at most 0.023.
Values may be sent and summed in bfloat16 or wider, within the bound.
No kernel may reach another device: no remote copies, remote signals or barrier semaphores. Data moves between devices by JAX's collectives and lax.ppermute only.
A program may use at most 128 MiB of HBM per device.

v0:
```python
import jax
import jax.numpy as jnp
from jax import lax
from jax.sharding import PartitionSpec as P

HD = 128


def shifted(block, axis, distance):
    devices = range(lax.axis_size(axis))
    route = [((i - distance) % len(devices), i) for i in devices]
    return lax.ppermute(block, axis, route)


def shards(qkv, stale_kv, out_weight, residual, gate, patch_of_section):
    groups = lax.axis_size("head")
    tok_here = qkv.shape[1]
    patch_rows = tok_here * groups
    heads_here = stale_kv.shape[3] // HD
    key_count = stale_kv.shape[1]
    blocked = qkv[0].reshape(tok_here, 3, groups, heads_here, HD)
    history = stale_kv[0].reshape(key_count, 2, heads_here, HD)
    own_start = patch_of_section[0] * patch_rows
    inv_root = 1.0 / HD**0.5
    positions = jnp.arange(key_count, dtype=jnp.int32)
    replaced = (positions >= own_start) & (positions < own_start + patch_rows)
    arrived = lax.all_to_all(blocked, "head", split_axis=2, concat_axis=0, tiled=True)
    queries = arrived[:, 0, 0]
    fresh_keys = arrived[:, 1, 0]
    fresh_values = arrived[:, 2, 0]
    raw = (
        jnp.einsum("qhd,khd->hqk", queries, history[:, 0], preferred_element_type=jnp.float32)
        * inv_root
    )
    distant = jnp.where(replaced[None, None, :], -1e30, raw)
    nearby = (
        jnp.einsum("qhd,khd->hqk", queries, fresh_keys, preferred_element_type=jnp.float32)
        * inv_root
    )
    highest = jnp.maximum(jnp.max(distant, axis=-1), jnp.max(nearby, axis=-1))[..., None]
    distant_exp = jnp.exp(distant - highest)
    nearby_exp = jnp.exp(nearby - highest)
    denominator = jnp.sum(distant_exp, axis=-1, keepdims=True) + jnp.sum(
        nearby_exp, axis=-1, keepdims=True
    )
    distant_w = (distant_exp / denominator).astype(jnp.bfloat16)
    nearby_w = (nearby_exp / denominator).astype(jnp.bfloat16)
    attended = jnp.einsum(
        "hqk,khd->qhd", distant_w, history[:, 1], preferred_element_type=jnp.float32
    )
    attended = attended + jnp.einsum(
        "hqk,khd->qhd", nearby_w, fresh_values, preferred_element_type=jnp.float32
    )
    attended = attended.astype(jnp.bfloat16).reshape(patch_rows, heads_here * HD)
    weight = out_weight[0]
    partial_value = jnp.dot(attended, weight, preferred_element_type=jnp.float32)
    summed = lax.psum_scatter(
        partial_value.astype(jnp.bfloat16), "head", scatter_dimension=0, tiled=True
    ).astype(jnp.float32)
    updated = (residual[0].astype(jnp.float32) + gate[0][None, :] * summed).astype(jnp.bfloat16)
    handed = shifted(updated, "section", 1)
    return handed[None]


def solution(mesh):
    placed = (
        P("section", "head", None, None),
        P("section", None, None, "head"),
        P("section", "head", None),
        P("section", "head", None),
        P("section", None),
        P("section"),
    )
    return jax.shard_map(
        shards, mesh=mesh, in_specs=placed, out_specs=P("section", "head", None), check_vma=False
    )
```

profile of v0, /device:TPU:9, one launch (start us, length us, event | category | flops | bytes accessed | tf_op | source)
XLA Modules:
  0.0 167.7 jit_solution(7202157487577409992)
XLA Ops:
  0.0 2.6 %reshape.27 = bf16[18,3,16,3,128]{4,3,2,1,0:T(4,128)(2,1)S(1)} reshape(bf16[1,18,3,6144]{3,2,1,0:T(4,128)(2,1)} %param.6) | data formatting | bytes 1327104 | tf_op jit(solution)/shard_map/reshape;squeeze | solution.py:21
  2.6 1.2 copy.20
  3.8 6.6 %all-to-all-start = ((bf16[18,3,16,3,128]{4,3,0,1,2:T(4,128)(2,1)}), bf16[18,3,16,3,128]{4,3,0,1,2:T(4,128)(2,1)S(1)}, u32[]{:S(2)}, u32[]{:S(2)}) async-start(bf16[18,3,16,3,128]{4,3,0,1,2:T(4,128)(2,1)} %copy.20), calls=%async_computation | async-start | bytes 1769472 | tf_op jit(solution)/shard_map/all_to_all | solution.py:27
  11.0 18.0 %copy.23 = bf16[1,4608,2,384]{1,3,2,0:T(8,128)(2,1)} copy(bf16[1,4608,2,384]{3,2,1,0:T(2,128)(2,1)} %param.7) | data formatting | bytes 14155776 | tf_op args[1]
  29.1 0.0 all-to-all-done
  29.1 0.2 copy.21
  29.3 0.2 all_to_all.16
  29.5 0.0 slice-start
  29.5 1.4 fusion.15
  30.9 0.0 slice-start.1
  30.9 10.5 %fusion.1 = (f32[3,288]{1,0:T(4,128)S(1)}, f32[3,288,4608]{2,1,0:T(8,128)}) fusion(pred[4608]{0:T(1024)(128)(4,1)S(1)} %fusion.12, bf16[4608,2,3,128]{0,3,2,1:T(8,128)(2,1)} %bitcast.53, bf16[288,3,1,3,128]{4,0,3,2,1:T(8,128)(2,1)S(1)} %bitcast.59), kind=kOutput, calls=%fused_computation.3 | convolution fusion | flops 1031158912 | bytes 19693952 | tf_op jit(solution)/shard_map/qhd,khd->hqk/dot_general | solution.py:32
  41.4 9.1 %fusion.2 = f32[3,288]{1,0:T(4,128)S(1)} fusion(f32[3,288,4608]{2,1,0:T(8,128)} %get-tuple-element.6, f32[3,288]{1,0:T(4,128)S(1)} %max.7, pred[4608]{0:T(1024)(128)(4,1)S(1)} %fusion.12), kind=kLoop, calls=%fused_computation.4 | loop fusion | flops 15924384 | bytes 15936768 | tf_op jit(solution)/shard_map/reduce_sum | solution.py:43
  50.5 1.5 fusion.7
  52.0 0.0 slice-done
  52.0 0.0 slice-done.1
  52.0 0.0 copy-start
  52.0 7.9 %fusion.3 = f32[3,288,128]{2,1,0:T(8,128)S(1)} fusion(f32[3,288,4608]{2,1,0:T(8,128)} %get-tuple-element.6, f32[3,288]{1,0:T(4,128)S(1)} %add.21, f32[3,288]{1,0:T(4,128)S(1)} %max.7, pred[4608]{0:T(1024)(128)(4,1)S(1)} %fusion.12, bf16[4608,2,3,128]{0,3,2,1:T(8,128)(2,1)S(1)} %bitcast.56), kind=kOutput, calls=%fused_computation.5 | convolution fusion | flops 1039122432 | bytes 19923968 | tf_op jit(solution)/shard_map/hqk,khd->qhd/dot_general | solution.py:48
  59.9 0.0 copy-done
  59.9 0.5 fusion.8
  60.4 0.0 copy-start.1
  60.4 4.3 %convolution_convert_fusion = bf16[288,6144]{1,0:T(8,128)(2,1)S(1)} fusion(bf16[1,384,6144]{2,1,0:T(8,128)(2,1)} %param.8, bf16[3,36,8,128]{3,2,1,0:T(8,128)(2,1)S(1)} %fusion.8), kind=kOutput, calls=%fused_computation.6 | convolution fusion | flops 1360723968 | bytes 8478720 | tf_op jit(solution)/shard_map/dot_general | solution.py:56
  64.8 52.5 %fusion = bf16[24,6144]{1,0:T(8,128)(2,1)} fusion(bf16[288,6144]{1,0:T(8,128)(2,1)S(1)} %convolution_convert_fusion), kind=kCustom, calls=%all-reduce-scatter | all-reduce-scatter fusion | flops 2359297 | bytes 3834880
  117.3 4.3 %collective-permute-start.1 = (bf16[24,6144]{1,0:T(8,128)(2,1)}, bf16[24,6144]{1,0:T(8,128)(2,1)S(1)}, u32[]{:S(2)}, u32[]{:S(2)}) collective-permute-start(bf16[24,6144]{1,0:T(8,128)(2,1)} %fusion), channel_id=1, source_target_pairs={{0,1},{1,2},{2,3},{3,4},{4,5},{5,6},{6,7},{7,8},{8,9},{9,10},{10,1... | collective-permute-start | bytes 884744
  121.6 4.3 %collective-permute-start.2 = (bf16[24,6144]{1,0:T(8,128)(2,1)}, bf16[24,6144]{1,0:T(8,128)(2,1)S(1)}, u32[]{:S(2)}, u32[]{:S(2)}) collective-permute-start(bf16[24,6144]{1,0:T(8,128)(2,1)} %fusion), channel_id=1, source_target_pairs={{0,2},{1,3},{2,4},{3,5},{4,6},{5,7},{6,8},{7,9},{8,10},{9,11},{10,... | collective-permute-start | bytes 884744
  126.0 1.9 %collective-permute-start.3 = (bf16[24,6144]{1,0:T(8,128)(2,1)}, bf16[24,6144]{1,0:T(8,128)(2,1)S(1)}, u32[]{:S(2)}, u32[]{:S(2)}) collective-permute-start(bf16[24,6144]{1,0:T(8,128)(2,1)} %fusion), channel_id=1, source_target_pairs={{0,3},{1,4},{2,5},{3,6},{4,7},{5,8},{6,9},{7,10},{8,11},{9,12},{10... | collective-permute-start | bytes 884744
  127.9 1.0 slice.25
  128.9 3.0 %collective-permute-start.4 = (bf16[18,6144]{1,0:T(8,128)(2,1)S(1)}, bf16[18,6144]{1,0:T(8,128)(2,1)S(1)}, u32[]{:S(2)}, u32[]{:S(2)}) collective-permute-start(bf16[18,6144]{1,0:T(8,128)(2,1)S(1)} %slice.25), channel_id=1, source_target_pairs={{0,4},{1,5},{2,6},{3,7},{4,8},{5,9},{6,10},{7,11},{8,12},{9,13},{1... | collective-permute-start | bytes 663560
  132.0 0.0 copy-done.1
  132.0 0.6 dynamic-slice.4
  133.1 14.0 %collective-permute-done.4 = bf16[18,6144]{1,0:T(8,128)(2,1)S(1)} collective-permute-done((bf16[18,6144]{1,0:T(8,128)(2,1)S(1)}, bf16[18,6144]{1,0:T(8,128)(2,1)S(1)}, u32[]{:S(2)}, u32[]{:S(2)}) %collective-permute-start.4) | collective-permute-done | bytes 221216
  147.1 0.0 collective-permute-done.1
  147.1 0.0 collective-permute-done.2
  147.1 0.0 collective-permute-done.3
  147.1 4.5 %concatenate = bf16[114,6144]{1,0:T(8,128)(2,1)S(1)} concatenate(bf16[18,6144]{1,0:T(8,128)(2,1)S(1)} %collective-permute-done.4, bf16[24,6144]{1,0:T(8,128)(2,1)S(1)} %collective-permute-done.3, bf16[24,6144]{1,0:T(8,128)(2,1)S(1)} %collective-permute-done.2, bf16[24,6144]{1,0:T(8,128)(2,1)S(1)} %collective-permute-done.1, bf16[24,6144]{1,0:T(8,128)(2,1)} %fusion), dimensions={0} | concatenate | bytes 2801664
  151.7 1.1 fusion.9
  152.8 3.1 %collective-permute-start = (bf16[18,6144]{1,0:T(8,128)(2,1)S(1)}, bf16[18,6144]{1,0:T(8,128)(2,1)S(1)}, u32[]{:S(2)}, u32[]{:S(2)}) collective-permute-start(bf16[18,6144]{1,0:T(8,128)(2,1)S(1)} %fusion.9), channel_id=1, source_target_pairs={{240,0},{0,16},{16,32},{32,48},{48,64},{64,80},{80,96},{96,112},{1... | collective-permute-start | bytes 663560 | tf_op jit(solution)/shard_map/ppermute | solution.py:12
  155.8 11.1 %collective-permute-done = bf16[18,6144]{1,0:T(8,128)(2,1)S(1)} collective-permute-done((bf16[18,6144]{1,0:T(8,128)(2,1)S(1)}, bf16[18,6144]{1,0:T(8,128)(2,1)S(1)}, u32[]{:S(2)}, u32[]{:S(2)}) %collective-permute-start) | collective-permute-done | bytes 221216 | tf_op jit(solution)/shard_map/ppermute | solution.py:12
  166.9 0.7 copy.42
  (4 shorter events, 0.0 us)
Async XLA Ops:
  3.8 25.3 %all-to-all-start = ((bf16[18,3,16,3,128]{4,3,0,1,2:T(4,128)(2,1)}), bf16[18,3,16,3,128]{4,3,0,1,2:T(4,128)(2,1)S(1)}, u32[]{:S(2)}, u32[]{:S(2)}) async-start(bf16[18,3,16,3,128]{4,3,0,1,2:T(4,128)(2,1)} %copy.20), calls=%async_computation | async-start | bytes 1769472 | tf_op jit(solution)/shard_map/all_to_all | solution.py:27
  29.5 22.5 %slice-start = ((s8[7077888]{0:T(1024)(128)(4,1)}), s8[4194304]{0:T(1024)(128)(4,1)S(1)}, s32[]{:S(2)}) async-start(s8[7077888]{0:T(1024)(128)(4,1)} %bitcast.54), calls=%async_computation.1 | async-start | bytes 8388608
  30.9 21.1 %slice-start.1 = ((s8[7077888]{0:T(1024)(128)(4,1)}), s8[2883584]{0:T(1024)(128)(4,1)S(1)}, s32[]{:S(2)}) async-start(s8[7077888]{0:T(1024)(128)(4,1)} %bitcast.54), calls=%async_computation.2 | async-start | bytes 5767168
  52.0 7.9 %copy-start = (f32[3,288,288]{1,2,0:T(8,128)S(1)}, f32[3,288,288]{1,2,0:T(8,128)}, u32[]{:S(2)}) copy-start(f32[3,288,288]{1,2,0:T(8,128)} %get-tuple-element.8) | copy-start | bytes 2985988
  60.4 71.6 %copy-start.1 = (u32[256]{0:T(256)S(1)}, u32[256]{0:T(256)}, u32[]{:S(2)}) copy-start(u32[256]{0:T(256)} %constant.21) | copy-start | bytes 3076
  117.3 29.9 %collective-permute-start.1 = (bf16[24,6144]{1,0:T(8,128)(2,1)}, bf16[24,6144]{1,0:T(8,128)(2,1)S(1)}, u32[]{:S(2)}, u32[]{:S(2)}) collective-permute-start(bf16[24,6144]{1,0:T(8,128)(2,1)} %fusion), channel_id=1, source_target_pairs={{0,1},{1,2},{2,3},{3,4},{4,5},{5,6},{6,7},{7,8},{8,9},{9,10},{10,1... | collective-permute-start | bytes 884744
  121.6 25.5 %collective-permute-start.2 = (bf16[24,6144]{1,0:T(8,128)(2,1)}, bf16[24,6144]{1,0:T(8,128)(2,1)S(1)}, u32[]{:S(2)}, u32[]{:S(2)}) collective-permute-start(bf16[24,6144]{1,0:T(8,128)(2,1)} %fusion), channel_id=1, source_target_pairs={{0,2},{1,3},{2,4},{3,5},{4,6},{5,7},{6,8},{7,9},{8,10},{9,11},{10,... | collective-permute-start | bytes 884744
  126.0 21.2 %collective-permute-start.3 = (bf16[24,6144]{1,0:T(8,128)(2,1)}, bf16[24,6144]{1,0:T(8,128)(2,1)S(1)}, u32[]{:S(2)}, u32[]{:S(2)}) collective-permute-start(bf16[24,6144]{1,0:T(8,128)(2,1)} %fusion), channel_id=1, source_target_pairs={{0,3},{1,4},{2,5},{3,6},{4,7},{5,8},{6,9},{7,10},{8,11},{9,12},{10... | collective-permute-start | bytes 884744
  128.9 18.2 %collective-permute-start.4 = (bf16[18,6144]{1,0:T(8,128)(2,1)S(1)}, bf16[18,6144]{1,0:T(8,128)(2,1)S(1)}, u32[]{:S(2)}, u32[]{:S(2)}) collective-permute-start(bf16[18,6144]{1,0:T(8,128)(2,1)S(1)} %slice.25), channel_id=1, source_target_pairs={{0,4},{1,5},{2,6},{3,7},{4,8},{5,9},{6,10},{7,11},{8,12},{9,13},{1... | collective-permute-start | bytes 663560
  152.8 14.2 %collective-permute-start = (bf16[18,6144]{1,0:T(8,128)(2,1)S(1)}, bf16[18,6144]{1,0:T(8,128)(2,1)S(1)}, u32[]{:S(2)}, u32[]{:S(2)}) collective-permute-start(bf16[18,6144]{1,0:T(8,128)(2,1)S(1)} %fusion.9), channel_id=1, source_target_pairs={{240,0},{0,16},{16,32},{32,48},{48,64},{64,80},{80,96},{96,112},{1... | collective-permute-start | bytes 663560 | tf_op jit(solution)/shard_map/ppermute | solution.py:12
where the time goes:
time: 169 us; the launch traced here: 168 us
  blocking collectives  52.5 us (31%)
  local copies, waits for them, and re-layouts  29 us (17%)
  waiting for transfers between devices  25.1 us (15%)
  matrix products  24.6 us (15%)
  starting transfers between devices  23.3 us (14%)
  other arithmetic  11.7 us (7%)
    unnamed x1, blocking collectives  52.5 us
    unnamed x13, local copies, waits for them, and re-layouts  24.9 us
    unnamed x4, waiting for transfers between devices  14 us
    unnamed x4, starting transfers between devices  13.6 us
    ppermute x1, waiting for transfers between devices, shifted(): return lax.ppermute(block, axis, route)  11.1 us
    dot_general x1, matrix products, shards(): jnp.einsum('qhd,khd->hqk', queries, history[:, 0], preferred_element_type...  10.5 us
    reduce_sum x1, other arithmetic, shards(): jnp.sum(distant_exp, axis=-1, keepdims=True)  9.07 us
    dot_general x1, matrix products, shards(): jnp.einsum('hqk,khd->qhd', distant_w, history[:, 1], preferred_element_ty...  7.88 us
  transfers between devices with their start and end apart: 6, of which 2 were waited for; matrix products, arithmetic and copies ran while one was open for 12% of the time, Pallas kernels for 0%

commit v1 on v0

v1 whole, which is shorter than its diff:
```python
import functools
import math

import jax
import jax.numpy as jnp
from jax import lax
from jax.experimental import pallas as pl
from jax.experimental.pallas import tpu as pltpu
from jax.sharding import PartitionSpec as P

HD = 128
CORES = 2
MAIN = 16
VMEM_LIMIT = 56 * 2**20


def attend_kernel(scalars, arrived, kv, keep, send, q_s, fresh_s, kv_s, sems, *, heads, chunk):
    groups = arrived.shape[0]
    tok = arrived.shape[1] // 3
    half = tok * groups // CORES
    peers = groups // CORES
    keys = kv.shape[1]
    patch = tok * groups
    rest = tok - MAIN
    scale = math.log2(math.e) / math.sqrt(HD)
    copies = []
    for h in range(heads):
        for t in range(2):
            cols = pl.ds(h * HD, HD)
            copy = pltpu.make_async_copy(
                kv.at[t, :, cols], kv_s.at[t, :, cols], sems.at[2 * h + t]
            )
            copy.start()
            copies.append(copy)
    core = scalars[1]
    for side in range(CORES):
        which = core if side == 0 else 1 - core
        for k in range(peers):
            block = arrived[CORES * k + which]
            for t in range(3):
                target = q_s if t == 0 else fresh_s.at[t - 1]
                rows = block[t * tok : (t + 1) * tok]
                target[pl.ds(side * half + MAIN * k, MAIN), :] = rows[:MAIN]
                target[pl.ds(side * half + MAIN * peers + rest * k, rest), :] = rows[MAIN:]
    own = pl.multiple_of(scalars[0] * patch, MAIN)
    for h in range(heads):
        cols = slice(h * HD, (h + 1) * HD)
        for t in range(2):
            copies[2 * h + t].wait()
            kv_s[t, pl.ds(own, patch), cols] = fresh_s[t, :, cols]
        q = q_s[:, cols]

        def score(j):
            k = kv_s[0, chunk * j : chunk * (j + 1), cols]
            return lax.dot_general(
                q, k, (((1,), (1,)), ((), ())), preferred_element_type=jnp.float32
            )

        top = total = acc = None
        upcoming = score(0)
        for j in range(keys // chunk):
            s = upcoming
            if j + 1 < keys // chunk:
                upcoming = score(j + 1)
            high = jnp.max(s, axis=1, keepdims=True)
            new_top = high if j == 0 else jnp.maximum(top, high)
            p = jnp.exp2((s - new_top) * scale)
            part = jnp.sum(p, axis=1, keepdims=True)
            v = kv_s[1, chunk * j : chunk * (j + 1), cols]
            out = jnp.dot(p.astype(jnp.bfloat16), v, preferred_element_type=jnp.float32)
            if j == 0:
                total, acc = part, out
            else:
                fade = jnp.exp2((top - new_top) * scale)
                total = total * fade + part
                acc = acc * fade + out
            top = new_top
        done = (acc / total).astype(jnp.bfloat16)
        keep[:, cols] = done[:half]
        send[:, cols] = done[half:]


def attend(scalars, arrived, kv):
    groups, rows, width = arrived.shape
    heads = width // HD
    keys = kv.shape[1]
    patch = rows // 3 * groups
    result = jax.ShapeDtypeStruct((patch // CORES, width), jnp.bfloat16)
    vmem = pl.BlockSpec(memory_space=pltpu.VMEM)
    return pl.pallas_call(
        functools.partial(attend_kernel, heads=heads, chunk=keys // 6),
        in_specs=[pl.BlockSpec(memory_space=pltpu.SMEM), vmem, pl.BlockSpec(memory_space=pl.ANY)],
        out_specs=[vmem, vmem],
        out_shape=[result, result],
        scratch_shapes=[
            pltpu.VMEM((patch, width), jnp.bfloat16),
            pltpu.VMEM((2, patch, width), jnp.bfloat16),
            pltpu.VMEM((2, keys, width), jnp.bfloat16),
            pltpu.SemaphoreType.DMA((2 * heads,)),
        ],
        compiler_params=pltpu.CompilerParams(vmem_limit_bytes=VMEM_LIMIT),
        name="attend",
    )(scalars, arrived, kv)


def project_kernel(keep, other, w_keep, w_other, out, rest_s, *, cuts, peers, per_step):
    step = pl.program_id(0)
    rest = keep.shape[0] // peers - MAIN
    width = out.shape[2] // per_step
    y = jnp.dot(keep[...], w_keep[...], preferred_element_type=jnp.float32)
    y = y + jnp.dot(other[...], w_other[...], preferred_element_type=jnp.float32)
    for d in range(peers):
        out[d] = y[MAIN * d : MAIN * (d + 1)].astype(jnp.bfloat16)
    for b in range(per_step):
        for d in range(peers):
            for t in range(rest):
                row = MAIN * peers + rest * d + t
                value = y[row : row + 1, width * b : width * (b + 1)]
                for s in range(cuts // per_step + 1):
                    cut = s * per_step + b
                    if cut < cuts:

                        @pl.when(step == s)
                        def _():
                            rest_s[d, cuts * t + cut : cuts * t + cut + 1, :] = value

    last = cuts % per_step

    @pl.when(step == cuts // per_step)
    def _():
        for d in range(peers):
            out[d, :, width * last : width * (last + 1)] = rest_s[d].astype(jnp.bfloat16)


def project(keep, other, w_keep, w_other, peers):
    rows, width = keep.shape
    columns = w_keep.shape[1]
    rest = rows // peers - MAIN
    cuts = MAIN // rest
    cut = columns // cuts
    per_step = 3
    steps = cuts // per_step + 1
    whole = pl.BlockSpec((rows, width), lambda i: (0, 0))
    weights = pl.BlockSpec((width, per_step * cut), lambda i: (0, i))
    return pl.pallas_call(
        functools.partial(project_kernel, cuts=cuts, peers=peers, per_step=per_step),
        grid=(steps,),
        in_specs=[whole, whole, weights, weights],
        out_specs=pl.BlockSpec((peers, MAIN, per_step * cut), lambda i: (0, 0, i)),
        out_shape=jax.ShapeDtypeStruct((peers, MAIN, columns + cut), jnp.bfloat16),
        scratch_shapes=[pltpu.VMEM((peers, MAIN, cut), jnp.float32)],
        compiler_params=pltpu.CompilerParams(vmem_limit_bytes=VMEM_LIMIT),
        name="project",
    )(keep, other, w_keep, w_other)


def update_kernel(parts, residual, residual_rest, gate, gate_rest, out):
    columns = residual.shape[1]
    total = parts[0].astype(jnp.float32)
    for d in range(1, parts.shape[0]):
        total = total + parts[d].astype(jnp.float32)
    main = residual[0:MAIN, :].astype(jnp.float32) + gate[...] * total[:, :columns]
    out[:, :columns] = main.astype(jnp.bfloat16)
    tail = residual_rest[...].astype(jnp.float32) + gate_rest[...] * total[:, columns:]
    out[:, columns:] = tail.astype(jnp.bfloat16)


def update(parts, residual, residual_rest, gate, gate_rest):
    vmem = pl.BlockSpec(memory_space=pltpu.VMEM)
    return pl.pallas_call(
        update_kernel,
        in_specs=[vmem] * 5,
        out_specs=vmem,
        out_shape=jax.ShapeDtypeStruct(parts.shape[1:], jnp.bfloat16),
        compiler_params=pltpu.CompilerParams(vmem_limit_bytes=VMEM_LIMIT),
        name="update",
    )(parts, residual, residual_rest, gate, gate_rest)


def unpack_kernel(packed, out):
    rows, columns = out.shape
    rest = rows - MAIN
    cuts = MAIN // rest
    cut = columns // cuts
    out[0:MAIN, :] = packed[:, :columns]
    tail = packed[:, columns:].astype(jnp.float32)
    for b in range(cuts):
        pieces = [tail[cuts * t + b : cuts * t + b + 1] for t in range(rest)]
        out[MAIN:rows, b * cut : (b + 1) * cut] = jnp.concatenate(pieces, axis=0).astype(
            jnp.bfloat16
        )


def unpack(packed, rows, columns):
    vmem = pl.BlockSpec(memory_space=pltpu.VMEM)
    return pl.pallas_call(
        unpack_kernel,
        in_specs=[vmem],
        out_specs=vmem,
        out_shape=jax.ShapeDtypeStruct((rows, columns), jnp.bfloat16),
        name="unpack",
    )(packed)


def shards(qkv, stale_kv, out_weight, residual, gate, patch_of_section):
    groups = lax.axis_size("head")
    sections = lax.axis_size("section")
    peers = groups // CORES
    tok = qkv.shape[1]
    rest = tok - MAIN
    cuts = MAIN // rest
    width = stale_kv.shape[3]
    columns = out_weight.shape[2]
    swap = [(i, i ^ 1) for i in range(groups)]
    same_core = [[CORES * k + c for k in range(peers)] for c in range(CORES)]

    core = lax.axis_index("head") % CORES
    scalars = jnp.stack([patch_of_section[0], core.astype(jnp.int32)])
    blocked = (
        qkv[0].reshape(tok, 3, groups, width).transpose(2, 1, 0, 3).reshape(groups, 3 * tok, width)
    )
    arrived = lax.all_to_all(blocked, "head", split_axis=0, concat_axis=0, tiled=True)
    weight = out_weight[0]
    weight_other = lax.ppermute(weight, "head", swap)
    kv = jnp.transpose(stale_kv[0], (1, 0, 2))
    residual_rest = residual[0, MAIN:].reshape(MAIN, columns // cuts)
    gate_rest = jnp.tile(gate[0].reshape(cuts, columns // cuts), (rest, 1))

    keep, send = attend(scalars, arrived, kv)
    other = lax.ppermute(send, "head", swap)
    partial_sums = project(keep, other, weight, weight_other, peers)
    parts = lax.all_to_all(
        partial_sums, "head", split_axis=0, concat_axis=0, tiled=True, axis_index_groups=same_core
    )
    updated = update(parts, residual[0], residual_rest, gate, gate_rest)
    handed = lax.ppermute(
        updated, "section", [(i, (i + 1) % sections) for i in range(sections)]
    )
    return unpack(handed, tok, columns)[None]


def solution(mesh):
    placed = (
        P("section", "head", None, None),
        P("section", None, None, "head"),
        P("section", "head", None),
        P("section", "head", None),
        P("section", None),
        P("section"),
    )
    return jax.shard_map(
        shards, mesh=mesh, in_specs=placed, out_specs=P("section", "head", None), check_vma=False
    )
```

time: 169 us -> 92.6 us (0.55)
  the two profiles are of different devices: /device:TPU:9 before, /device:TPU:32 now
where the time goes in v1:
time: 92.6 us; the launch traced here: 92.1 us
  waiting for transfers between devices  38.5 us (42%)
  Pallas kernels  21 us (23%)
  local copies, waits for them, and re-layouts  16.4 us (18%)
  starting transfers between devices  14.3 us (15%)
  other arithmetic  1.29 us (1%)
    all_to_all x1, waiting for transfers between devices, shards(): lax.all_to_all(partial_sums, 'head', split_axis=0, concat_axis=0, tiled=T...  19.5 us
    ppermute x1, waiting for transfers between devices, shards(): lax.ppermute(updated, 'section', [(i, (i + 1) % sections) for i in range(...  14.2 us
    unnamed x12, local copies, waits for them, and re-layouts  10.8 us
    pallas_call x1, Pallas kernels, attend(): pl.pallas_call(functools.partial(attend_kernel, heads=heads, chunk=keys /...  9.14 us
    pallas_call x1, Pallas kernels, project(): pl.pallas_call(functools.partial(project_kernel, cuts=cuts, peers=peers,...  7.59 us
    all_to_all x1, starting transfers between devices, shards(): lax.all_to_all(blocked, 'head', split_axis=0, concat_axis=0, tiled=True)  6.06 us
    all_to_all x1, starting transfers between devices, shards(): lax.all_to_all(partial_sums, 'head', split_axis=0, concat_axis=0, tiled=T...  4.76 us
    all_to_all x1, waiting for transfers between devices, shards(): lax.all_to_all(blocked, 'head', split_axis=0, concat_axis=0, tiled=True)  3.39 us
  transfers between devices with their start and end apart: 5, of which 4 were waited for; matrix products, arithmetic and copies ran while one was open for 15% of the time, Pallas kernels for 10%

profile of v1, /device:TPU:32, one launch (start us, length us, event | category | flops | bytes accessed | tf_op | source)
XLA Modules:
  0.0 92.1 jit_solution(12937646600953420004)
XLA Ops:
  0.0 0.0 collective-permute-start.1
  0.0 2.4 %reshape.8 = bf16[18,3,16,384]{3,2,1,0:T(8,128)(2,1)S(1)} reshape(bf16[1,18,3,6144]{3,2,1,0:T(4,128)(2,1)} %param.6) | data formatting | bytes 1327104 | tf_op jit(solution)/shard_map/reshape;squeeze | solution.py:220
  2.4 0.1 copy.12
  2.5 1.0 %copy.10 = bf16[16,54,384]{2,1,0:T(8,128)(2,1)} copy(bf16[16,54,384]{2,0,1:T(8,128)(2,1)S(1)} %bitcast.17) | data formatting | bytes 1327104 | tf_op jit(solution)/shard_map/reshape | solution.py:220
  3.5 6.1 %all-to-all-start = ((bf16[16,54,384]{2,1,0:T(8,128)(2,1)}), bf16[16,54,384]{2,1,0:T(8,128)(2,1)S(1)}, u32[]{:S(2)}, u32[]{:S(2)}) async-start(bf16[16,54,384]{2,1,0:T(8,128)(2,1)} %copy.10), calls=%async_computation | async-start | bytes 1376256 | tf_op jit(solution)/shard_map/all_to_all | solution.py:222
  10.2 6.9 %copy.14 = bf16[1,4608,2,384]{3,1,2,0:T(8,128)(2,1)} copy(bf16[1,4608,2,384]{3,2,1,0:T(2,128)(2,1)} %param.7) | data formatting | bytes 14155776 | tf_op args[1]
  17.0 0.6 pad_add_fusion.scalars
  17.6 3.4 %all-to-all-done.arrived = bf16[16,54,384]{2,1,0:T(8,128)(2,1)S(1)} async-done(((bf16[16,54,384]{2,1,0:T(8,128)(2,1)}), bf16[16,54,384]{2,1,0:T(8,128)(2,1)S(1)}, u32[]{:S(2)}, u32[]{:S(2)}) %all-to-all-start) | async-done | bytes 663584 | tf_op jit(solution)/shard_map/all_to_all | solution.py:222
  21.0 0.0 copy-start.1
  21.0 0.8 copy-done.1
  21.9 9.1 %attend.1 = (bf16[144,384]{1,0:T(8,128)(2,1)}, bf16[144,384]{1,0:T(8,128)(2,1)}) custom-call(s32[2]{0:T(128)} %pad_add_fusion.scalars, bf16[16,54,384]{2,1,0:T(8,128)(2,1)} %copy-done.1, bf16[2,4608,384]{2,1,0:T(8,128)(2,1)} %bitcast.14), custom_call_target="tpu_custom_call" | custom-call | tf_op jit(solution)/shard_map/attend/pallas_call | solution.py:90
  31.0 0.2 collective-permute-start
  31.2 1.4 %collective-permute-done.other = bf16[144,384]{1,0:T(8,128)(2,1)S(1)} collective-permute-done((bf16[144,384]{1,0:T(8,128)(2,1)}, bf16[144,384]{1,0:T(8,128)(2,1)S(1)}, u32[]{:S(2)}, u32[]{:S(2)}) %collective-permute-start) | collective-permute-done | bytes 110624 | tf_op jit(solution)/shard_map/ppermute | solution.py:230
  32.6 0.0 copy-start.3
  32.6 0.0 collective-permute-done.1.w_other
  32.6 0.6 copy-done.3
  33.3 0.0 copy-start.4
  33.3 7.6 %project.1 = bf16[8,16,6912]{2,1,0:T(8,128)(2,1)} custom-call(bf16[144,384]{1,0:T(8,128)(2,1)} %get-tuple-element.7.keep, bf16[144,384]{1,0:T(8,128)(2,1)} %copy-done.3, bf16[384,6144]{1,0:T(8,128)(2,1)} %bitcast.16, bf16[384,6144]{1,0:T(8,128)(2,1)} %collective-permute-done.1.w_other), custom_call_target="tpu_custom_call" | custom-call | tf_op jit(solution)/shard_map/project/pallas_call | solution.py:145
  40.9 4.8 %all-to-all-start.1 = ((bf16[8,16,6912]{2,1,0:T(8,128)(2,1)}), bf16[8,16,6912]{2,1,0:T(8,128)(2,1)S(1)}, u32[]{:S(2)}, u32[]{:S(2)}) async-start(bf16[8,16,6912]{2,1,0:T(8,128)(2,1)} %project.1), calls=%async_computation.1 | async-start | bytes 3538944 | tf_op jit(solution)/shard_map/all_to_all | solution.py:232
  45.6 0.9 slice.3
  46.5 0.6 reshape_squeeze.7.residual_rest
  47.2 0.5 broadcast.6
  47.7 0.0 copy-done.4
  47.7 0.7 reduce.3
  48.4 0.6 broadcast_bitcast_fusion.gate_rest
  49.0 19.5 %all-to-all-done.1.parts = bf16[8,16,6912]{2,1,0:T(8,128)(2,1)S(1)} async-done(((bf16[8,16,6912]{2,1,0:T(8,128)(2,1)}), bf16[8,16,6912]{2,1,0:T(8,128)(2,1)S(1)}, u32[]{:S(2)}, u32[]{:S(2)}) %all-to-all-start.1) | async-done | bytes 1769504 | tf_op jit(solution)/shard_map/all_to_all | solution.py:232
  68.5 0.0 copy-start
  68.5 1.2 %copy-done = bf16[8,16,6912]{2,1,0:T(8,128)(2,1)} copy-done((bf16[8,16,6912]{2,1,0:T(8,128)(2,1)}, bf16[8,16,6912]{2,1,0:T(8,128)(2,1)S(1)}, u32[]{:S(2)}) %copy-start) | copy-done | bytes 1769496
  69.7 2.6 %update.1 = bf16[16,6912]{1,0:T(8,128)(2,1)} custom-call(bf16[8,16,6912]{2,1,0:T(8,128)(2,1)} %copy-done, bf16[18,6144]{1,0:T(8,128)(2,1)} %bitcast.18, bf16[16,768]{1,0:T(8,128)(2,1)} %reshape_squeeze.7.residual_rest, f32[1,6144]{1,0:T(1,128)} %gate.1, f32[16,768]{1,0:T(8,128)} %broadcast_bitcast_fusion.gate_rest), custom_call_target="tpu_custom_call" | custom-call | tf_op jit(solution)/shard_map/update/pallas_call | solution.py:170
  72.3 3.3 %collective-permute-start.2 = (bf16[16,6912]{1,0:T(8,128)(2,1)}, bf16[16,6912]{1,0:T(8,128)(2,1)S(1)}, u32[]{:S(2)}, u32[]{:S(2)}) collective-permute-start(bf16[16,6912]{1,0:T(8,128)(2,1)} %update.1), channel_id=1, source_target_pairs={{0,16},{16,32},{32,48},{48,64},{64,80},{80,96},{96,112},{112,128},... | collective-permute-start | bytes 663560 | tf_op jit(solution)/shard_map/ppermute | solution.py:236
  75.6 14.2 %collective-permute-done.2.packed = bf16[16,6912]{1,0:T(8,128)(2,1)S(1)} collective-permute-done((bf16[16,6912]{1,0:T(8,128)(2,1)}, bf16[16,6912]{1,0:T(8,128)(2,1)S(1)}, u32[]{:S(2)}, u32[]{:S(2)}) %collective-permute-start.2) | collective-permute-done | bytes 221216 | tf_op jit(solution)/shard_map/ppermute | solution.py:236
  89.8 0.0 copy-start.2
  89.8 0.7 copy-done.2
  90.4 1.7 %unpack.1 = bf16[18,6144]{1,0:T(8,128)(2,1)} custom-call(bf16[16,6912]{1,0:T(8,128)(2,1)} %copy-done.2), custom_call_target="tpu_custom_call" | custom-call | tf_op jit(solution)/shard_map/unpack/pallas_call | solution.py:196
  (1 shorter events, 0.0 us)
Async XLA Ops:
  0.0 32.6 %collective-permute-start.1 = (bf16[384,6144]{1,0:T(8,128)(2,1)}, bf16[384,6144]{1,0:T(8,128)(2,1)}, u32[]{:S(2)}, u32[]{:S(2)}) collective-permute-start(bf16[384,6144]{1,0:T(8,128)(2,1)} %bitcast.15), channel_id=1, source_target_pairs={{0,1},{1,0},{2,3},{3,2},{4,5},{5,4},{6,7},{7,6},{8,9},{9,8},{10,11... | collective-permute-start | bytes 14155784 | tf_op jit(solution)/shard_map/ppermute | solution.py:224
  3.5 17.6 %all-to-all-start = ((bf16[16,54,384]{2,1,0:T(8,128)(2,1)}), bf16[16,54,384]{2,1,0:T(8,128)(2,1)S(1)}, u32[]{:S(2)}, u32[]{:S(2)}) async-start(bf16[16,54,384]{2,1,0:T(8,128)(2,1)} %copy.10), calls=%async_computation | async-start | bytes 1376256 | tf_op jit(solution)/shard_map/all_to_all | solution.py:222
  21.0 0.8 copy-start.1
  31.0 1.6 %collective-permute-start = (bf16[144,384]{1,0:T(8,128)(2,1)}, bf16[144,384]{1,0:T(8,128)(2,1)S(1)}, u32[]{:S(2)}, u32[]{:S(2)}) collective-permute-start(bf16[144,384]{1,0:T(8,128)(2,1)} %get-tuple-element.8), channel_id=1, source_target_pairs={{0,1},{1,0},{2,3},{3,2},{4,5},{5,4},{6,7},{7,6},{8,9},{9,8},{10,11... | collective-permute-start | bytes 331784 | tf_op jit(solution)/shard_map/ppermute | solution.py:230
  32.6 0.6 copy-start.3
  33.3 14.4 %copy-start.4 = (f32[1,6144]{1,0:T(1,128)S(1)}, f32[1,6144]{1,0:T(1,128)}, u32[]{:S(2)}) copy-start(f32[1,6144]{1,0:T(1,128)} %gate.1) | copy-start | bytes 73732
  40.9 27.6 %all-to-all-start.1 = ((bf16[8,16,6912]{2,1,0:T(8,128)(2,1)}), bf16[8,16,6912]{2,1,0:T(8,128)(2,1)S(1)}, u32[]{:S(2)}, u32[]{:S(2)}) async-start(bf16[8,16,6912]{2,1,0:T(8,128)(2,1)} %project.1), calls=%async_computation.1 | async-start | bytes 3538944 | tf_op jit(solution)/shard_map/all_to_all | solution.py:232
  68.5 1.2 %copy-start = (bf16[8,16,6912]{2,1,0:T(8,128)(2,1)}, bf16[8,16,6912]{2,1,0:T(8,128)(2,1)S(1)}, u32[]{:S(2)}) copy-start(bf16[8,16,6912]{2,1,0:T(8,128)(2,1)S(1)} %all-to-all-done.1.parts) | copy-start | bytes 5308420
  72.3 17.5 %collective-permute-start.2 = (bf16[16,6912]{1,0:T(8,128)(2,1)}, bf16[16,6912]{1,0:T(8,128)(2,1)S(1)}, u32[]{:S(2)}, u32[]{:S(2)}) collective-permute-start(bf16[16,6912]{1,0:T(8,128)(2,1)} %update.1), channel_id=1, source_target_pairs={{0,16},{16,32},{32,48},{48,64},{64,80},{80,96},{96,112},{112,128},... | collective-permute-start | bytes 663560 | tf_op jit(solution)/shard_map/ppermute | solution.py:236
  89.8 0.7 copy-start.2

commit v2 on v1

v2 whole, which is shorter than its diff:
```python
import functools
import math

import jax
import jax.numpy as jnp
from jax import lax
from jax.experimental import pallas as pl
from jax.experimental.pallas import tpu as pltpu
from jax.sharding import PartitionSpec as P

HD = 128
CORES = 2
MAIN = 16
SPLIT = (1,)
CHUNKS = 6
ATTEND_VMEM = 36 * 2**20
VMEM_LIMIT = 8 * 2**20


def in_vmem(x):
    return pltpu.with_memory_space_constraint(x, pltpu.VMEM)


def in_hbm(x):
    return pltpu.with_memory_space_constraint(x, pltpu.HBM)


def pack_kernel(qkv, out, rows_s):
    tok = qkv.shape[1]
    width = out.shape[2]
    for i in range(tok):
        value = qkv[0, i].astype(jnp.float32)
        for t in range(3):
            rows_s[t * tok + i : t * tok + i + 1, :] = value[t : t + 1]
    for g in range(out.shape[0]):
        out[g] = rows_s[:, g * width : (g + 1) * width].astype(jnp.bfloat16)


def pack(qkv, groups):
    _, tok, _, columns = qkv.shape
    vmem = pl.BlockSpec(memory_space=pltpu.VMEM)
    return pl.pallas_call(
        pack_kernel,
        in_specs=[vmem],
        out_specs=vmem,
        out_shape=jax.ShapeDtypeStruct((groups, 3 * tok, columns // groups), jnp.bfloat16),
        scratch_shapes=[pltpu.VMEM((3 * tok, columns), jnp.float32)],
        compiler_params=pltpu.CompilerParams(vmem_limit_bytes=VMEM_LIMIT),
        name="pack",
    )(qkv)


def stream_kernel(residual, gate, *packed, chunks):
    rest = residual.shape[0] - MAIN
    cuts = MAIN // rest
    stream = residual[...].astype(jnp.float32)
    gates = gate[...]
    for i, (start, size) in enumerate(chunks):
        res_out, gate_out = packed[2 * i : 2 * i + 2]
        cut = size // cuts
        res_out[:, :size] = stream[:MAIN, start : start + size]
        gate_out[:, :size] = jnp.broadcast_to(gates[:, start : start + size], (MAIN, size))
        for b in range(cuts):
            cols = slice(start + b * cut, start + (b + 1) * cut)
            for t in range(rest):
                row = cuts * t + b
                res_out[row : row + 1, size:] = stream[MAIN + t : MAIN + t + 1, cols]
                gate_out[row : row + 1, size:] = gates[:, cols]


def stream(residual, gate, chunks):
    vmem = pl.BlockSpec(memory_space=pltpu.VMEM)
    packed = []
    for _, size in chunks:
        packed += [pltpu.VMEM((MAIN, packed_width(size, residual.shape[0])), jnp.float32)] * 2
    return pl.pallas_call(
        functools.partial(stream_kernel, chunks=chunks),
        in_specs=[vmem, vmem],
        out_specs=[vmem] * len(packed),
        out_shape=packed,
        compiler_params=pltpu.CompilerParams(vmem_limit_bytes=VMEM_LIMIT),
        name="stream",
    )(residual, gate)


def attend_kernel(
    scalars, arrived, kv, w_keep, w_other, keep, send, w_out, q_s, fresh_s, sems, *kv_s, heads, chunk
):
    copies = []
    for h in range(heads):
        for t in range(2):
            copies.append(
                pltpu.make_async_copy(
                    kv.at[t, :, pl.ds(h * HD, HD)], kv_s[2 * h + t], sems.at[2 * h + t]
                )
            )
    for i, w in enumerate((w_keep, w_other)):
        copies.append(pltpu.make_async_copy(w, w_out.at[i], sems.at[2 * heads + i]))
    for copy in copies:
        copy.start()
    groups = arrived.shape[0]
    tok = arrived.shape[1] // 3
    half = tok * groups // CORES
    peers = groups // CORES
    patch = tok * groups
    rest = tok - MAIN
    scale = math.log2(math.e) / math.sqrt(HD)
    core = scalars[1]
    for side in range(CORES):
        which = core if side == 0 else 1 - core
        for k in range(peers):
            block = arrived[CORES * k + which]
            for t in range(3):
                target = q_s if t == 0 else fresh_s.at[t - 1]
                rows = block[t * tok : (t + 1) * tok]
                target[pl.ds(side * half + MAIN * k, MAIN), :] = rows[:MAIN]
                target[pl.ds(side * half + MAIN * peers + rest * k, rest), :] = rows[MAIN:]
    own = pl.ds(pl.multiple_of(scalars[0] * patch, MAIN), patch)

    def ready(h, t):
        copies[2 * h + t].wait()
        kv_s[2 * h + t][own, :] = fresh_s[t, :, h * HD : (h + 1) * HD]

    keys = kv_s[0].shape[0]
    for h in range(heads):
        ready(h, 0)
        ready(h, 1)
        cols = slice(h * HD, (h + 1) * HD)
        q = q_s[:, cols]

        def score(j):
            k = kv_s[2 * h][j * chunk : (j + 1) * chunk, :]
            return lax.dot_general(
                q, k, (((1,), (1,)), ((), ())), preferred_element_type=jnp.float32
            )

        top = total = acc = None
        upcoming = score(0)
        for j in range(keys // chunk):
            s = upcoming
            if j + 1 < keys // chunk:
                upcoming = score(j + 1)
            high = jnp.max(s, axis=1, keepdims=True)
            new_top = high if j == 0 else jnp.maximum(top, high)
            p = jnp.exp2((s - new_top) * scale)
            part = jnp.sum(p, axis=1, keepdims=True)
            v = kv_s[2 * h + 1][j * chunk : (j + 1) * chunk, :]
            out = jnp.dot(p.astype(jnp.bfloat16), v, preferred_element_type=jnp.float32)
            if j == 0:
                total, acc = part, out
            else:
                fade = jnp.exp2((top - new_top) * scale)
                total = total * fade + part
                acc = acc * fade + out
            top = new_top
        done = (acc / total).astype(jnp.bfloat16)
        keep[:, cols] = done[:half]
        send[:, cols] = done[half:]
    for copy in copies[2 * heads :]:
        copy.wait()


def attend(scalars, arrived, kv, w_keep, w_other):
    groups, rows, width = arrived.shape
    keys = kv.shape[1]
    heads = width // HD
    patch = rows // 3 * groups
    result = pltpu.VMEM((patch // CORES, width), jnp.bfloat16)
    vmem = pl.BlockSpec(memory_space=pltpu.VMEM)
    anywhere = pl.BlockSpec(memory_space=pl.ANY)
    return pl.pallas_call(
        functools.partial(attend_kernel, heads=heads, chunk=keys // CHUNKS),
        in_specs=[pl.BlockSpec(memory_space=pltpu.SMEM), vmem] + [anywhere] * 3,
        out_specs=[vmem] * 3,
        out_shape=[
            result,
            result,
            pltpu.VMEM((CORES,) + w_keep.shape, w_keep.dtype),
        ],
        scratch_shapes=[
            pltpu.VMEM((patch, width), jnp.bfloat16),
            pltpu.VMEM((2, patch, width), jnp.bfloat16),
            pltpu.SemaphoreType.DMA((2 * heads + 2,)),
        ]
        + [pltpu.VMEM((keys, HD), jnp.bfloat16)] * (2 * heads),
        compiler_params=pltpu.CompilerParams(vmem_limit_bytes=ATTEND_VMEM),
        name="attend",
    )(scalars, in_vmem(arrived), *map(in_hbm, (kv, w_keep, w_other)))


def packed_width(size, tok):
    return size * tok // MAIN


def project_kernel(keep, other, weights, out, rest_s, *, start, size):
    peers = out.shape[0]
    cut = out.shape[2] - size
    cuts = size // cut
    rest = MAIN // cuts
    both = jnp.concatenate([keep[...], other[...]], axis=1)
    for b in range(cuts):
        cols = slice(start + b * cut, start + (b + 1) * cut)
        w = jnp.concatenate([weights[i, :, cols] for i in range(CORES)], axis=0)
        y = jnp.dot(both, w, preferred_element_type=jnp.float32)
        for d in range(peers):
            rows = y[MAIN * d : MAIN * (d + 1)]
            out[d, :, b * cut : (b + 1) * cut] = rows.astype(jnp.bfloat16)
            for t in range(rest):
                row = MAIN * peers + rest * d + t
                rest_s[d, cuts * t + b : cuts * t + b + 1, :] = y[row : row + 1]
    for d in range(peers):
        out[d, :, size:] = rest_s[d].astype(jnp.bfloat16)


def project(keep, other, weights, peers, start, size):
    rows, _ = keep.shape
    width = packed_width(size, rows // peers)
    vmem = pl.BlockSpec(memory_space=pltpu.VMEM)
    return pl.pallas_call(
        functools.partial(project_kernel, start=start, size=size),
        in_specs=[vmem] * 3,
        out_specs=vmem,
        out_shape=pltpu.VMEM((peers, MAIN, width), jnp.bfloat16),
        scratch_shapes=[pltpu.VMEM((peers, MAIN, width - size), jnp.float32)],
        compiler_params=pltpu.CompilerParams(vmem_limit_bytes=VMEM_LIMIT),
        name=f"project_{start}",
    )(in_vmem(keep), in_vmem(other), in_vmem(weights))


def update_kernel(parts, residual, gate, out):
    total = parts[0].astype(jnp.float32)
    for d in range(1, parts.shape[0]):
        total = total + parts[d].astype(jnp.float32)
    out[...] = (residual[...] + gate[...] * total).astype(jnp.bfloat16)


def update(parts, residual, gate):
    vmem = pl.BlockSpec(memory_space=pltpu.VMEM)
    return pl.pallas_call(
        update_kernel,
        in_specs=[vmem] * 3,
        out_specs=vmem,
        out_shape=pltpu.VMEM(parts.shape[1:], jnp.bfloat16),
        compiler_params=pltpu.CompilerParams(vmem_limit_bytes=VMEM_LIMIT),
        name="update",
    )(in_vmem(parts), in_vmem(residual), in_vmem(gate))


def unpack_kernel(*refs, chunks):
    out = refs[-1]
    rest = out.shape[0] - MAIN
    cuts = MAIN // rest
    for packed, (start, size) in zip(refs, chunks):
        cut = size // cuts
        out[0:MAIN, start : start + size] = packed[:, :size]
        tail = packed[:, size:].astype(jnp.float32)
        for b in range(cuts):
            pieces = [tail[cuts * t + b : cuts * t + b + 1] for t in range(rest)]
            cols = slice(start + b * cut, start + (b + 1) * cut)
            out[MAIN:, cols] = jnp.concatenate(pieces, axis=0).astype(jnp.bfloat16)


def unpack(packed, rows, columns, chunks):
    vmem = pl.BlockSpec(memory_space=pltpu.VMEM)
    return pl.pallas_call(
        functools.partial(unpack_kernel, chunks=chunks),
        in_specs=[vmem] * len(packed),
        out_specs=vmem,
        out_shape=jax.ShapeDtypeStruct((rows, columns), jnp.bfloat16),
        compiler_params=pltpu.CompilerParams(vmem_limit_bytes=VMEM_LIMIT),
        name="unpack",
    )(*map(in_vmem, packed))


def shards(qkv, stale_kv, out_weight, residual, gate, patch_of_section):
    groups = lax.axis_size("head")
    sections = lax.axis_size("section")
    peers = groups // CORES
    tok = qkv.shape[1]
    columns = out_weight.shape[2]
    swap = [(i, i ^ 1) for i in range(groups)]
    same_core = [[CORES * k + c for k in range(peers)] for c in range(CORES)]
    chunks = []
    for parts in SPLIT:
        start = sum(size for _, size in chunks)
        chunks.append((start, columns * parts // sum(SPLIT)))

    core = lax.axis_index("head") % CORES
    scalars = jnp.stack([patch_of_section[0], core.astype(jnp.int32)])
    weight = out_weight[0]
    weight_other = lax.ppermute(weight, "head", swap)
    blocked = pack(qkv, groups)
    arrived = lax.all_to_all(blocked, "head", split_axis=0, concat_axis=0, tiled=True)
    kv = jnp.transpose(stale_kv[0], (1, 0, 2))

    keep, send, weights = attend(scalars, arrived, kv, weight, weight_other)
    other = lax.ppermute(send, "head", swap)
    packed = stream(residual[0], gate, chunks)
    handed = []
    for i, (start, size) in enumerate(chunks):
        sums = project(keep, other, weights, peers, start, size)
        parts = lax.all_to_all(
            sums, "head", split_axis=0, concat_axis=0, tiled=True, axis_index_groups=same_core
        )
        updated = update(parts, packed[2 * i], packed[2 * i + 1])
        handed.append(
            lax.ppermute(updated, "section", [(j, (j + 1) % sections) for j in range(sections)])
        )
    return unpack(handed, tok, columns, chunks)[None]


def solution(mesh):
    placed = (
        P("section", "head", None, None),
        P("section", None, None, "head"),
        P("section", "head", None),
        P("section", "head", None),
        P("section", None),
        P("section"),
    )
    return jax.shard_map(
        shards, mesh=mesh, in_specs=placed, out_specs=P("section", "head", None), check_vma=False
    )
```

time: 92.6 us -> 78.5 us (0.85)
  local copies, waits for them, and re-layouts: 16.4 us -> 8.03 us
  Pallas kernels: 21 us -> 13.1 us
  waiting for transfers between devices: 38.5 us -> 41.9 us
  other arithmetic: 1.29 us -> 0.07 us
    pallas_call x3 -> x5, Pallas kernels: 11.8 us -> 5.27 us  [the longest x1 2.94 us: project(): pl.pallas_call(functools.partial(project_kernel, start=start, size=size),...]
    another operation x5 -> x0, local copies, waits for them, and re-layouts: 3.7 us -> none  [the longest x2 2.45 us: shards(): qkv[0].reshape(tok, 3, groups, width).transpose(2, 1, 0, 3)]
    all_to_all x1, waiting for transfers between devices: 19.5 us -> 22.8 us  [shards(): lax.all_to_all(sums, 'head', split_axis=0, concat_axis=0, tiled=True, axi...]
    unnamed x12 -> x7, local copies, waits for them, and re-layouts: 10.8 us -> 8.03 us
    pallas_call x1, Pallas kernels: 9.14 us -> 7.87 us  [attend(): pl.pallas_call(functools.partial(attend_kernel, heads=heads, chunk=keys /...]
    reshape x1 -> x0, local copies, waits for them, and re-layouts: 0.99 us -> none  [shards(): qkv[0].reshape(tok, 3, groups, width).transpose(2, 1, 0, 3)]
  transfers between devices with their start and end apart: 5 -> 5, of which waited for: 4 -> 4; matrix products, arithmetic and copies ran while one was open for 15% -> 9% of each run, Pallas kernels for 10% -> 2%
where the time goes in v2:
time: 78.5 us; the launch traced here: 78.2 us
  waiting for transfers between devices  41.9 us (53%)
  starting transfers between devices  14.4 us (18%)
  Pallas kernels  13.1 us (17%)
  local copies, waits for them, and re-layouts  8.03 us (10%)
    all_to_all x1, waiting for transfers between devices, shards(): lax.all_to_all(sums, 'head', split_axis=0, concat_axis=0, tiled=True, axi...  22.8 us
    ppermute x1, waiting for transfers between devices, shards(): lax.ppermute(updated, 'section', [(j, (j + 1) % sections) for j in range(...  14 us
    unnamed x7, local copies, waits for them, and re-layouts  8.03 us
    pallas_call x1, Pallas kernels, attend(): pl.pallas_call(functools.partial(attend_kernel, heads=heads, chunk=keys /...  7.87 us
    all_to_all x1, starting transfers between devices, shards(): lax.all_to_all(blocked, 'head', split_axis=0, concat_axis=0, tiled=True)  6.06 us
    all_to_all x1, starting transfers between devices, shards(): lax.all_to_all(sums, 'head', split_axis=0, concat_axis=0, tiled=True, axi...  4.76 us
    all_to_all x1, waiting for transfers between devices, shards(): lax.all_to_all(blocked, 'head', split_axis=0, concat_axis=0, tiled=True)  3.91 us
    ppermute x1, starting transfers between devices, shards(): lax.ppermute(updated, 'section', [(j, (j + 1) % sections) for j in range(...  3.35 us
  transfers between devices with their start and end apart: 5, of which 4 were waited for; matrix products, arithmetic and copies ran while one was open for 9% of the time, Pallas kernels for 2%

profile of v2, /device:TPU:32, one launch (start us, length us, event | category | flops | bytes accessed | tf_op | source)
XLA Modules:
  0.0 78.2 jit_solution(5419453267085947759)
XLA Ops:
  0.0 0.0 collective-permute-start
  0.0 0.0 copy-start
  0.0 1.2 %copy-done = bf16[1,18,3,6144]{3,2,1,0:T(4,128)(2,1)S(1)} copy-done((bf16[1,18,3,6144]{3,2,1,0:T(4,128)(2,1)S(1)}, bf16[1,18,3,6144]{3,2,1,0:T(4,128)(2,1)}, u32[]{:S(2)}) %copy-start) | copy-done | bytes 663576
  1.2 1.3 %pack.1 = bf16[16,54,384]{2,1,0:T(8,128)(2,1)} custom-call(bf16[1,18,3,6144]{3,2,1,0:T(4,128)(2,1)S(1)} %copy-done), custom_call_target="tpu_custom_call" | custom-call | tf_op jit(solution)/shard_map/pack/pallas_call | solution.py:42
  2.4 6.1 %all-to-all-start = ((bf16[16,54,384]{2,1,0:T(8,128)(2,1)}), bf16[16,54,384]{2,1,0:T(8,128)(2,1)S(1)}, u32[]{:S(2)}, u32[]{:S(2)}) async-start(bf16[16,54,384]{2,1,0:T(8,128)(2,1)} %pack.1), calls=%async_computation | async-start | bytes 1376256 | tf_op jit(solution)/shard_map/all_to_all | solution.py:293
  9.1 6.9 %copy.9 = bf16[1,4608,2,384]{3,1,2,0:T(8,128)(2,1)} copy(bf16[1,4608,2,384]{3,2,1,0:T(2,128)(2,1)} %param.7) | data formatting | bytes 14155776 | tf_op args[1]
  16.0 0.1 pad_add_fusion.scalars
  16.1 3.9 %all-to-all-done.arrived = bf16[16,54,384]{2,1,0:T(8,128)(2,1)S(1)} async-done(((bf16[16,54,384]{2,1,0:T(8,128)(2,1)}), bf16[16,54,384]{2,1,0:T(8,128)(2,1)S(1)}, u32[]{:S(2)}, u32[]{:S(2)}) %all-to-all-start) | async-done | bytes 663584 | tf_op jit(solution)/shard_map/all_to_all | solution.py:293
  20.0 0.0 collective-permute-done.w_other
  20.0 7.9 %attend.1 = (bf16[144,384]{1,0:T(8,128)(2,1)S(1)}, bf16[144,384]{1,0:T(8,128)(2,1)S(1)}, bf16[2,384,6144]{2,1,0:T(8,128)(2,1)S(1)}) custom-call(s32[2]{0:T(128)S(1)} %pad_add_fusion.scalars, bf16[16,54,384]{2,1,0:T(8,128)(2,1)S(1)} %all-to-all-done.arrived, bf16[2,4608,384]{2,1,0:T(8,128)(2,1)} %bitcast.10, bf16[384,6144]{1,0:T(8,128)(2,1)} %bitcast.12, ...), custom_call_target="tpu_custom_call" | custom-call | tf_op jit(solution)/shard_map/attend/pallas_call | solution.py:171
  27.9 0.2 collective-permute-start.1
  28.1 1.2 %collective-permute-done.1.other = bf16[144,384]{1,0:T(8,128)(2,1)S(1)} collective-permute-done((bf16[144,384]{1,0:T(8,128)(2,1)S(1)}, bf16[144,384]{1,0:T(8,128)(2,1)S(1)}, u32[]{:S(2)}, u32[]{:S(2)}) %collective-permute-start.1) | collective-permute-done | bytes 110624 | tf_op jit(solution)/shard_map/ppermute | solution.py:297
  29.3 0.0 copy-start.1
  29.3 0.0 copy-start.2
  29.3 2.9 %project_0.1 = bf16[8,16,6912]{2,1,0:T(8,128)(2,1)} custom-call(bf16[144,384]{1,0:T(8,128)(2,1)S(1)} %get-tuple-element.10.keep, bf16[144,384]{1,0:T(8,128)(2,1)S(1)} %collective-permute-done.1.other, bf16[2,384,6144]{2,1,0:T(8,128)(2,1)S(1)} %get-tuple-element.12.weights), custom_call_target="tpu_custom_call" | custom-call | tf_op jit(solution)/shard_map/project_0/pallas_call | solution.py:219
  32.2 4.8 %all-to-all-start.1 = ((bf16[8,16,6912]{2,1,0:T(8,128)(2,1)}), bf16[8,16,6912]{2,1,0:T(8,128)(2,1)S(1)}, u32[]{:S(2)}, u32[]{:S(2)}) async-start(bf16[8,16,6912]{2,1,0:T(8,128)(2,1)} %project_0.1), calls=%async_computation.1 | async-start | bytes 3538944 | tf_op jit(solution)/shard_map/all_to_all | solution.py:302
  37.0 0.0 copy-done.1
  37.0 0.0 copy-done.2
  37.0 0.1 stream.1
  37.0 22.8 %all-to-all-done.1.parts = bf16[8,16,6912]{2,1,0:T(8,128)(2,1)S(1)} async-done(((bf16[8,16,6912]{2,1,0:T(8,128)(2,1)}), bf16[8,16,6912]{2,1,0:T(8,128)(2,1)S(1)}, u32[]{:S(2)}, u32[]{:S(2)}) %all-to-all-start.1) | async-done | bytes 1769504 | tf_op jit(solution)/shard_map/all_to_all | solution.py:302
  59.8 0.3 update.1
  60.1 3.4 %collective-permute-start.2 = (bf16[16,6912]{1,0:T(8,128)(2,1)S(1)}, bf16[16,6912]{1,0:T(8,128)(2,1)S(1)}, u32[]{:S(2)}, u32[]{:S(2)}) collective-permute-start(bf16[16,6912]{1,0:T(8,128)(2,1)S(1)} %update.1), channel_id=1, source_target_pairs={{0,16},{16,32},{32,48},{48,64},{64,80},{80,96},{96,112},{112,128},... | collective-permute-start | bytes 663560 | tf_op jit(solution)/shard_map/ppermute | solution.py:307
  63.5 14.0 %collective-permute-done.2.refs_0_ = bf16[16,6912]{1,0:T(8,128)(2,1)S(1)} collective-permute-done((bf16[16,6912]{1,0:T(8,128)(2,1)S(1)}, bf16[16,6912]{1,0:T(8,128)(2,1)S(1)}, u32[]{:S(2)}, u32[]{:S(2)}) %collective-permute-start.2) | collective-permute-done | bytes 221216 | tf_op jit(solution)/shard_map/ppermute | solution.py:307
  77.4 0.8 unpack.1
Async XLA Ops:
  0.0 20.0 %collective-permute-start = (bf16[384,6144]{1,0:T(8,128)(2,1)}, bf16[384,6144]{1,0:T(8,128)(2,1)}, u32[]{:S(2)}, u32[]{:S(2)}) collective-permute-start(bf16[384,6144]{1,0:T(8,128)(2,1)} %bitcast.11), channel_id=1, source_target_pairs={{0,1},{1,0},{2,3},{3,2},{4,5},{5,4},{6,7},{7,6},{8,9},{9,8},{10,11... | collective-permute-start | bytes 14155784 | tf_op jit(solution)/shard_map/ppermute | solution.py:291
  0.0 1.2 %copy-start = (bf16[1,18,3,6144]{3,2,1,0:T(4,128)(2,1)S(1)}, bf16[1,18,3,6144]{3,2,1,0:T(4,128)(2,1)}, u32[]{:S(2)}) copy-start(bf16[1,18,3,6144]{3,2,1,0:T(4,128)(2,1)} %qkv.1) | copy-start | bytes 1990660
  2.4 17.6 %all-to-all-start = ((bf16[16,54,384]{2,1,0:T(8,128)(2,1)}), bf16[16,54,384]{2,1,0:T(8,128)(2,1)S(1)}, u32[]{:S(2)}, u32[]{:S(2)}) async-start(bf16[16,54,384]{2,1,0:T(8,128)(2,1)} %pack.1), calls=%async_computation | async-start | bytes 1376256 | tf_op jit(solution)/shard_map/all_to_all | solution.py:293
  27.9 1.4 %collective-permute-start.1 = (bf16[144,384]{1,0:T(8,128)(2,1)S(1)}, bf16[144,384]{1,0:T(8,128)(2,1)S(1)}, u32[]{:S(2)}, u32[]{:S(2)}) collective-permute-start(bf16[144,384]{1,0:T(8,128)(2,1)S(1)} %get-tuple-element.11), channel_id=1, source_target_pairs={{0,1},{1,0},{2,3},{3,2},{4,5},{5,4},{6,7},{7,6},{8,9},{9,8},{10,11... | collective-permute-start | bytes 331784 | tf_op jit(solution)/shard_map/ppermute | solution.py:297
  29.3 7.7 %copy-start.1 = (bf16[1,18,6144]{2,1,0:T(8,128)(2,1)S(1)}, bf16[1,18,6144]{2,1,0:T(8,128)(2,1)}, u32[]{:S(2)}) copy-start(bf16[1,18,6144]{2,1,0:T(8,128)(2,1)} %param.9) | copy-start | bytes 663556
  29.3 7.7 %copy-start.2 = (f32[1,6144]{1,0:T(1,128)S(1)}, f32[1,6144]{1,0:T(1,128)}, u32[]{:S(2)}) copy-start(f32[1,6144]{1,0:T(1,128)} %gate.1) | copy-start | bytes 73732
  32.2 27.6 %all-to-all-start.1 = ((bf16[8,16,6912]{2,1,0:T(8,128)(2,1)}), bf16[8,16,6912]{2,1,0:T(8,128)(2,1)S(1)}, u32[]{:S(2)}, u32[]{:S(2)}) async-start(bf16[8,16,6912]{2,1,0:T(8,128)(2,1)} %project_0.1), calls=%async_computation.1 | async-start | bytes 3538944 | tf_op jit(solution)/shard_map/all_to_all | solution.py:302
  60.1 17.3 %collective-permute-start.2 = (bf16[16,6912]{1,0:T(8,128)(2,1)S(1)}, bf16[16,6912]{1,0:T(8,128)(2,1)S(1)}, u32[]{:S(2)}, u32[]{:S(2)}) collective-permute-start(bf16[16,6912]{1,0:T(8,128)(2,1)S(1)} %update.1), channel_id=1, source_target_pairs={{0,16},{16,32},{32,48},{48,64},{64,80},{80,96},{96,112},{112,128},... | collective-permute-start | bytes 663560 | tf_op jit(solution)/shard_map/ppermute | solution.py:307

commit v3 on v2

--- a/solution.py
+++ b/solution.py
@@ -25,29 +25,57 @@
     return pltpu.with_memory_space_constraint(x, pltpu.HBM)
 
 
-def pack_kernel(qkv, out, rows_s):
+def pack_kernel(qkv, out, in_s, rows_s, out_s, in_sems, out_sems, *, pieces):
     tok = qkv.shape[1]
-    width = out.shape[2]
-    for i in range(tok):
-        value = qkv[0, i].astype(jnp.float32)
-        for t in range(3):
-            rows_s[t * tok + i : t * tok + i + 1, :] = value[t : t + 1]
-    for g in range(out.shape[0]):
-        out[g] = rows_s[:, g * width : (g + 1) * width].astype(jnp.bfloat16)
+    groups, _, width = out.shape
+    part = tok // pieces
+    step = groups // pieces_out(groups)
+    arriving = []
+    for n in range(pieces):
+        rows = pl.ds(n * part, part)
+        arriving.append(pltpu.make_async_copy(qkv.at[0, rows], in_s.at[rows], in_sems.at[n]))
+        arriving[-1].start()
+    for n in range(pieces):
+        arriving[n].wait()
+        for i in range(n * part, (n + 1) * part):
+            value = in_s[i].astype(jnp.float32)
+            for t in range(3):
+                rows_s[t * tok + i : t * tok + i + 1, :] = value[t : t + 1]
+    leaving = []
+    for n in range(pieces_out(groups)):
+        for g in range(n * step, (n + 1) * step):
+            out_s[g] = rows_s[:, g * width : (g + 1) * width].astype(jnp.bfloat16)
+        some = pl.ds(n * step, step)
+        leaving.append(pltpu.make_async_copy(out_s.at[some], out.at[some], out_sems.at[n]))
+        leaving[-1].start()
+    for copy in leaving:
+        copy.wait()
+
+
+def pieces_out(groups):
+    return 4 if groups % 4 == 0 else 1
 
 
 def pack(qkv, groups):
     _, tok, _, columns = qkv.shape
-    vmem = pl.BlockSpec(memory_space=pltpu.VMEM)
-    return pl.pallas_call(
-        pack_kernel,
-        in_specs=[vmem],
-        out_specs=vmem,
-        out_shape=jax.ShapeDtypeStruct((groups, 3 * tok, columns // groups), jnp.bfloat16),
-        scratch_shapes=[pltpu.VMEM((3 * tok, columns), jnp.float32)],
+    shape = (groups, 3 * tok, columns // groups)
+    pieces = 3 if tok % 3 == 0 else 1
+    anywhere = pl.BlockSpec(memory_space=pl.ANY)
+    return pl.pallas_call(
+        functools.partial(pack_kernel, pieces=pieces),
+        in_specs=[anywhere],
+        out_specs=anywhere,
+        out_shape=pltpu.HBM(shape, jnp.bfloat16),
+        scratch_shapes=[
+            pltpu.VMEM((tok, 3, columns), jnp.bfloat16),
+            pltpu.VMEM((3 * tok, columns), jnp.float32),
+            pltpu.VMEM(shape, jnp.bfloat16),
+            pltpu.SemaphoreType.DMA((pieces,)),
+            pltpu.SemaphoreType.DMA((pieces_out(groups),)),
+        ],
         compiler_params=pltpu.CompilerParams(vmem_limit_bytes=VMEM_LIMIT),
         name="pack",
-    )(qkv)
+    )(in_hbm(qkv))
 
 
 def stream_kernel(residual, gate, *packed, chunks):
@@ -83,19 +111,41 @@
     )(residual, gate)
 
 
+def prefetch_kernel(kv, out, sems):
+    copies = []
+    for t in range(2):
+        copies.append(pltpu.make_async_copy(kv.at[t, :, pl.ds(0, HD)], out.at[t], sems.at[t]))
+        copies[-1].start()
+    for copy in copies:
+        copy.wait()
+
+
+def prefetch(kv):
+    return pl.pallas_call(
+        prefetch_kernel,
+        in_specs=[pl.BlockSpec(memory_space=pl.ANY)],
+        out_specs=pl.BlockSpec(memory_space=pltpu.VMEM),
+        out_shape=pltpu.VMEM((2, kv.shape[1], HD), kv.dtype),
+        scratch_shapes=[pltpu.SemaphoreType.DMA((2,))],
+        compiler_params=pltpu.CompilerParams(vmem_limit_bytes=2**20),
+        name="prefetch",
+    )(in_hbm(kv))
+
+
 def attend_kernel(
-    scalars, arrived, kv, w_keep, w_other, keep, send, w_out, q_s, fresh_s, sems, *kv_s, heads, chunk
+    scalars, arrived, first_in, kv, w_keep, w_other,
+    keep, send, w_out, first, q_s, fresh_s, sems, *kv_s, heads, chunk
 ):
     copies = []
-    for h in range(heads):
+    kv_s = (first.at[0], first.at[1]) + kv_s
+    for h in range(1, heads):
         for t in range(2):
+            n = 2 * (h - 1) + t
             copies.append(
-                pltpu.make_async_copy(
-                    kv.at[t, :, pl.ds(h * HD, HD)], kv_s[2 * h + t], sems.at[2 * h + t]
-                )
+                pltpu.make_async_copy(kv.at[t, :, pl.ds(h * HD, HD)], kv_s[2 * h + t], sems.at[n])
             )
     for i, w in enumerate((w_keep, w_other)):
-        copies.append(pltpu.make_async_copy(w, w_out.at[i], sems.at[2 * heads + i]))
+        copies.append(pltpu.make_async_copy(w, w_out.at[i], sems.at[2 * heads - 2 + i]))
     for copy in copies:
         copy.start()
     groups = arrived.shape[0]
@@ -118,7 +168,8 @@
     own = pl.ds(pl.multiple_of(scalars[0] * patch, MAIN), patch)
 
     def ready(h, t):
-        copies[2 * h + t].wait()
+        if h > 0:
+            copies[2 * (h - 1) + t].wait()
         kv_s[2 * h + t][own, :] = fresh_s[t, :, h * HD : (h + 1) * HD]
 
     keys = kv_s[0].shape[0]
@@ -143,9 +194,10 @@
             high = jnp.max(s, axis=1, keepdims=True)
             new_top = high if j == 0 else jnp.maximum(top, high)
             p = jnp.exp2((s - new_top) * scale)
-            part = jnp.sum(p, axis=1, keepdims=True)
             v = kv_s[2 * h + 1][j * chunk : (j + 1) * chunk, :]
+            v = jnp.concatenate([v, jnp.ones_like(v)], axis=1)
             out = jnp.dot(p.astype(jnp.bfloat16), v, preferred_element_type=jnp.float32)
+            out, part = out[:, :HD], out[:, HD:]
             if j == 0:
                 total, acc = part, out
             else:
@@ -156,11 +208,11 @@
         done = (acc / total).astype(jnp.bfloat16)
         keep[:, cols] = done[:half]
         send[:, cols] = done[half:]
-    for copy in copies[2 * heads :]:
+    for copy in copies[2 * heads - 2 :]:
         copy.wait()
 
 
-def attend(scalars, arrived, kv, w_keep, w_other):
+def attend(scalars, arrived, first, kv, w_keep, w_other):
     groups, rows, width = arrived.shape
     keys = kv.shape[1]
     heads = width // HD
@@ -170,46 +222,59 @@
     anywhere = pl.BlockSpec(memory_space=pl.ANY)
     return pl.pallas_call(
         functools.partial(attend_kernel, heads=heads, chunk=keys // CHUNKS),
-        in_specs=[pl.BlockSpec(memory_space=pltpu.SMEM), vmem] + [anywhere] * 3,
-        out_specs=[vmem] * 3,
+        in_specs=[pl.BlockSpec(memory_space=pltpu.SMEM), vmem, vmem] + [anywhere] * 3,
+        out_specs=[vmem] * 4,
         out_shape=[
             result,
             result,
             pltpu.VMEM((CORES,) + w_keep.shape, w_keep.dtype),
+            pltpu.VMEM(first.shape, first.dtype),
         ],
         scratch_shapes=[
             pltpu.VMEM((patch, width), jnp.bfloat16),
             pltpu.VMEM((2, patch, width), jnp.bfloat16),
-            pltpu.SemaphoreType.DMA((2 * heads + 2,)),
+            pltpu.SemaphoreType.DMA((2 * heads,)),
         ]
-        + [pltpu.VMEM((keys, HD), jnp.bfloat16)] * (2 * heads),
+        + [pltpu.VMEM((keys, HD), jnp.bfloat16)] * (2 * heads - 2),
+        input_output_aliases={2: 3},
         compiler_params=pltpu.CompilerParams(vmem_limit_bytes=ATTEND_VMEM),
         name="attend",
-    )(scalars, in_vmem(arrived), *map(in_hbm, (kv, w_keep, w_other)))
+    )(scalars, in_vmem(arrived), in_vmem(first), *map(in_hbm, (kv, w_keep, w_other)))
 
 
 def packed_width(size, tok):
     return size * tok // MAIN
 
 
-def project_kernel(keep, other, weights, out, rest_s, *, start, size):
+def project_kernel(keep, other, weights, out, out_s, rest_s, sems, *, start, size):
     peers = out.shape[0]
     cut = out.shape[2] - size
     cuts = size // cut
     rest = MAIN // cuts
     both = jnp.concatenate([keep[...], other[...]], axis=1)
+    copies = []
+
+    def leave(b):
+        cols = pl.ds(b * cut, cut)
+        copies.append(pltpu.make_async_copy(out_s.at[:, :, cols], out.at[:, :, cols], sems.at[b]))
+        copies[-1].start()
+
     for b in range(cuts):
         cols = slice(start + b * cut, start + (b + 1) * cut)
         w = jnp.concatenate([weights[i, :, cols] for i in range(CORES)], axis=0)
         y = jnp.dot(both, w, preferred_element_type=jnp.float32)
         for d in range(peers):
             rows = y[MAIN * d : MAIN * (d + 1)]
-            out[d, :, b * cut : (b + 1) * cut] = rows.astype(jnp.bfloat16)
+            out_s[d, :, b * cut : (b + 1) * cut] = rows.astype(jnp.bfloat16)
             for t in range(rest):
                 row = MAIN * peers + rest * d + t
                 rest_s[d, cuts * t + b : cuts * t + b + 1, :] = y[row : row + 1]
+        leave(b)
     for d in range(peers):
-        out[d, :, size:] = rest_s[d].astype(jnp.bfloat16)
+        out_s[d, :, size:] = rest_s[d].astype(jnp.bfloat16)
+    leave(cuts)
+    for copy in copies:
+        copy.wait()
 
 
 def project(keep, other, weights, peers, start, size):
@@ -219,9 +284,13 @@
     return pl.pallas_call(
         functools.partial(project_kernel, start=start, size=size),
         in_specs=[vmem] * 3,
-        out_specs=vmem,
-        out_shape=pltpu.VMEM((peers, MAIN, width), jnp.bfloat16),
-        scratch_shapes=[pltpu.VMEM((peers, MAIN, width - size), jnp.float32)],
+        out_specs=pl.BlockSpec(memory_space=pl.ANY),
+        out_shape=pltpu.HBM((peers, MAIN, width), jnp.bfloat16),
+        scratch_shapes=[
+            pltpu.VMEM((peers, MAIN, width), jnp.bfloat16),
+            pltpu.VMEM((peers, MAIN, width - size), jnp.float32),
+            pltpu.SemaphoreType.DMA((width // (width - size),)),
+        ],
         compiler_params=pltpu.CompilerParams(vmem_limit_bytes=VMEM_LIMIT),
         name=f"project_{start}",
     )(in_vmem(keep), in_vmem(other), in_vmem(weights))
@@ -293,7 +362,7 @@
     arrived = lax.all_to_all(blocked, "head", split_axis=0, concat_axis=0, tiled=True)
     kv = jnp.transpose(stale_kv[0], (1, 0, 2))
 
-    keep, send, weights = attend(scalars, arrived, kv, weight, weight_other)
+    keep, send, weights, _ = attend(scalars, arrived, prefetch(kv), kv, weight, weight_other)
     other = lax.ppermute(send, "head", swap)
     packed = stream(residual[0], gate, chunks)
     handed = []

time: 78.5 us -> 76.3 us (0.972)
  waiting for transfers between devices: 41.9 us -> 40.2 us
  local copies, waits for them, and re-layouts: 8.03 us -> 6.87 us
    pallas_call x1 -> x2, Pallas kernels: 1.25 us -> 3.85 us  [the longest x1 2.21 us: pack(): pl.pallas_call(functools.partial(pack_kernel, pieces=pieces), in_specs=[a...]
    pallas_call x1, Pallas kernels: 7.87 us -> 6.2 us  [attend(): pl.pallas_call(functools.partial(attend_kernel, heads=heads, chunk=keys /...]
    all_to_all x1, waiting for transfers between devices: 3.91 us -> 2.25 us  [shards(): lax.all_to_all(blocked, 'head', split_axis=0, concat_axis=0, tiled=True)]
    unnamed x7 -> x5, local copies, waits for them, and re-layouts: 8.03 us -> 6.87 us
  transfers between devices with their start and end apart: 5 -> 5, of which waited for: 4 -> 4; matrix products, arithmetic and copies ran while one was open for 9% -> 9% of each run, Pallas kernels for 2% -> 5%
where the time goes in v3:
time: 76.3 us; the launch traced here: 76 us
  waiting for transfers between devices  40.2 us (53%)
  starting transfers between devices  14.4 us (19%)
  Pallas kernels  13.8 us (18%)
  local copies, waits for them, and re-layouts  6.87 us (9%)
    all_to_all x1, waiting for transfers between devices, shards(): lax.all_to_all(sums, 'head', split_axis=0, concat_axis=0, tiled=True, axi...  22.7 us
    ppermute x1, waiting for transfers between devices, shards(): lax.ppermute(updated, 'section', [(j, (j + 1) % sections) for j in range(...  14 us
    unnamed x5, local copies, waits for them, and re-layouts  6.87 us
    pallas_call x1, Pallas kernels, attend(): pl.pallas_call(functools.partial(attend_kernel, heads=heads, chunk=keys /...  6.2 us
    all_to_all x1, starting transfers between devices, shards(): lax.all_to_all(blocked, 'head', split_axis=0, concat_axis=0, tiled=True)  6.07 us
    all_to_all x1, starting transfers between devices, shards(): lax.all_to_all(sums, 'head', split_axis=0, concat_axis=0, tiled=True, axi...  4.77 us
    ppermute x1, starting transfers between devices, shards(): lax.ppermute(updated, 'section', [(j, (j + 1) % sections) for j in range(...  3.35 us
    pallas_call x1, Pallas kernels, project(): pl.pallas_call(functools.partial(project_kernel, start=start, size=size),...  2.63 us
  transfers between devices with their start and end apart: 5, of which 4 were waited for; matrix products, arithmetic and copies ran while one was open for 9% of the time, Pallas kernels for 5%

profile of v3, /device:TPU:32, one launch (start us, length us, event | category | flops | bytes accessed | tf_op | source)
XLA Modules:
  0.0 76.0 jit_solution(8638061263372554720)
XLA Ops:
  0.0 0.0 collective-permute-start
  0.0 2.2 %pack.1 = bf16[16,54,384]{2,1,0:T(8,128)(2,1)} custom-call(bf16[1,18,3,6144]{3,2,1,0:T(4,128)(2,1)} %qkv.1), custom_call_target="tpu_custom_call" | custom-call | tf_op jit(solution)/shard_map/pack/pallas_call | solution.py:64
  2.2 6.1 %all-to-all-start = ((bf16[16,54,384]{2,1,0:T(8,128)(2,1)}), bf16[16,54,384]{2,1,0:T(8,128)(2,1)S(1)}, u32[]{:S(2)}, u32[]{:S(2)}) async-start(bf16[16,54,384]{2,1,0:T(8,128)(2,1)} %pack.1), calls=%async_computation | async-start | bytes 1376256 | tf_op jit(solution)/shard_map/all_to_all | solution.py:362
  8.9 6.9 %copy.10 = bf16[1,4608,2,384]{3,1,2,0:T(8,128)(2,1)} copy(bf16[1,4608,2,384]{3,2,1,0:T(2,128)(2,1)} %param.7) | data formatting | bytes 14155776 | tf_op args[1]
  15.8 1.6 %prefetch.1.first_in = bf16[2,4608,128]{2,1,0:T(8,128)(2,1)S(1)} custom-call(bf16[2,4608,384]{2,1,0:T(8,128)(2,1)} %bitcast.10), custom_call_target="tpu_custom_call" | custom-call | tf_op jit(solution)/shard_map/prefetch/pallas_call | solution.py:124
  17.5 0.1 pad_add_fusion.scalars
  17.5 2.3 %all-to-all-done.arrived = bf16[16,54,384]{2,1,0:T(8,128)(2,1)S(1)} async-done(((bf16[16,54,384]{2,1,0:T(8,128)(2,1)}), bf16[16,54,384]{2,1,0:T(8,128)(2,1)S(1)}, u32[]{:S(2)}, u32[]{:S(2)}) %all-to-all-start) | async-done | bytes 663584 | tf_op jit(solution)/shard_map/all_to_all | solution.py:362
  19.8 0.0 collective-permute-done.w_other
  19.8 6.2 %attend.1 = (bf16[144,384]{1,0:T(8,128)(2,1)S(1)}, bf16[144,384]{1,0:T(8,128)(2,1)S(1)}, bf16[2,384,6144]{2,1,0:T(8,128)(2,1)S(1)}, bf16[2,4608,128]{2,1,0:T(8,128)(2,1)S(1)}) custom-call(s32[2]{0:T(128)S(1)} %pad_add_fusion.scalars, bf16[16,54,384]{2,1,0:T(8,128)(2,1)S(1)} %all-to-all-done.arrived, ...), custom_call_target="tpu_custom_call", output_to_operand_aliasing={{3}: (2, {})} | custom-call | tf_op jit(solution)/shard_map/attend/pallas_call | solution.py:223
  26.0 0.2 collective-permute-start.1
  26.2 1.2 %collective-permute-done.1.other = bf16[144,384]{1,0:T(8,128)(2,1)S(1)} collective-permute-done((bf16[144,384]{1,0:T(8,128)(2,1)S(1)}, bf16[144,384]{1,0:T(8,128)(2,1)S(1)}, u32[]{:S(2)}, u32[]{:S(2)}) %collective-permute-start.1) | collective-permute-done | bytes 110624 | tf_op jit(solution)/shard_map/ppermute | solution.py:366
  27.4 0.0 copy-start
  27.4 0.0 copy-start.1
  27.4 2.6 %project_0.1 = bf16[8,16,6912]{2,1,0:T(8,128)(2,1)} custom-call(bf16[144,384]{1,0:T(8,128)(2,1)S(1)} %get-tuple-element.10.keep, bf16[144,384]{1,0:T(8,128)(2,1)S(1)} %collective-permute-done.1.other, bf16[2,384,6144]{2,1,0:T(8,128)(2,1)S(1)} %get-tuple-element.12.weights), custom_call_target="tpu_custom_call" | custom-call | tf_op jit(solution)/shard_map/project_0/pallas_call | solution.py:284
  30.0 4.8 %all-to-all-start.1 = ((bf16[8,16,6912]{2,1,0:T(8,128)(2,1)}), bf16[8,16,6912]{2,1,0:T(8,128)(2,1)S(1)}, u32[]{:S(2)}, u32[]{:S(2)}) async-start(bf16[8,16,6912]{2,1,0:T(8,128)(2,1)} %project_0.1), calls=%async_computation.1 | async-start | bytes 3538944 | tf_op jit(solution)/shard_map/all_to_all | solution.py:371
  34.8 0.0 copy-done
  34.8 0.0 copy-done.1
  34.8 0.1 stream.1
  34.9 22.7 %all-to-all-done.1.parts = bf16[8,16,6912]{2,1,0:T(8,128)(2,1)S(1)} async-done(((bf16[8,16,6912]{2,1,0:T(8,128)(2,1)}), bf16[8,16,6912]{2,1,0:T(8,128)(2,1)S(1)}, u32[]{:S(2)}, u32[]{:S(2)}) %all-to-all-start.1) | async-done | bytes 1769504 | tf_op jit(solution)/shard_map/all_to_all | solution.py:371
  57.6 0.3 update.1
  57.9 3.4 %collective-permute-start.2 = (bf16[16,6912]{1,0:T(8,128)(2,1)S(1)}, bf16[16,6912]{1,0:T(8,128)(2,1)S(1)}, u32[]{:S(2)}, u32[]{:S(2)}) collective-permute-start(bf16[16,6912]{1,0:T(8,128)(2,1)S(1)} %update.1), channel_id=1, source_target_pairs={{0,16},{16,32},{32,48},{48,64},{64,80},{80,96},{96,112},{112,128},... | collective-permute-start | bytes 663560 | tf_op jit(solution)/shard_map/ppermute | solution.py:376
  61.3 14.0 %collective-permute-done.2.refs_0_ = bf16[16,6912]{1,0:T(8,128)(2,1)S(1)} collective-permute-done((bf16[16,6912]{1,0:T(8,128)(2,1)S(1)}, bf16[16,6912]{1,0:T(8,128)(2,1)S(1)}, u32[]{:S(2)}, u32[]{:S(2)}) %collective-permute-start.2) | collective-permute-done | bytes 221216 | tf_op jit(solution)/shard_map/ppermute | solution.py:376
  75.3 0.8 unpack.1
Async XLA Ops:
  0.0 19.8 %collective-permute-start = (bf16[384,6144]{1,0:T(8,128)(2,1)}, bf16[384,6144]{1,0:T(8,128)(2,1)}, u32[]{:S(2)}, u32[]{:S(2)}) collective-permute-start(bf16[384,6144]{1,0:T(8,128)(2,1)} %bitcast.12), channel_id=1, source_target_pairs={{0,1},{1,0},{2,3},{3,2},{4,5},{5,4},{6,7},{7,6},{8,9},{9,8},{10,11... | collective-permute-start | bytes 14155784 | tf_op jit(solution)/shard_map/ppermute | solution.py:360
  2.2 17.6 %all-to-all-start = ((bf16[16,54,384]{2,1,0:T(8,128)(2,1)}), bf16[16,54,384]{2,1,0:T(8,128)(2,1)S(1)}, u32[]{:S(2)}, u32[]{:S(2)}) async-start(bf16[16,54,384]{2,1,0:T(8,128)(2,1)} %pack.1), calls=%async_computation | async-start | bytes 1376256 | tf_op jit(solution)/shard_map/all_to_all | solution.py:362
  26.0 1.4 %collective-permute-start.1 = (bf16[144,384]{1,0:T(8,128)(2,1)S(1)}, bf16[144,384]{1,0:T(8,128)(2,1)S(1)}, u32[]{:S(2)}, u32[]{:S(2)}) collective-permute-start(bf16[144,384]{1,0:T(8,128)(2,1)S(1)} %get-tuple-element.11), channel_id=1, source_target_pairs={{0,1},{1,0},{2,3},{3,2},{4,5},{5,4},{6,7},{7,6},{8,9},{9,8},{10,11... | collective-permute-start | bytes 331784 | tf_op jit(solution)/shard_map/ppermute | solution.py:366
  27.4 7.4 %copy-start = (bf16[1,18,6144]{2,1,0:T(8,128)(2,1)S(1)}, bf16[1,18,6144]{2,1,0:T(8,128)(2,1)}, u32[]{:S(2)}) copy-start(bf16[1,18,6144]{2,1,0:T(8,128)(2,1)} %param.9) | copy-start | bytes 663556
  27.4 7.4 %copy-start.1 = (f32[1,6144]{1,0:T(1,128)S(1)}, f32[1,6144]{1,0:T(1,128)}, u32[]{:S(2)}) copy-start(f32[1,6144]{1,0:T(1,128)} %gate.1) | copy-start | bytes 73732
  30.0 27.6 %all-to-all-start.1 = ((bf16[8,16,6912]{2,1,0:T(8,128)(2,1)}), bf16[8,16,6912]{2,1,0:T(8,128)(2,1)S(1)}, u32[]{:S(2)}, u32[]{:S(2)}) async-start(bf16[8,16,6912]{2,1,0:T(8,128)(2,1)} %project_0.1), calls=%async_computation.1 | async-start | bytes 3538944 | tf_op jit(solution)/shard_map/all_to_all | solution.py:371
  57.9 17.3 %collective-permute-start.2 = (bf16[16,6912]{1,0:T(8,128)(2,1)S(1)}, bf16[16,6912]{1,0:T(8,128)(2,1)S(1)}, u32[]{:S(2)}, u32[]{:S(2)}) collective-permute-start(bf16[16,6912]{1,0:T(8,128)(2,1)S(1)} %update.1), channel_id=1, source_target_pairs={{0,16},{16,32},{32,48},{48,64},{64,80},{80,96},{96,112},{112,128},... | collective-permute-start | bytes 663560 | tf_op jit(solution)/shard_map/ppermute | solution.py:376

commit v4 on v3

--- a/solution.py
+++ b/solution.py
@@ -10,8 +10,10 @@
 
 HD = 128
 CORES = 2
+PAIR = 2
+PLACES = ((0, 0), (0, 1), (2, 0), (2, 1), (1, 0), (1, 1), (3, 0), (3, 1))
 MAIN = 16
-SPLIT = (1,)
+SPLIT = (1, 1)
 CHUNKS = 6
 ATTEND_VMEM = 36 * 2**20
 VMEM_LIMIT = 8 * 2**20
@@ -155,11 +157,14 @@
     patch = tok * groups
     rest = tok - MAIN
     scale = math.log2(math.e) / math.sqrt(HD)
-    core = scalars[1]
+    core = lax.rem(scalars[1], CORES)
+    here = lax.div(scalars[1], CORES)
+    y_here, z_here = lax.div(here, PAIR), lax.rem(here, PAIR)
     for side in range(CORES):
         which = core if side == 0 else 1 - core
-        for k in range(peers):
-            block = arrived[CORES * k + which]
+        for k, (dy, dz) in enumerate(PLACES):
+            chip = lax.rem(y_here + dy, peers // PAIR) * PAIR + lax.rem(z_here + dz, PAIR)
+            block = arrived[CORES * chip + which]
             for t in range(3):
                 target = q_s if t == 0 else fresh_s.at[t - 1]
                 rows = block[t * tok : (t + 1) * tok]
@@ -246,35 +251,25 @@
     return size * tok // MAIN
 
 
-def project_kernel(keep, other, weights, out, out_s, rest_s, sems, *, start, size):
-    peers = out.shape[0]
-    cut = out.shape[2] - size
+def project_kernel(keep, other, weights, stay, across, ahead, behind, rest_s, *, start, size):
+    blocks = [ref.at[n] for ref in (stay, across, ahead, behind) for n in range(ref.shape[0])]
+    peers = len(blocks)
+    cut = stay.shape[2] - size
     cuts = size // cut
     rest = MAIN // cuts
     both = jnp.concatenate([keep[...], other[...]], axis=1)
-    copies = []
-
-    def leave(b):
-        cols = pl.ds(b * cut, cut)
-        copies.append(pltpu.make_async_copy(out_s.at[:, :, cols], out.at[:, :, cols], sems.at[b]))
-        copies[-1].start()
-
     for b in range(cuts):
         cols = slice(start + b * cut, start + (b + 1) * cut)
         w = jnp.concatenate([weights[i, :, cols] for i in range(CORES)], axis=0)
         y = jnp.dot(both, w, preferred_element_type=jnp.float32)
         for d in range(peers):
             rows = y[MAIN * d : MAIN * (d + 1)]
-            out_s[d, :, b * cut : (b + 1) * cut] = rows.astype(jnp.bfloat16)
+            blocks[d][:, b * cut : (b + 1) * cut] = rows.astype(jnp.bfloat16)
             for t in range(rest):
                 row = MAIN * peers + rest * d + t
                 rest_s[d, cuts * t + b : cuts * t + b + 1, :] = y[row : row + 1]
-        leave(b)
     for d in range(peers):
-        out_s[d, :, size:] = rest_s[d].astype(jnp.bfloat16)
-    leave(cuts)
-    for copy in copies:
-        copy.wait()
+        blocks[d][:, size:] = rest_s[d].astype(jnp.bfloat16)
 
 
 def project(keep, other, weights, peers, start, size):
@@ -284,35 +279,52 @@
     return pl.pallas_call(
         functools.partial(project_kernel, start=start, size=size),
         in_specs=[vmem] * 3,
-        out_specs=pl.BlockSpec(memory_space=pl.ANY),
-        out_shape=pltpu.HBM((peers, MAIN, width), jnp.bfloat16),
-        scratch_shapes=[
-            pltpu.VMEM((peers, MAIN, width), jnp.bfloat16),
-            pltpu.VMEM((peers, MAIN, width - size), jnp.float32),
-            pltpu.SemaphoreType.DMA((width // (width - size),)),
-        ],
+        out_specs=[vmem] * 4,
+        out_shape=[pltpu.VMEM((n, MAIN, width), jnp.bfloat16) for n in (3, 1, 2, 2)],
+        scratch_shapes=[pltpu.VMEM((peers, MAIN, width - size), jnp.float32)],
         compiler_params=pltpu.CompilerParams(vmem_limit_bytes=VMEM_LIMIT),
         name=f"project_{start}",
     )(in_vmem(keep), in_vmem(other), in_vmem(weights))
 
 
-def update_kernel(parts, residual, gate, out):
-    total = parts[0].astype(jnp.float32)
-    for d in range(1, parts.shape[0]):
-        total = total + parts[d].astype(jnp.float32)
+def add_kernel(*refs, picks):
+    total = None
+    for ref, pick in zip(refs, picks):
+        term = ref[pick].astype(jnp.float32)
+        total = term if total is None else total + term
+    refs[-1][...] = total.astype(jnp.bfloat16)
+
+
+def add(arrays, picks, name):
+    vmem = pl.BlockSpec(memory_space=pltpu.VMEM)
+    return pl.pallas_call(
+        functools.partial(add_kernel, picks=picks),
+        in_specs=[vmem] * len(arrays),
+        out_specs=vmem,
+        out_shape=pltpu.VMEM(arrays[0].shape[1:], jnp.bfloat16),
+        compiler_params=pltpu.CompilerParams(vmem_limit_bytes=VMEM_LIMIT),
+        name=name,
+    )(*map(in_vmem, arrays))
+
+
+def update_kernel(*refs):
+    residual, gate, out = refs[-3:]
+    total = refs[0][0].astype(jnp.float32)
+    for ref in refs[1:-3]:
+        total = total + ref[0].astype(jnp.float32)
     out[...] = (residual[...] + gate[...] * total).astype(jnp.bfloat16)
 
 
-def update(parts, residual, gate):
+def update(arrays, residual, gate, name):
     vmem = pl.BlockSpec(memory_space=pltpu.VMEM)
     return pl.pallas_call(
         update_kernel,
-        in_specs=[vmem] * 3,
+        in_specs=[vmem] * (len(arrays) + 2),
         out_specs=vmem,
-        out_shape=pltpu.VMEM(parts.shape[1:], jnp.bfloat16),
-        compiler_params=pltpu.CompilerParams(vmem_limit_bytes=VMEM_LIMIT),
-        name="update",
-    )(in_vmem(parts), in_vmem(residual), in_vmem(gate))
+        out_shape=pltpu.VMEM(residual.shape, jnp.bfloat16),
+        compiler_params=pltpu.CompilerParams(vmem_limit_bytes=VMEM_LIMIT),
+        name=name,
+    )(*map(in_vmem, (*arrays, residual, gate)))
 
 
 def unpack_kernel(*refs, chunks):
@@ -348,14 +360,12 @@
     tok = qkv.shape[1]
     columns = out_weight.shape[2]
     swap = [(i, i ^ 1) for i in range(groups)]
-    same_core = [[CORES * k + c for k in range(peers)] for c in range(CORES)]
     chunks = []
     for parts in SPLIT:
         start = sum(size for _, size in chunks)
         chunks.append((start, columns * parts // sum(SPLIT)))
 
-    core = lax.axis_index("head") % CORES
-    scalars = jnp.stack([patch_of_section[0], core.astype(jnp.int32)])
+    scalars = jnp.stack([patch_of_section[0], lax.axis_index("head").astype(jnp.int32)])
     weight = out_weight[0]
     weight_other = lax.ppermute(weight, "head", swap)
     blocked = pack(qkv, groups)
@@ -365,16 +375,25 @@
     keep, send, weights, _ = attend(scalars, arrived, prefetch(kv), kv, weight, weight_other)
     other = lax.ppermute(send, "head", swap)
     packed = stream(residual[0], gate, chunks)
+    forward = [(j, (j + 1) % sections) for j in range(sections)]
+
+    def along(x, dy, dz):
+        route = [(i, (i + dy * PAIR * CORES) % groups ^ dz * CORES) for i in range(groups)]
+        return lax.ppermute(x, "head", route)
+
     handed = []
     for i, (start, size) in enumerate(chunks):
-        sums = project(keep, other, weights, peers, start, size)
-        parts = lax.all_to_all(
-            sums, "head", split_axis=0, concat_axis=0, tiled=True, axis_index_groups=same_core
-        )
-        updated = update(parts, packed[2 * i], packed[2 * i + 1])
-        handed.append(
-            lax.ppermute(updated, "section", [(j, (j + 1) % sections) for j in range(sections)])
-        )
+        stay, across, ahead, behind = project(keep, other, weights, peers, start, size)
+        from_z = along(across, 0, 1)
+        from_last = along(ahead, 1, 0)
+        from_next = along(behind, -1, 0)
+        opposite = add((stay, from_z), (2, 0), f"opposite_{i}")
+        from_opposite = along(opposite[None], 2, 0)
+        pair = add((stay, from_last, from_next), (1, 1, 1), f"pair_{i}")
+        from_pair = along(pair[None], 0, 1)
+        terms = (stay, from_last, from_next, from_opposite, from_pair)
+        updated = update(terms, packed[2 * i], packed[2 * i + 1], f"update_{i}")
+        handed.append(lax.ppermute(updated, "section", forward))
     return unpack(handed, tok, columns, chunks)[None]
 
 

time: 76.3 us -> 67.5 us (0.88)
  waiting for transfers between devices: 40.2 us -> 18.7 us
  starting transfers between devices: 14.4 us -> 27.4 us
    all_to_all x1 -> x0, waiting for transfers between devices: 22.7 us -> none  [shards(): lax.all_to_all(sums, 'head', split_axis=0, concat_axis=0, tiled=True, axi...]
    ppermute x1 -> x12, starting transfers between devices: 3.35 us -> 21.1 us  [the longest x10 14.4 us: along(): return lax.ppermute(x, 'head', route)]
    all_to_all x1 -> x0, starting transfers between devices: 4.77 us -> none  [shards(): lax.all_to_all(sums, 'head', split_axis=0, concat_axis=0, tiled=True, axi...]
    ppermute x1 -> x12, waiting for transfers between devices: 14 us -> 15.2 us  [the longest x2 9.29 us: shards(): handed.append(lax.ppermute(updated, 'section', forward))]
    pallas_call x1 -> x2, Pallas kernels: 2.63 us -> 2.25 us  [project(): pl.pallas_call(functools.partial(project_kernel, start=start, size=size),...]
  transfers between devices with their start and end apart: 5 -> 15, of which waited for: 4 -> 7; matrix products, arithmetic and copies ran while one was open for 9% -> 10% of each run, Pallas kernels for 5% -> 8%
where the time goes in v4:
time: 67.5 us; the launch traced here: 67.3 us
  starting transfers between devices  27.4 us (41%)
  waiting for transfers between devices  18.7 us (28%)
  Pallas kernels  13.6 us (20%)
  local copies, waits for them, and re-layouts  6.78 us (10%)
  between operations  0.76 us (1%)
    ppermute x10, starting transfers between devices, along(): return lax.ppermute(x, 'head', route)  14.4 us
    ppermute x2, waiting for transfers between devices, shards(): handed.append(lax.ppermute(updated, 'section', forward))  9.29 us
    unnamed x5, local copies, waits for them, and re-layouts  6.78 us
    ppermute x2, starting transfers between devices, shards(): handed.append(lax.ppermute(updated, 'section', forward))  6.73 us
    pallas_call x1, Pallas kernels, attend(): pl.pallas_call(functools.partial(attend_kernel, heads=heads, chunk=keys /...  6.28 us
    all_to_all x1, starting transfers between devices, shards(): lax.all_to_all(blocked, 'head', split_axis=0, concat_axis=0, tiled=True)  6.07 us
    ppermute x10, waiting for transfers between devices, along(): return lax.ppermute(x, 'head', route)  5.87 us
    all_to_all x1, waiting for transfers between devices, shards(): lax.all_to_all(blocked, 'head', split_axis=0, concat_axis=0, tiled=True)  2.34 us
  transfers between devices with their start and end apart: 15, of which 7 were waited for; matrix products, arithmetic and copies ran while one was open for 10% of the time, Pallas kernels for 8%

profile of v4, /device:TPU:32, one launch (start us, length us, event | category | flops | bytes accessed | tf_op | source)
XLA Modules:
  0.0 67.3 jit_solution(1632689883134427187)
XLA Ops:
  0.0 0.0 collective-permute-start
  0.0 2.2 %pack.1 = bf16[16,54,384]{2,1,0:T(8,128)(2,1)} custom-call(bf16[1,18,3,6144]{3,2,1,0:T(4,128)(2,1)} %qkv.1), custom_call_target="tpu_custom_call" | custom-call | tf_op jit(solution)/shard_map/pack/pallas_call | solution.py:66
  2.2 6.1 %all-to-all-start = ((bf16[16,54,384]{2,1,0:T(8,128)(2,1)}), bf16[16,54,384]{2,1,0:T(8,128)(2,1)S(1)}, u32[]{:S(2)}, u32[]{:S(2)}) async-start(bf16[16,54,384]{2,1,0:T(8,128)(2,1)} %pack.1), calls=%async_computation | async-start | bytes 1376256 | tf_op jit(solution)/shard_map/all_to_all | solution.py:372
  8.3 6.8 %copy.10 = bf16[1,4608,2,384]{3,1,2,0:T(8,128)(2,1)} copy(bf16[1,4608,2,384]{3,2,1,0:T(2,128)(2,1)} %param.7) | data formatting | bytes 14155776 | tf_op args[1]
  15.1 1.6 %prefetch.1.first_in = bf16[2,4608,128]{2,1,0:T(8,128)(2,1)S(1)} custom-call(bf16[2,4608,384]{2,1,0:T(8,128)(2,1)} %bitcast.18), custom_call_target="tpu_custom_call" | custom-call | tf_op jit(solution)/shard_map/prefetch/pallas_call | solution.py:126
  17.4 0.1 pad_add_fusion.scalars
  17.4 2.3 %all-to-all-done.arrived = bf16[16,54,384]{2,1,0:T(8,128)(2,1)S(1)} async-done(((bf16[16,54,384]{2,1,0:T(8,128)(2,1)}), bf16[16,54,384]{2,1,0:T(8,128)(2,1)S(1)}, u32[]{:S(2)}, u32[]{:S(2)}) %all-to-all-start) | async-done | bytes 663584 | tf_op jit(solution)/shard_map/all_to_all | solution.py:372
  19.8 0.0 collective-permute-done.w_other
  19.8 6.3 %attend.1 = (bf16[144,384]{1,0:T(8,128)(2,1)S(1)}, bf16[144,384]{1,0:T(8,128)(2,1)S(1)}, bf16[2,384,6144]{2,1,0:T(8,128)(2,1)S(1)}, bf16[2,4608,128]{2,1,0:T(8,128)(2,1)S(1)}) custom-call(s32[2]{0:T(128)S(1)} %pad_add_fusion.scalars, bf16[16,54,384]{2,1,0:T(8,128)(2,1)S(1)} %all-to-all-done.arrived, ...), custom_call_target="tpu_custom_call", output_to_operand_aliasing={{3}: (2, {})} | custom-call | tf_op jit(solution)/shard_map/attend/pallas_call | solution.py:228
  26.1 0.2 collective-permute-start.1
  26.3 1.2 %collective-permute-done.1.other = bf16[144,384]{1,0:T(8,128)(2,1)S(1)} collective-permute-done((bf16[144,384]{1,0:T(8,128)(2,1)S(1)}, bf16[144,384]{1,0:T(8,128)(2,1)S(1)}, u32[]{:S(2)}, u32[]{:S(2)}) %collective-permute-start.1) | collective-permute-done | bytes 110624 | tf_op jit(solution)/shard_map/ppermute | solution.py:376
  27.5 1.1 %project_3072.1 = (bf16[3,16,3456]{2,1,0:T(8,128)(2,1)S(1)}, bf16[1,16,3456]{2,1,0:T(8,128)(2,1)S(1)}, bf16[2,16,3456]{2,1,0:T(8,128)(2,1)S(1)}, bf16[2,16,3456]{2,1,0:T(8,128)(2,1)S(1)}) custom-call(bf16[144,384]{1,0:T(8,128)(2,1)S(1)} %get-tuple-element.20.keep, bf16[144,384]{1,0:T(8,128)(2,1)S(1)} %collective-permute-done.1.other, ...), custom_call_target="tpu_custom_call" | custom-call | tf_op jit(solution)/shard_map/project_3072/pallas_call | solution.py:279
  28.6 1.4 %collective-permute-start.10 = (bf16[1,16,3456]{2,1,0:T(8,128)(2,1)S(1)}, bf16[1,16,3456]{2,1,0:T(8,128)(2,1)S(1)}, u32[]{:S(2)}, u32[]{:S(2)}) collective-permute-start(bf16[1,16,3456]{2,1,0:T(8,128)(2,1)S(1)} %get-tuple-element.32), channel_id=1, source_target_pairs={{0,2},{1,3},{2,0},{3,1},{4,6},{5,7},{6,4},{7,5},{8,10},{9,11},{10,... | collective-permute-start | bytes 331784 | tf_op jit(solution)/shard_map/ppermute | solution.py:382
  30.0 0.0 collective-permute-start.8
  30.0 0.0 copy-start
  30.0 0.0 copy-start.1
  30.0 3.2 %collective-permute-start.9 = (bf16[2,16,3456]{2,1,0:T(8,128)(2,1)S(1)}, bf16[2,16,3456]{2,1,0:T(8,128)(2,1)S(1)}, u32[]{:S(2)}, u32[]{:S(2)}) collective-permute-start(bf16[2,16,3456]{2,1,0:T(8,128)(2,1)S(1)} %get-tuple-element.31), channel_id=1, source_target_pairs={{0,12},{1,13},{2,14},{3,15},{4,0},{5,1},{6,2},{7,3},{8,4},{9,5},{1... | collective-permute-start | bytes 663560 | tf_op jit(solution)/shard_map/ppermute | solution.py:382
  33.2 1.1 %project_0.1 = (bf16[3,16,3456]{2,1,0:T(8,128)(2,1)S(1)}, bf16[1,16,3456]{2,1,0:T(8,128)(2,1)S(1)}, bf16[2,16,3456]{2,1,0:T(8,128)(2,1)S(1)}, bf16[2,16,3456]{2,1,0:T(8,128)(2,1)S(1)}) custom-call(bf16[144,384]{1,0:T(8,128)(2,1)S(1)} %get-tuple-element.20.keep, bf16[144,384]{1,0:T(8,128)(2,1)S(1)} %collective-permute-done.1.other, ...), custom_call_target="tpu_custom_call" | custom-call | tf_op jit(solution)/shard_map/project_0/pallas_call | solution.py:279
  34.3 0.1 collective-permute-start.2
  34.4 3.2 %collective-permute-start.3 = (bf16[2,16,3456]{2,1,0:T(8,128)(2,1)S(1)}, bf16[2,16,3456]{2,1,0:T(8,128)(2,1)S(1)}, u32[]{:S(2)}, u32[]{:S(2)}) collective-permute-start(bf16[2,16,3456]{2,1,0:T(8,128)(2,1)S(1)} %get-tuple-element.25), channel_id=1, source_target_pairs={{0,12},{1,13},{2,14},{3,15},{4,0},{5,1},{6,2},{7,3},{8,4},{9,5},{1... | collective-permute-start | bytes 663560 | tf_op jit(solution)/shard_map/ppermute | solution.py:382
  37.7 0.0 collective-permute-done.10.refs_1_
  37.7 0.8 %collective-permute-start.4 = (bf16[1,16,3456]{2,1,0:T(8,128)(2,1)S(1)}, bf16[1,16,3456]{2,1,0:T(8,128)(2,1)S(1)}, u32[]{:S(2)}, u32[]{:S(2)}) collective-permute-start(bf16[1,16,3456]{2,1,0:T(8,128)(2,1)S(1)} %get-tuple-element.26), channel_id=1, source_target_pairs={{0,2},{1,3},{2,0},{3,1},{4,6},{5,7},{6,4},{7,5},{8,10},{9,11},{10,... | collective-permute-start | bytes 331784 | tf_op jit(solution)/shard_map/ppermute | solution.py:382
  38.5 4.0 %collective-permute-done.4.refs_1_ = bf16[1,16,3456]{2,1,0:T(8,128)(2,1)S(1)} collective-permute-done((bf16[1,16,3456]{2,1,0:T(8,128)(2,1)S(1)}, bf16[1,16,3456]{2,1,0:T(8,128)(2,1)S(1)}, u32[]{:S(2)}, u32[]{:S(2)}) %collective-permute-start.4) | collective-permute-done | bytes 110624 | tf_op jit(solution)/shard_map/ppermute | solution.py:382
  42.4 0.0 collective-permute-start.11
  42.4 0.0 collective-permute-done.8.refs_1_
  42.5 0.0 collective-permute-done.9.refs_2_
  42.5 0.8 %collective-permute-start.12 = (bf16[1,16,3456]{2,1,0:T(8,128)(2,1)S(1)}, bf16[1,16,3456]{2,1,0:T(8,128)(2,1)S(1)}, u32[]{:S(2)}, u32[]{:S(2)}) collective-permute-start(bf16[1,16,3456]{2,1,0:T(8,128)(2,1)S(1)} %bitcast.15), channel_id=1, source_target_pairs={{0,2},{1,3},{2,0},{3,1},{4,6},{5,7},{6,4},{7,5},{8,10},{9,11},{10,... | collective-permute-start | bytes 331784 | tf_op jit(solution)/shard_map/ppermute | solution.py:382
  43.4 3.5 %collective-permute-start.5 = (bf16[1,16,3456]{2,1,0:T(8,128)(2,1)S(1)}, bf16[1,16,3456]{2,1,0:T(8,128)(2,1)S(1)}, u32[]{:S(2)}, u32[]{:S(2)}) collective-permute-start(bf16[1,16,3456]{2,1,0:T(8,128)(2,1)S(1)} %bitcast.16), channel_id=1, source_target_pairs={{0,8},{1,9},{2,10},{3,11},{4,12},{5,13},{6,14},{7,15},{8,0},{9,1},... | collective-permute-start | bytes 331784 | tf_op jit(solution)/shard_map/ppermute | solution.py:382
  46.9 0.0 collective-permute-done.2.refs_1_
  46.9 0.0 collective-permute-done.3.refs_2_
  47.0 1.4 %collective-permute-start.6 = (bf16[1,16,3456]{2,1,0:T(8,128)(2,1)S(1)}, bf16[1,16,3456]{2,1,0:T(8,128)(2,1)S(1)}, u32[]{:S(2)}, u32[]{:S(2)}) collective-permute-start(bf16[1,16,3456]{2,1,0:T(8,128)(2,1)S(1)} %bitcast.14), channel_id=1, source_target_pairs={{0,2},{1,3},{2,0},{3,1},{4,6},{5,7},{6,4},{7,5},{8,10},{9,11},{10,... | collective-permute-start | bytes 331784 | tf_op jit(solution)/shard_map/ppermute | solution.py:382
  48.3 0.0 copy-done
  48.3 0.0 copy-done.1
  48.3 0.1 stream.1
  48.4 0.3 collective-permute-done.11.refs_3_
  48.7 0.0 collective-permute-done.12.refs_4_
  48.7 0.1 update_1.1
  48.8 3.3 %collective-permute-start.13 = (bf16[16,3456]{1,0:T(8,128)(2,1)S(1)}, bf16[16,3456]{1,0:T(8,128)(2,1)S(1)}, u32[]{:S(2)}, u32[]{:S(2)}) collective-permute-start(bf16[16,3456]{1,0:T(8,128)(2,1)S(1)} %update_1.1), channel_id=1, source_target_pairs={{0,16},{16,32},{32,48},{48,64},{64,80},{80,96},{96,112},{112,128},... | collective-permute-start | bytes 331784 | tf_op jit(solution)/shard_map/ppermute | solution.py:396
  52.1 0.0 collective-permute-done.5.refs_3_
  52.1 1.6 %collective-permute-done.6.refs_4_ = bf16[1,16,3456]{2,1,0:T(8,128)(2,1)S(1)} collective-permute-done((bf16[1,16,3456]{2,1,0:T(8,128)(2,1)S(1)}, bf16[1,16,3456]{2,1,0:T(8,128)(2,1)S(1)}, u32[]{:S(2)}, u32[]{:S(2)}) %collective-permute-start.6) | collective-permute-done | bytes 110624 | tf_op jit(solution)/shard_map/ppermute | solution.py:382
  53.7 0.1 update_0.1
  53.9 3.4 %collective-permute-start.7 = (bf16[16,3456]{1,0:T(8,128)(2,1)S(1)}, bf16[16,3456]{1,0:T(8,128)(2,1)S(1)}, u32[]{:S(2)}, u32[]{:S(2)}) collective-permute-start(bf16[16,3456]{1,0:T(8,128)(2,1)S(1)} %update_0.1), channel_id=1, source_target_pairs={{0,16},{16,32},{32,48},{48,64},{64,80},{80,96},{96,112},{112,128},... | collective-permute-start | bytes 331784 | tf_op jit(solution)/shard_map/ppermute | solution.py:396
  57.2 3.3 %collective-permute-done.13.refs_1_ = bf16[16,3456]{1,0:T(8,128)(2,1)S(1)} collective-permute-done((bf16[16,3456]{1,0:T(8,128)(2,1)S(1)}, bf16[16,3456]{1,0:T(8,128)(2,1)S(1)}, u32[]{:S(2)}, u32[]{:S(2)}) %collective-permute-start.13) | collective-permute-done | bytes 110624 | tf_op jit(solution)/shard_map/ppermute | solution.py:396
  60.5 6.0 %collective-permute-done.7.refs_0_ = bf16[16,3456]{1,0:T(8,128)(2,1)S(1)} collective-permute-done((bf16[16,3456]{1,0:T(8,128)(2,1)S(1)}, bf16[16,3456]{1,0:T(8,128)(2,1)S(1)}, u32[]{:S(2)}, u32[]{:S(2)}) %collective-permute-start.7) | collective-permute-done | bytes 110624 | tf_op jit(solution)/shard_map/ppermute | solution.py:396
  66.5 0.7 %unpack.1 = bf16[18,6144]{1,0:T(8,128)(2,1)} custom-call(bf16[16,3456]{1,0:T(8,128)(2,1)S(1)} %collective-permute-done.7.refs_0_, bf16[16,3456]{1,0:T(8,128)(2,1)S(1)} %collective-permute-done.13.refs_1_), custom_call_target="tpu_custom_call" | custom-call | tf_op jit(solution)/shard_map/unpack/pallas_call | solution.py:346
  (4 shorter events, 0.2 us)
Async XLA Ops:
  0.0 19.8 %collective-permute-start = (bf16[384,6144]{1,0:T(8,128)(2,1)}, bf16[384,6144]{1,0:T(8,128)(2,1)}, u32[]{:S(2)}, u32[]{:S(2)}) collective-permute-start(bf16[384,6144]{1,0:T(8,128)(2,1)} %bitcast.20), channel_id=1, source_target_pairs={{0,1},{1,0},{2,3},{3,2},{4,5},{5,4},{6,7},{7,6},{8,9},{9,8},{10,11... | collective-permute-start | bytes 14155784 | tf_op jit(solution)/shard_map/ppermute | solution.py:370
  2.2 17.6 %all-to-all-start = ((bf16[16,54,384]{2,1,0:T(8,128)(2,1)}), bf16[16,54,384]{2,1,0:T(8,128)(2,1)S(1)}, u32[]{:S(2)}, u32[]{:S(2)}) async-start(bf16[16,54,384]{2,1,0:T(8,128)(2,1)} %pack.1), calls=%async_computation | async-start | bytes 1376256 | tf_op jit(solution)/shard_map/all_to_all | solution.py:372
  26.1 1.4 %collective-permute-start.1 = (bf16[144,384]{1,0:T(8,128)(2,1)S(1)}, bf16[144,384]{1,0:T(8,128)(2,1)S(1)}, u32[]{:S(2)}, u32[]{:S(2)}) collective-permute-start(bf16[144,384]{1,0:T(8,128)(2,1)S(1)} %get-tuple-element.21), channel_id=1, source_target_pairs={{0,1},{1,0},{2,3},{3,2},{4,5},{5,4},{6,7},{7,6},{8,9},{9,8},{10,11... | collective-permute-start | bytes 331784 | tf_op jit(solution)/shard_map/ppermute | solution.py:376
  28.6 9.0 %collective-permute-start.10 = (bf16[1,16,3456]{2,1,0:T(8,128)(2,1)S(1)}, bf16[1,16,3456]{2,1,0:T(8,128)(2,1)S(1)}, u32[]{:S(2)}, u32[]{:S(2)}) collective-permute-start(bf16[1,16,3456]{2,1,0:T(8,128)(2,1)S(1)} %get-tuple-element.32), channel_id=1, source_target_pairs={{0,2},{1,3},{2,0},{3,1},{4,6},{5,7},{6,4},{7,5},{8,10},{9,11},{10,... | collective-permute-start | bytes 331784 | tf_op jit(solution)/shard_map/ppermute | solution.py:382
  30.0 12.5 %collective-permute-start.8 = (bf16[2,16,3456]{2,1,0:T(8,128)(2,1)S(1)}, bf16[2,16,3456]{2,1,0:T(8,128)(2,1)S(1)}, u32[]{:S(2)}, u32[]{:S(2)}) collective-permute-start(bf16[2,16,3456]{2,1,0:T(8,128)(2,1)S(1)} %get-tuple-element.30), channel_id=1, source_target_pairs={{0,4},{1,5},{2,6},{3,7},{4,8},{5,9},{6,10},{7,11},{8,12},{9,13},{1... | collective-permute-start | bytes 663560 | tf_op jit(solution)/shard_map/ppermute | solution.py:382
  30.0 18.3 %copy-start = (bf16[1,18,6144]{2,1,0:T(8,128)(2,1)S(1)}, bf16[1,18,6144]{2,1,0:T(8,128)(2,1)}, u32[]{:S(2)}) copy-start(bf16[1,18,6144]{2,1,0:T(8,128)(2,1)} %param.9) | copy-start | bytes 663556
  30.0 18.3 %copy-start.1 = (f32[1,6144]{1,0:T(1,128)S(1)}, f32[1,6144]{1,0:T(1,128)}, u32[]{:S(2)}) copy-start(f32[1,6144]{1,0:T(1,128)} %gate.1) | copy-start | bytes 73732
  30.0 12.5 %collective-permute-start.9 = (bf16[2,16,3456]{2,1,0:T(8,128)(2,1)S(1)}, bf16[2,16,3456]{2,1,0:T(8,128)(2,1)S(1)}, u32[]{:S(2)}, u32[]{:S(2)}) collective-permute-start(bf16[2,16,3456]{2,1,0:T(8,128)(2,1)S(1)} %get-tuple-element.31), channel_id=1, source_target_pairs={{0,12},{1,13},{2,14},{3,15},{4,0},{5,1},{6,2},{7,3},{8,4},{9,5},{1... | collective-permute-start | bytes 663560 | tf_op jit(solution)/shard_map/ppermute | solution.py:382
  34.3 12.6 %collective-permute-start.2 = (bf16[2,16,3456]{2,1,0:T(8,128)(2,1)S(1)}, bf16[2,16,3456]{2,1,0:T(8,128)(2,1)S(1)}, u32[]{:S(2)}, u32[]{:S(2)}) collective-permute-start(bf16[2,16,3456]{2,1,0:T(8,128)(2,1)S(1)} %get-tuple-element.24), channel_id=1, source_target_pairs={{0,4},{1,5},{2,6},{3,7},{4,8},{5,9},{6,10},{7,11},{8,12},{9,13},{1... | collective-permute-start | bytes 663560 | tf_op jit(solution)/shard_map/ppermute | solution.py:382
  34.4 12.5 %collective-permute-start.3 = (bf16[2,16,3456]{2,1,0:T(8,128)(2,1)S(1)}, bf16[2,16,3456]{2,1,0:T(8,128)(2,1)S(1)}, u32[]{:S(2)}, u32[]{:S(2)}) collective-permute-start(bf16[2,16,3456]{2,1,0:T(8,128)(2,1)S(1)} %get-tuple-element.25), channel_id=1, source_target_pairs={{0,12},{1,13},{2,14},{3,15},{4,0},{5,1},{6,2},{7,3},{8,4},{9,5},{1... | collective-permute-start | bytes 663560 | tf_op jit(solution)/shard_map/ppermute | solution.py:382
  37.7 4.7 %collective-permute-start.4 = (bf16[1,16,3456]{2,1,0:T(8,128)(2,1)S(1)}, bf16[1,16,3456]{2,1,0:T(8,128)(2,1)S(1)}, u32[]{:S(2)}, u32[]{:S(2)}) collective-permute-start(bf16[1,16,3456]{2,1,0:T(8,128)(2,1)S(1)} %get-tuple-element.26), channel_id=1, source_target_pairs={{0,2},{1,3},{2,0},{3,1},{4,6},{5,7},{6,4},{7,5},{8,10},{9,11},{10,... | collective-permute-start | bytes 331784 | tf_op jit(solution)/shard_map/ppermute | solution.py:382
  42.4 6.3 %collective-permute-start.11 = (bf16[1,16,3456]{2,1,0:T(8,128)(2,1)S(1)}, bf16[1,16,3456]{2,1,0:T(8,128)(2,1)S(1)}, u32[]{:S(2)}, u32[]{:S(2)}) collective-permute-start(bf16[1,16,3456]{2,1,0:T(8,128)(2,1)S(1)} %bitcast.17), channel_id=1, source_target_pairs={{0,8},{1,9},{2,10},{3,11},{4,12},{5,13},{6,14},{7,15},{8,0},{9,1},... | collective-permute-start | bytes 331784 | tf_op jit(solution)/shard_map/ppermute | solution.py:382
  42.5 6.1 %collective-permute-start.12 = (bf16[1,16,3456]{2,1,0:T(8,128)(2,1)S(1)}, bf16[1,16,3456]{2,1,0:T(8,128)(2,1)S(1)}, u32[]{:S(2)}, u32[]{:S(2)}) collective-permute-start(bf16[1,16,3456]{2,1,0:T(8,128)(2,1)S(1)} %bitcast.15), channel_id=1, source_target_pairs={{0,2},{1,3},{2,0},{3,1},{4,6},{5,7},{6,4},{7,5},{8,10},{9,11},{10,... | collective-permute-start | bytes 331784 | tf_op jit(solution)/shard_map/ppermute | solution.py:382
  43.4 8.8 %collective-permute-start.5 = (bf16[1,16,3456]{2,1,0:T(8,128)(2,1)S(1)}, bf16[1,16,3456]{2,1,0:T(8,128)(2,1)S(1)}, u32[]{:S(2)}, u32[]{:S(2)}) collective-permute-start(bf16[1,16,3456]{2,1,0:T(8,128)(2,1)S(1)} %bitcast.16), channel_id=1, source_target_pairs={{0,8},{1,9},{2,10},{3,11},{4,12},{5,13},{6,14},{7,15},{8,0},{9,1},... | collective-permute-start | bytes 331784 | tf_op jit(solution)/shard_map/ppermute | solution.py:382
  47.0 6.8 %collective-permute-start.6 = (bf16[1,16,3456]{2,1,0:T(8,128)(2,1)S(1)}, bf16[1,16,3456]{2,1,0:T(8,128)(2,1)S(1)}, u32[]{:S(2)}, u32[]{:S(2)}) collective-permute-start(bf16[1,16,3456]{2,1,0:T(8,128)(2,1)S(1)} %bitcast.14), channel_id=1, source_target_pairs={{0,2},{1,3},{2,0},{3,1},{4,6},{5,7},{6,4},{7,5},{8,10},{9,11},{10,... | collective-permute-start | bytes 331784 | tf_op jit(solution)/shard_map/ppermute | solution.py:382
  48.8 11.7 %collective-permute-start.13 = (bf16[16,3456]{1,0:T(8,128)(2,1)S(1)}, bf16[16,3456]{1,0:T(8,128)(2,1)S(1)}, u32[]{:S(2)}, u32[]{:S(2)}) collective-permute-start(bf16[16,3456]{1,0:T(8,128)(2,1)S(1)} %update_1.1), channel_id=1, source_target_pairs={{0,16},{16,32},{32,48},{48,64},{64,80},{80,96},{96,112},{112,128},... | collective-permute-start | bytes 331784 | tf_op jit(solution)/shard_map/ppermute | solution.py:396
  53.9 12.7 %collective-permute-start.7 = (bf16[16,3456]{1,0:T(8,128)(2,1)S(1)}, bf16[16,3456]{1,0:T(8,128)(2,1)S(1)}, u32[]{:S(2)}, u32[]{:S(2)}) collective-permute-start(bf16[16,3456]{1,0:T(8,128)(2,1)S(1)} %update_0.1), channel_id=1, source_target_pairs={{0,16},{16,32},{32,48},{48,64},{64,80},{80,96},{96,112},{112,128},... | collective-permute-start | bytes 331784 | tf_op jit(solution)/shard_map/ppermute | solution.py:396

commit v5 on v4

--- a/solution.py
+++ b/solution.py
@@ -251,7 +251,7 @@
     return size * tok // MAIN
 
 
-def project_kernel(keep, other, weights, stay, across, ahead, behind, rest_s, *, start, size):
+def project_kernel(keep, other, weights, after, stay, across, ahead, behind, rest_s, *, start, size):
     blocks = [ref.at[n] for ref in (stay, across, ahead, behind) for n in range(ref.shape[0])]
     peers = len(blocks)
     cut = stay.shape[2] - size
@@ -272,19 +272,19 @@
         blocks[d][:, size:] = rest_s[d].astype(jnp.bfloat16)
 
 
-def project(keep, other, weights, peers, start, size):
+def project(keep, other, weights, after, peers, start, size):
     rows, _ = keep.shape
     width = packed_width(size, rows // peers)
     vmem = pl.BlockSpec(memory_space=pltpu.VMEM)
     return pl.pallas_call(
         functools.partial(project_kernel, start=start, size=size),
-        in_specs=[vmem] * 3,
+        in_specs=[vmem] * 3 + [pl.BlockSpec(memory_space=pl.ANY)],
         out_specs=[vmem] * 4,
         out_shape=[pltpu.VMEM((n, MAIN, width), jnp.bfloat16) for n in (3, 1, 2, 2)],
         scratch_shapes=[pltpu.VMEM((peers, MAIN, width - size), jnp.float32)],
         compiler_params=pltpu.CompilerParams(vmem_limit_bytes=VMEM_LIMIT),
         name=f"project_{start}",
-    )(in_vmem(keep), in_vmem(other), in_vmem(weights))
+    )(in_vmem(keep), in_vmem(other), in_vmem(weights), after)
 
 
 def add_kernel(*refs, picks):
@@ -295,16 +295,16 @@
     refs[-1][...] = total.astype(jnp.bfloat16)
 
 
-def add(arrays, picks, name):
+def add(arrays, after, picks, name):
     vmem = pl.BlockSpec(memory_space=pltpu.VMEM)
     return pl.pallas_call(
         functools.partial(add_kernel, picks=picks),
-        in_specs=[vmem] * len(arrays),
+        in_specs=[vmem] * len(arrays) + [pl.BlockSpec(memory_space=pl.ANY)],
         out_specs=vmem,
         out_shape=pltpu.VMEM(arrays[0].shape[1:], jnp.bfloat16),
         compiler_params=pltpu.CompilerParams(vmem_limit_bytes=VMEM_LIMIT),
         name=name,
-    )(*map(in_vmem, arrays))
+    )(*map(in_vmem, arrays), after)
 
 
 def update_kernel(*refs):
@@ -382,18 +382,20 @@
         return lax.ppermute(x, "head", route)
 
     handed = []
+    turns = [keep] * 3
     for i, (start, size) in enumerate(chunks):
-        stay, across, ahead, behind = project(keep, other, weights, peers, start, size)
+        stay, across, ahead, behind = project(keep, other, weights, turns[0], peers, start, size)
         from_z = along(across, 0, 1)
         from_last = along(ahead, 1, 0)
         from_next = along(behind, -1, 0)
-        opposite = add((stay, from_z), (2, 0), f"opposite_{i}")
+        opposite = add((stay, from_z), turns[1], (2, 0), f"opposite_{i}")
         from_opposite = along(opposite[None], 2, 0)
-        pair = add((stay, from_last, from_next), (1, 1, 1), f"pair_{i}")
+        pair = add((stay, from_last, from_next), turns[2], (1, 1, 1), f"pair_{i}")
         from_pair = along(pair[None], 0, 1)
         terms = (stay, from_last, from_next, from_opposite, from_pair)
         updated = update(terms, packed[2 * i], packed[2 * i + 1], f"update_{i}")
         handed.append(lax.ppermute(updated, "section", forward))
+        turns = [across, pair, updated]
     return unpack(handed, tok, columns, chunks)[None]
 
 

time: 67.5 us -> 65.8 us (0.975)
  waiting for transfers between devices: 18.7 us -> 17 us
    ppermute x2, waiting for transfers between devices: 9.29 us -> 6.63 us  [shards(): handed.append(lax.ppermute(updated, 'section', forward))]
    ppermute x10, starting transfers between devices: 14.4 us -> 12.3 us  [along(): return lax.ppermute(x, 'head', route)]
    ppermute x2, starting transfers between devices: 6.73 us -> 8.66 us  [shards(): handed.append(lax.ppermute(updated, 'section', forward))]
    ppermute x10, waiting for transfers between devices: 5.87 us -> 6.85 us  [along(): return lax.ppermute(x, 'head', route)]
  transfers between devices with their start and end apart: 15 -> 15, of which waited for: 7 -> 8; matrix products, arithmetic and copies ran while one was open for 10% -> 10% of each run, Pallas kernels for 8% -> 8%
where the time goes in v5:
time: 65.8 us; the launch traced here: 65.5 us
  starting transfers between devices  27.3 us (41%)
  waiting for transfers between devices  17 us (26%)
  Pallas kernels  13.6 us (21%)
  local copies, waits for them, and re-layouts  6.78 us (10%)
  between operations  0.77 us (1%)
    ppermute x10, starting transfers between devices, along(): return lax.ppermute(x, 'head', route)  12.3 us
    ppermute x2, starting transfers between devices, shards(): handed.append(lax.ppermute(updated, 'section', forward))  8.66 us
    ppermute x10, waiting for transfers between devices, along(): return lax.ppermute(x, 'head', route)  6.85 us
    unnamed x5, local copies, waits for them, and re-layouts  6.78 us
    ppermute x2, waiting for transfers between devices, shards(): handed.append(lax.ppermute(updated, 'section', forward))  6.63 us
    pallas_call x1, Pallas kernels, attend(): pl.pallas_call(functools.partial(attend_kernel, heads=heads, chunk=keys /...  6.21 us
    all_to_all x1, starting transfers between devices, shards(): lax.all_to_all(blocked, 'head', split_axis=0, concat_axis=0, tiled=True)  6.07 us
    all_to_all x1, waiting for transfers between devices, shards(): lax.all_to_all(blocked, 'head', split_axis=0, concat_axis=0, tiled=True)  2.34 us
  transfers between devices with their start and end apart: 15, of which 8 were waited for; matrix products, arithmetic and copies ran while one was open for 10% of the time, Pallas kernels for 8%

profile of v5, /device:TPU:32, one launch (start us, length us, event | category | flops | bytes accessed | tf_op | source)
XLA Modules:
  0.0 65.5 jit_solution(371529219609739013)
XLA Ops:
  0.0 0.0 collective-permute-start
  0.0 2.2 %pack.1 = bf16[16,54,384]{2,1,0:T(8,128)(2,1)} custom-call(bf16[1,18,3,6144]{3,2,1,0:T(4,128)(2,1)} %qkv.1), custom_call_target="tpu_custom_call" | custom-call | tf_op jit(solution)/shard_map/pack/pallas_call | solution.py:66
  2.2 6.1 %all-to-all-start = ((bf16[16,54,384]{2,1,0:T(8,128)(2,1)}), bf16[16,54,384]{2,1,0:T(8,128)(2,1)S(1)}, u32[]{:S(2)}, u32[]{:S(2)}) async-start(bf16[16,54,384]{2,1,0:T(8,128)(2,1)} %pack.1), calls=%async_computation | async-start | bytes 1376256 | tf_op jit(solution)/shard_map/all_to_all | solution.py:372
  8.3 6.8 %copy.10 = bf16[1,4608,2,384]{3,1,2,0:T(8,128)(2,1)} copy(bf16[1,4608,2,384]{3,2,1,0:T(2,128)(2,1)} %param.7) | data formatting | bytes 14155776 | tf_op args[1]
  15.1 1.6 %prefetch.1.first_in = bf16[2,4608,128]{2,1,0:T(8,128)(2,1)S(1)} custom-call(bf16[2,4608,384]{2,1,0:T(8,128)(2,1)} %bitcast.18), custom_call_target="tpu_custom_call" | custom-call | tf_op jit(solution)/shard_map/prefetch/pallas_call | solution.py:126
  17.4 0.1 pad_add_fusion.scalars
  17.4 2.3 %all-to-all-done.arrived = bf16[16,54,384]{2,1,0:T(8,128)(2,1)S(1)} async-done(((bf16[16,54,384]{2,1,0:T(8,128)(2,1)}), bf16[16,54,384]{2,1,0:T(8,128)(2,1)S(1)}, u32[]{:S(2)}, u32[]{:S(2)}) %all-to-all-start) | async-done | bytes 663584 | tf_op jit(solution)/shard_map/all_to_all | solution.py:372
  19.8 0.0 collective-permute-done.w_other
  19.8 6.2 %attend.1 = (bf16[144,384]{1,0:T(8,128)(2,1)S(1)}, bf16[144,384]{1,0:T(8,128)(2,1)S(1)}, bf16[2,384,6144]{2,1,0:T(8,128)(2,1)S(1)}, bf16[2,4608,128]{2,1,0:T(8,128)(2,1)S(1)}) custom-call(s32[2]{0:T(128)S(1)} %pad_add_fusion.scalars, bf16[16,54,384]{2,1,0:T(8,128)(2,1)S(1)} %all-to-all-done.arrived, ...), custom_call_target="tpu_custom_call", output_to_operand_aliasing={{3}: (2, {})} | custom-call | tf_op jit(solution)/shard_map/attend/pallas_call | solution.py:228
  26.0 0.2 collective-permute-start.1
  26.2 1.2 %collective-permute-done.1.other = bf16[144,384]{1,0:T(8,128)(2,1)S(1)} collective-permute-done((bf16[144,384]{1,0:T(8,128)(2,1)S(1)}, bf16[144,384]{1,0:T(8,128)(2,1)S(1)}, u32[]{:S(2)}, u32[]{:S(2)}) %collective-permute-start.1) | collective-permute-done | bytes 110624 | tf_op jit(solution)/shard_map/ppermute | solution.py:376
  27.4 1.2 %project_0.1 = (bf16[3,16,3456]{2,1,0:T(8,128)(2,1)S(1)}, bf16[1,16,3456]{2,1,0:T(8,128)(2,1)S(1)}, bf16[2,16,3456]{2,1,0:T(8,128)(2,1)S(1)}, bf16[2,16,3456]{2,1,0:T(8,128)(2,1)S(1)}) custom-call(bf16[144,384]{1,0:T(8,128)(2,1)S(1)} %get-tuple-element.20.keep.after.refs_2_.refs_3_, bf16[144,384]{1,0:T(8,128)(2,1)S(1)} %collective-permute-done.1.other, ...), custom_call_target="tpu_custom_call" | custom-call | tf_op jit(solution)/shard_map/project_0/pallas_call | solution.py:279
  28.6 0.1 collective-permute-start.2
  28.7 3.2 %collective-permute-start.3 = (bf16[2,16,3456]{2,1,0:T(8,128)(2,1)S(1)}, bf16[2,16,3456]{2,1,0:T(8,128)(2,1)S(1)}, u32[]{:S(2)}, u32[]{:S(2)}) collective-permute-start(bf16[2,16,3456]{2,1,0:T(8,128)(2,1)S(1)} %get-tuple-element.25), channel_id=1, source_target_pairs={{0,12},{1,13},{2,14},{3,15},{4,0},{5,1},{6,2},{7,3},{8,4},{9,5},{1... | collective-permute-start | bytes 663560 | tf_op jit(solution)/shard_map/ppermute | solution.py:382
  31.9 0.0 copy-start
  31.9 0.0 copy-start.1
  31.9 1.3 %collective-permute-start.4 = (bf16[1,16,3456]{2,1,0:T(8,128)(2,1)S(1)}, bf16[1,16,3456]{2,1,0:T(8,128)(2,1)S(1)}, u32[]{:S(2)}, u32[]{:S(2)}) collective-permute-start(bf16[1,16,3456]{2,1,0:T(8,128)(2,1)S(1)} %get-tuple-element.26.after), channel_id=1, source_target_pairs={{0,2},{1,3},{2,0},{3,1},{4,6},{5,7},{6,4},{7,5},{8,10},{9,11},{10,... | collective-permute-start | bytes 331784 | tf_op jit(solution)/shard_map/ppermute | solution.py:382
  33.2 1.2 %project_3072.1 = (bf16[3,16,3456]{2,1,0:T(8,128)(2,1)S(1)}, bf16[1,16,3456]{2,1,0:T(8,128)(2,1)S(1)}, bf16[2,16,3456]{2,1,0:T(8,128)(2,1)S(1)}, bf16[2,16,3456]{2,1,0:T(8,128)(2,1)S(1)}) custom-call(bf16[144,384]{1,0:T(8,128)(2,1)S(1)} %get-tuple-element.20.keep.after.refs_2_.refs_3_, bf16[144,384]{1,0:T(8,128)(2,1)S(1)} %collective-permute-done.1.other, ...), custom_call_target="tpu_custom_call" | custom-call | tf_op jit(solution)/shard_map/project_3072/pallas_call | solution.py:279
  34.3 0.1 collective-permute-start.8
  34.4 3.2 %collective-permute-start.9 = (bf16[2,16,3456]{2,1,0:T(8,128)(2,1)S(1)}, bf16[2,16,3456]{2,1,0:T(8,128)(2,1)S(1)}, u32[]{:S(2)}, u32[]{:S(2)}) collective-permute-start(bf16[2,16,3456]{2,1,0:T(8,128)(2,1)S(1)} %get-tuple-element.31), channel_id=1, source_target_pairs={{0,12},{1,13},{2,14},{3,15},{4,0},{5,1},{6,2},{7,3},{8,4},{9,5},{1... | collective-permute-start | bytes 663560 | tf_op jit(solution)/shard_map/ppermute | solution.py:382
  37.6 0.0 collective-permute-done.4.refs_1_
  37.6 0.8 %collective-permute-start.10 = (bf16[1,16,3456]{2,1,0:T(8,128)(2,1)S(1)}, bf16[1,16,3456]{2,1,0:T(8,128)(2,1)S(1)}, u32[]{:S(2)}, u32[]{:S(2)}) collective-permute-start(bf16[1,16,3456]{2,1,0:T(8,128)(2,1)S(1)} %get-tuple-element.32), channel_id=1, source_target_pairs={{0,2},{1,3},{2,0},{3,1},{4,6},{5,7},{6,4},{7,5},{8,10},{9,11},{10,... | collective-permute-start | bytes 331784 | tf_op jit(solution)/shard_map/ppermute | solution.py:382
  38.4 0.0 collective-permute-done.2.refs_1_
  38.4 0.1 collective-permute-start.5
  38.5 0.0 collective-permute-done.3.refs_2_
  38.6 0.1 pair_0.1.refs_2_
  38.6 1.3 %collective-permute-start.6 = (bf16[1,16,3456]{2,1,0:T(8,128)(2,1)S(1)}, bf16[1,16,3456]{2,1,0:T(8,128)(2,1)S(1)}, u32[]{:S(2)}, u32[]{:S(2)}) collective-permute-start(bf16[1,16,3456]{2,1,0:T(8,128)(2,1)S(1)} %bitcast.13), channel_id=1, source_target_pairs={{0,2},{1,3},{2,0},{3,1},{4,6},{5,7},{6,4},{7,5},{8,10},{9,11},{10,... | collective-permute-start | bytes 331784 | tf_op jit(solution)/shard_map/ppermute | solution.py:382
  40.0 0.0 copy-done
  40.0 0.0 copy-done.1
  40.0 0.1 stream.1
  40.0 2.5 %collective-permute-done.10.refs_1_ = bf16[1,16,3456]{2,1,0:T(8,128)(2,1)S(1)} collective-permute-done((bf16[1,16,3456]{2,1,0:T(8,128)(2,1)S(1)}, bf16[1,16,3456]{2,1,0:T(8,128)(2,1)S(1)}, u32[]{:S(2)}, u32[]{:S(2)}) %collective-permute-start.10) | collective-permute-done | bytes 110624 | tf_op jit(solution)/shard_map/ppermute | solution.py:382
  42.6 1.1 %collective-permute-start.11 = (bf16[1,16,3456]{2,1,0:T(8,128)(2,1)S(1)}, bf16[1,16,3456]{2,1,0:T(8,128)(2,1)S(1)}, u32[]{:S(2)}, u32[]{:S(2)}) collective-permute-start(bf16[1,16,3456]{2,1,0:T(8,128)(2,1)S(1)} %bitcast.15), channel_id=1, source_target_pairs={{0,8},{1,9},{2,10},{3,11},{4,12},{5,13},{6,14},{7,15},{8,0},{9,1},... | collective-permute-start | bytes 331784 | tf_op jit(solution)/shard_map/ppermute | solution.py:382
  43.7 1.4 %collective-permute-done.5.refs_3_ = bf16[1,16,3456]{2,1,0:T(8,128)(2,1)S(1)} collective-permute-done((bf16[1,16,3456]{2,1,0:T(8,128)(2,1)S(1)}, bf16[1,16,3456]{2,1,0:T(8,128)(2,1)S(1)}, u32[]{:S(2)}, u32[]{:S(2)}) %collective-permute-start.5) | collective-permute-done | bytes 110624 | tf_op jit(solution)/shard_map/ppermute | solution.py:382
  45.1 0.0 collective-permute-done.6.refs_4_
  45.1 0.1 update_0.1.refs_3_
  45.2 0.0 collective-permute-done.8.refs_1_
  45.2 1.1 %collective-permute-done.9.refs_2_ = bf16[2,16,3456]{2,1,0:T(8,128)(2,1)S(1)} collective-permute-done((bf16[2,16,3456]{2,1,0:T(8,128)(2,1)S(1)}, bf16[2,16,3456]{2,1,0:T(8,128)(2,1)S(1)}, u32[]{:S(2)}, u32[]{:S(2)}) %collective-permute-start.9) | collective-permute-done | bytes 221216 | tf_op jit(solution)/shard_map/ppermute | solution.py:382
  46.3 1.2 %collective-permute-start.12 = (bf16[1,16,3456]{2,1,0:T(8,128)(2,1)S(1)}, bf16[1,16,3456]{2,1,0:T(8,128)(2,1)S(1)}, u32[]{:S(2)}, u32[]{:S(2)}) collective-permute-start(bf16[1,16,3456]{2,1,0:T(8,128)(2,1)S(1)} %bitcast.17), channel_id=1, source_target_pairs={{0,2},{1,3},{2,0},{3,1},{4,6},{5,7},{6,4},{7,5},{8,10},{9,11},{10,... | collective-permute-start | bytes 331784 | tf_op jit(solution)/shard_map/ppermute | solution.py:382
  47.5 3.3 %collective-permute-start.7 = (bf16[16,3456]{1,0:T(8,128)(2,1)S(1)}, bf16[16,3456]{1,0:T(8,128)(2,1)S(1)}, u32[]{:S(2)}, u32[]{:S(2)}) collective-permute-start(bf16[16,3456]{1,0:T(8,128)(2,1)S(1)} %update_0.1.refs_3_), channel_id=1, source_target_pairs={{0,16},{16,32},{32,48},{48,64},{64,80},{80,96},{96,112},{112,128},... | collective-permute-start | bytes 331784 | tf_op jit(solution)/shard_map/ppermute | solution.py:397
  50.8 0.0 collective-permute-done.11.refs_3_
  50.8 1.8 %collective-permute-done.12.refs_4_ = bf16[1,16,3456]{2,1,0:T(8,128)(2,1)S(1)} collective-permute-done((bf16[1,16,3456]{2,1,0:T(8,128)(2,1)S(1)}, bf16[1,16,3456]{2,1,0:T(8,128)(2,1)S(1)}, u32[]{:S(2)}, u32[]{:S(2)}) %collective-permute-start.12) | collective-permute-done | bytes 110624 | tf_op jit(solution)/shard_map/ppermute | solution.py:382
  52.6 0.1 update_1.1
  52.7 5.4 %collective-permute-start.13 = (bf16[16,3456]{1,0:T(8,128)(2,1)S(1)}, bf16[16,3456]{1,0:T(8,128)(2,1)S(1)}, u32[]{:S(2)}, u32[]{:S(2)}) collective-permute-start(bf16[16,3456]{1,0:T(8,128)(2,1)S(1)} %update_1.1), channel_id=1, source_target_pairs={{0,16},{16,32},{32,48},{48,64},{64,80},{80,96},{96,112},{112,128},... | collective-permute-start | bytes 331784 | tf_op jit(solution)/shard_map/ppermute | solution.py:397
  58.1 0.1 collective-permute-done.7.refs_0_
  58.2 6.5 %collective-permute-done.13.refs_1_ = bf16[16,3456]{1,0:T(8,128)(2,1)S(1)} collective-permute-done((bf16[16,3456]{1,0:T(8,128)(2,1)S(1)}, bf16[16,3456]{1,0:T(8,128)(2,1)S(1)}, u32[]{:S(2)}, u32[]{:S(2)}) %collective-permute-start.13) | collective-permute-done | bytes 110624 | tf_op jit(solution)/shard_map/ppermute | solution.py:397
  64.7 0.7 %unpack.1 = bf16[18,6144]{1,0:T(8,128)(2,1)} custom-call(bf16[16,3456]{1,0:T(8,128)(2,1)S(1)} %collective-permute-done.7.refs_0_, bf16[16,3456]{1,0:T(8,128)(2,1)S(1)} %collective-permute-done.13.refs_1_), custom_call_target="tpu_custom_call" | custom-call | tf_op jit(solution)/shard_map/unpack/pallas_call | solution.py:346
  (3 shorter events, 0.1 us)
Async XLA Ops:
  0.0 19.8 %collective-permute-start = (bf16[384,6144]{1,0:T(8,128)(2,1)}, bf16[384,6144]{1,0:T(8,128)(2,1)}, u32[]{:S(2)}, u32[]{:S(2)}) collective-permute-start(bf16[384,6144]{1,0:T(8,128)(2,1)} %bitcast.20), channel_id=1, source_target_pairs={{0,1},{1,0},{2,3},{3,2},{4,5},{5,4},{6,7},{7,6},{8,9},{9,8},{10,11... | collective-permute-start | bytes 14155784 | tf_op jit(solution)/shard_map/ppermute | solution.py:370
  2.2 17.6 %all-to-all-start = ((bf16[16,54,384]{2,1,0:T(8,128)(2,1)}), bf16[16,54,384]{2,1,0:T(8,128)(2,1)S(1)}, u32[]{:S(2)}, u32[]{:S(2)}) async-start(bf16[16,54,384]{2,1,0:T(8,128)(2,1)} %pack.1), calls=%async_computation | async-start | bytes 1376256 | tf_op jit(solution)/shard_map/all_to_all | solution.py:372
  26.0 1.4 %collective-permute-start.1 = (bf16[144,384]{1,0:T(8,128)(2,1)S(1)}, bf16[144,384]{1,0:T(8,128)(2,1)S(1)}, u32[]{:S(2)}, u32[]{:S(2)}) collective-permute-start(bf16[144,384]{1,0:T(8,128)(2,1)S(1)} %get-tuple-element.21), channel_id=1, source_target_pairs={{0,1},{1,0},{2,3},{3,2},{4,5},{5,4},{6,7},{7,6},{8,9},{9,8},{10,11... | collective-permute-start | bytes 331784 | tf_op jit(solution)/shard_map/ppermute | solution.py:376
  28.6 9.9 %collective-permute-start.2 = (bf16[2,16,3456]{2,1,0:T(8,128)(2,1)S(1)}, bf16[2,16,3456]{2,1,0:T(8,128)(2,1)S(1)}, u32[]{:S(2)}, u32[]{:S(2)}) collective-permute-start(bf16[2,16,3456]{2,1,0:T(8,128)(2,1)S(1)} %get-tuple-element.24), channel_id=1, source_target_pairs={{0,4},{1,5},{2,6},{3,7},{4,8},{5,9},{6,10},{7,11},{8,12},{9,13},{1... | collective-permute-start | bytes 663560 | tf_op jit(solution)/shard_map/ppermute | solution.py:382
  28.7 9.9 %collective-permute-start.3 = (bf16[2,16,3456]{2,1,0:T(8,128)(2,1)S(1)}, bf16[2,16,3456]{2,1,0:T(8,128)(2,1)S(1)}, u32[]{:S(2)}, u32[]{:S(2)}) collective-permute-start(bf16[2,16,3456]{2,1,0:T(8,128)(2,1)S(1)} %get-tuple-element.25), channel_id=1, source_target_pairs={{0,12},{1,13},{2,14},{3,15},{4,0},{5,1},{6,2},{7,3},{8,4},{9,5},{1... | collective-permute-start | bytes 663560 | tf_op jit(solution)/shard_map/ppermute | solution.py:382
  31.9 8.1 %copy-start = (bf16[1,18,6144]{2,1,0:T(8,128)(2,1)S(1)}, bf16[1,18,6144]{2,1,0:T(8,128)(2,1)}, u32[]{:S(2)}) copy-start(bf16[1,18,6144]{2,1,0:T(8,128)(2,1)} %param.9) | copy-start | bytes 663556
  31.9 8.1 %copy-start.1 = (f32[1,6144]{1,0:T(1,128)S(1)}, f32[1,6144]{1,0:T(1,128)}, u32[]{:S(2)}) copy-start(f32[1,6144]{1,0:T(1,128)} %gate.1) | copy-start | bytes 73732
  31.9 5.7 %collective-permute-start.4 = (bf16[1,16,3456]{2,1,0:T(8,128)(2,1)S(1)}, bf16[1,16,3456]{2,1,0:T(8,128)(2,1)S(1)}, u32[]{:S(2)}, u32[]{:S(2)}) collective-permute-start(bf16[1,16,3456]{2,1,0:T(8,128)(2,1)S(1)} %get-tuple-element.26.after), channel_id=1, source_target_pairs={{0,2},{1,3},{2,0},{3,1},{4,6},{5,7},{6,4},{7,5},{8,10},{9,11},{10,... | collective-permute-start | bytes 331784 | tf_op jit(solution)/shard_map/ppermute | solution.py:382
  34.3 10.9 %collective-permute-start.8 = (bf16[2,16,3456]{2,1,0:T(8,128)(2,1)S(1)}, bf16[2,16,3456]{2,1,0:T(8,128)(2,1)S(1)}, u32[]{:S(2)}, u32[]{:S(2)}) collective-permute-start(bf16[2,16,3456]{2,1,0:T(8,128)(2,1)S(1)} %get-tuple-element.30), channel_id=1, source_target_pairs={{0,4},{1,5},{2,6},{3,7},{4,8},{5,9},{6,10},{7,11},{8,12},{9,13},{1... | collective-permute-start | bytes 663560 | tf_op jit(solution)/shard_map/ppermute | solution.py:382
  34.4 11.9 %collective-permute-start.9 = (bf16[2,16,3456]{2,1,0:T(8,128)(2,1)S(1)}, bf16[2,16,3456]{2,1,0:T(8,128)(2,1)S(1)}, u32[]{:S(2)}, u32[]{:S(2)}) collective-permute-start(bf16[2,16,3456]{2,1,0:T(8,128)(2,1)S(1)} %get-tuple-element.31), channel_id=1, source_target_pairs={{0,12},{1,13},{2,14},{3,15},{4,0},{5,1},{6,2},{7,3},{8,4},{9,5},{1... | collective-permute-start | bytes 663560 | tf_op jit(solution)/shard_map/ppermute | solution.py:382
  37.6 4.9 %collective-permute-start.10 = (bf16[1,16,3456]{2,1,0:T(8,128)(2,1)S(1)}, bf16[1,16,3456]{2,1,0:T(8,128)(2,1)S(1)}, u32[]{:S(2)}, u32[]{:S(2)}) collective-permute-start(bf16[1,16,3456]{2,1,0:T(8,128)(2,1)S(1)} %get-tuple-element.32), channel_id=1, source_target_pairs={{0,2},{1,3},{2,0},{3,1},{4,6},{5,7},{6,4},{7,5},{8,10},{9,11},{10,... | collective-permute-start | bytes 331784 | tf_op jit(solution)/shard_map/ppermute | solution.py:382
  38.4 6.6 %collective-permute-start.5 = (bf16[1,16,3456]{2,1,0:T(8,128)(2,1)S(1)}, bf16[1,16,3456]{2,1,0:T(8,128)(2,1)S(1)}, u32[]{:S(2)}, u32[]{:S(2)}) collective-permute-start(bf16[1,16,3456]{2,1,0:T(8,128)(2,1)S(1)} %bitcast.16), channel_id=1, source_target_pairs={{0,8},{1,9},{2,10},{3,11},{4,12},{5,13},{6,14},{7,15},{8,0},{9,1},... | collective-permute-start | bytes 331784 | tf_op jit(solution)/shard_map/ppermute | solution.py:382
  38.6 6.5 %collective-permute-start.6 = (bf16[1,16,3456]{2,1,0:T(8,128)(2,1)S(1)}, bf16[1,16,3456]{2,1,0:T(8,128)(2,1)S(1)}, u32[]{:S(2)}, u32[]{:S(2)}) collective-permute-start(bf16[1,16,3456]{2,1,0:T(8,128)(2,1)S(1)} %bitcast.13), channel_id=1, source_target_pairs={{0,2},{1,3},{2,0},{3,1},{4,6},{5,7},{6,4},{7,5},{8,10},{9,11},{10,... | collective-permute-start | bytes 331784 | tf_op jit(solution)/shard_map/ppermute | solution.py:382
  42.6 8.2 %collective-permute-start.11 = (bf16[1,16,3456]{2,1,0:T(8,128)(2,1)S(1)}, bf16[1,16,3456]{2,1,0:T(8,128)(2,1)S(1)}, u32[]{:S(2)}, u32[]{:S(2)}) collective-permute-start(bf16[1,16,3456]{2,1,0:T(8,128)(2,1)S(1)} %bitcast.15), channel_id=1, source_target_pairs={{0,8},{1,9},{2,10},{3,11},{4,12},{5,13},{6,14},{7,15},{8,0},{9,1},... | collective-permute-start | bytes 331784 | tf_op jit(solution)/shard_map/ppermute | solution.py:382
  46.3 6.3 %collective-permute-start.12 = (bf16[1,16,3456]{2,1,0:T(8,128)(2,1)S(1)}, bf16[1,16,3456]{2,1,0:T(8,128)(2,1)S(1)}, u32[]{:S(2)}, u32[]{:S(2)}) collective-permute-start(bf16[1,16,3456]{2,1,0:T(8,128)(2,1)S(1)} %bitcast.17), channel_id=1, source_target_pairs={{0,2},{1,3},{2,0},{3,1},{4,6},{5,7},{6,4},{7,5},{8,10},{9,11},{10,... | collective-permute-start | bytes 331784 | tf_op jit(solution)/shard_map/ppermute | solution.py:382
  47.5 10.8 %collective-permute-start.7 = (bf16[16,3456]{1,0:T(8,128)(2,1)S(1)}, bf16[16,3456]{1,0:T(8,128)(2,1)S(1)}, u32[]{:S(2)}, u32[]{:S(2)}) collective-permute-start(bf16[16,3456]{1,0:T(8,128)(2,1)S(1)} %update_0.1.refs_3_), channel_id=1, source_target_pairs={{0,16},{16,32},{32,48},{48,64},{64,80},{80,96},{96,112},{112,128},... | collective-permute-start | bytes 331784 | tf_op jit(solution)/shard_map/ppermute | solution.py:397
  52.7 12.0 %collective-permute-start.13 = (bf16[16,3456]{1,0:T(8,128)(2,1)S(1)}, bf16[16,3456]{1,0:T(8,128)(2,1)S(1)}, u32[]{:S(2)}, u32[]{:S(2)}) collective-permute-start(bf16[16,3456]{1,0:T(8,128)(2,1)S(1)} %update_1.1), channel_id=1, source_target_pairs={{0,16},{16,32},{32,48},{48,64},{64,80},{80,96},{96,112},{112,128},... | collective-permute-start | bytes 331784 | tf_op jit(solution)/shard_map/ppermute | solution.py:397

commit v6 on v4

--- a/solution.py
+++ b/solution.py
@@ -11,9 +11,9 @@
 HD = 128
 CORES = 2
 PAIR = 2
-PLACES = ((0, 0), (0, 1), (2, 0), (2, 1), (1, 0), (1, 1), (3, 0), (3, 1))
+PLACES = ((0, 0), (0, 1), (1, 1), (3, 1), (1, 0), (3, 0), (2, 0), (2, 1))
 MAIN = 16
-SPLIT = (1, 1)
+SPLIT = (1, 2)
 CHUNKS = 6
 ATTEND_VMEM = 36 * 2**20
 VMEM_LIMIT = 8 * 2**20
@@ -251,74 +251,85 @@
     return size * tok // MAIN
 
 
-def project_kernel(keep, other, weights, stay, across, ahead, behind, rest_s, *, start, size):
-    blocks = [ref.at[n] for ref in (stay, across, ahead, behind) for n in range(ref.shape[0])]
-    peers = len(blocks)
-    cut = stay.shape[2] - size
-    cuts = size // cut
-    rest = MAIN // cuts
+def project_kernel(keep, other, weights, *refs, chunks):
+    outs, rest_s = refs[:-1], refs[-1]
+    peers = rest_s.shape[0]
+    rest = keep.shape[0] // peers - MAIN
+    cuts = MAIN // rest
     both = jnp.concatenate([keep[...], other[...]], axis=1)
-    for b in range(cuts):
-        cols = slice(start + b * cut, start + (b + 1) * cut)
-        w = jnp.concatenate([weights[i, :, cols] for i in range(CORES)], axis=0)
-        y = jnp.dot(both, w, preferred_element_type=jnp.float32)
+    offset = 0
+    for i, (start, size) in enumerate(chunks):
+        cut = size // cuts
+        width = size + cut
+        span = pl.ds(offset, width)
+        blocks = [ref.at[n, :, span] for ref in outs for n in range(ref.shape[0])]
+        for b in range(cuts):
+            cols = slice(start + b * cut, start + (b + 1) * cut)
+            w = jnp.concatenate([weights[n, :, cols] for n in range(CORES)], axis=0)
+            y = jnp.dot(both, w, preferred_element_type=jnp.float32)
+            for d in range(peers):
+                rows = y[MAIN * d : MAIN * (d + 1)]
+                blocks[d][:, b * cut : (b + 1) * cut] = rows.astype(jnp.bfloat16)
+                for t in range(rest):
+                    row = MAIN * peers + rest * d + t
+                    rest_s[d, cuts * t + b : cuts * t + b + 1, :cut] = y[row : row + 1]
         for d in range(peers):
-            rows = y[MAIN * d : MAIN * (d + 1)]
-            blocks[d][:, b * cut : (b + 1) * cut] = rows.astype(jnp.bfloat16)
-            for t in range(rest):
-                row = MAIN * peers + rest * d + t
-                rest_s[d, cuts * t + b : cuts * t + b + 1, :] = y[row : row + 1]
-    for d in range(peers):
-        blocks[d][:, size:] = rest_s[d].astype(jnp.bfloat16)
-
-
-def project(keep, other, weights, peers, start, size):
+            blocks[d][:, size:] = rest_s[d, :, :cut].astype(jnp.bfloat16)
+        offset += width
+
+
+def project(keep, other, weights, peers, chunks):
     rows, _ = keep.shape
-    width = packed_width(size, rows // peers)
-    vmem = pl.BlockSpec(memory_space=pltpu.VMEM)
-    return pl.pallas_call(
-        functools.partial(project_kernel, start=start, size=size),
+    widths = [packed_width(size, rows // peers) for _, size in chunks]
+    vmem = pl.BlockSpec(memory_space=pltpu.VMEM)
+    shapes = [(1, MAIN, sum(widths))] * peers
+    deepest = max(width - size for width, (_, size) in zip(widths, chunks))
+    return pl.pallas_call(
+        functools.partial(project_kernel, chunks=chunks),
         in_specs=[vmem] * 3,
-        out_specs=[vmem] * 4,
-        out_shape=[pltpu.VMEM((n, MAIN, width), jnp.bfloat16) for n in (3, 1, 2, 2)],
-        scratch_shapes=[pltpu.VMEM((peers, MAIN, width - size), jnp.float32)],
-        compiler_params=pltpu.CompilerParams(vmem_limit_bytes=VMEM_LIMIT),
-        name=f"project_{start}",
+        out_specs=[vmem] * len(shapes),
+        out_shape=[pltpu.VMEM(shape, jnp.bfloat16) for shape in shapes],
+        scratch_shapes=[pltpu.VMEM((peers, MAIN, deepest), jnp.float32)],
+        compiler_params=pltpu.CompilerParams(vmem_limit_bytes=VMEM_LIMIT),
+        name="project",
     )(in_vmem(keep), in_vmem(other), in_vmem(weights))
 
 
+def total_of(refs, picks, width):
+    total = None
+    for ref, (n, offset) in zip(refs, picks):
+        term = ref[n, :, offset : offset + width].astype(jnp.float32)
+        total = term if total is None else total + term
+    return total
+
+
 def add_kernel(*refs, picks):
-    total = None
-    for ref, pick in zip(refs, picks):
-        term = ref[pick].astype(jnp.float32)
-        total = term if total is None else total + term
-    refs[-1][...] = total.astype(jnp.bfloat16)
-
-
-def add(arrays, picks, name):
+    out = refs[-1]
+    out[0] = total_of(refs, picks, out.shape[2]).astype(jnp.bfloat16)
+
+
+def add(arrays, after, picks, width, name):
     vmem = pl.BlockSpec(memory_space=pltpu.VMEM)
     return pl.pallas_call(
         functools.partial(add_kernel, picks=picks),
-        in_specs=[vmem] * len(arrays),
+        in_specs=[vmem] * len(arrays) + [pl.BlockSpec(memory_space=pl.ANY)],
         out_specs=vmem,
-        out_shape=pltpu.VMEM(arrays[0].shape[1:], jnp.bfloat16),
+        out_shape=pltpu.VMEM((1, MAIN, width), jnp.bfloat16),
         compiler_params=pltpu.CompilerParams(vmem_limit_bytes=VMEM_LIMIT),
         name=name,
-    )(*map(in_vmem, arrays))
-
-
-def update_kernel(*refs):
+    )(*map(in_vmem, arrays), after)
+
+
+def update_kernel(*refs, picks):
     residual, gate, out = refs[-3:]
-    total = refs[0][0].astype(jnp.float32)
-    for ref in refs[1:-3]:
-        total = total + ref[0].astype(jnp.float32)
+    total = total_of(refs, picks, out.shape[1])
     out[...] = (residual[...] + gate[...] * total).astype(jnp.bfloat16)
 
 
-def update(arrays, residual, gate, name):
-    vmem = pl.BlockSpec(memory_space=pltpu.VMEM)
-    return pl.pallas_call(
-        update_kernel,
+def update(arrays, picks, residual, gate, name):
+    vmem = pl.BlockSpec(memory_space=pltpu.VMEM)
+    return pl.pallas_call(
+        functools.partial(update_kernel, picks=picks),
         in_specs=[vmem] * (len(arrays) + 2),
         out_specs=vmem,
         out_shape=pltpu.VMEM(residual.shape, jnp.bfloat16),
@@ -381,19 +392,31 @@
         route = [(i, (i + dy * PAIR * CORES) % groups ^ dz * CORES) for i in range(groups)]
         return lax.ppermute(x, "head", route)
 
+    mine, pair, ahead_far, behind_far, ahead, behind, opposite, across = project(
+        keep, other, weights, peers, chunks
+    )
+    far = (pair, along(ahead_far, 1, 0), along(behind_far, -1, 0))
+    across = along(across, 0, 1)
+    near = (mine, along(ahead, 1, 0), along(behind, -1, 0))
     handed = []
-    for i, (start, size) in enumerate(chunks):
-        stay, across, ahead, behind = project(keep, other, weights, peers, start, size)
-        from_z = along(across, 0, 1)
-        from_last = along(ahead, 1, 0)
-        from_next = along(behind, -1, 0)
-        opposite = add((stay, from_z), (2, 0), f"opposite_{i}")
-        from_opposite = along(opposite[None], 2, 0)
-        pair = add((stay, from_last, from_next), (1, 1, 1), f"pair_{i}")
-        from_pair = along(pair[None], 0, 1)
-        terms = (stay, from_last, from_next, from_opposite, from_pair)
-        updated = update(terms, packed[2 * i], packed[2 * i + 1], f"update_{i}")
+    turn = keep
+    offset = 0
+    width = mine.shape[2]
+    sums = add(far, keep, ((0, 0),) * 3, width, "pair")
+    from_pair = along(sums, 0, 1)
+    sums = add((opposite, across), sums, ((0, 0),) * 2, width, "opposite")
+    from_opposite = along(sums, 2, 0)
+    for i, (_, size) in enumerate(chunks):
+        width = packed_width(size, tok)
+        updated = update(
+            (*near, from_pair, from_opposite),
+            ((0, offset),) * 5,
+            packed[2 * i],
+            packed[2 * i + 1],
+            f"update_{i}",
+        )
         handed.append(lax.ppermute(updated, "section", forward))
+        offset += width
     return unpack(handed, tok, columns, chunks)[None]
 
 

time: 67.5 us -> 64.9 us (0.961); the launches traced: 67.3 us -> 63.8 us
  starting transfers between devices: 27.4 us -> 23.3 us
  waiting for transfers between devices: 18.7 us -> 19.9 us
  Pallas kernels: 13.6 us -> 12.9 us
    ppermute x10 -> x7, starting transfers between devices: 14.4 us -> 10.1 us  [along(): return lax.ppermute(x, 'head', route)]
    ppermute x10 -> x7, waiting for transfers between devices: 5.87 us -> 7.97 us  [along(): return lax.ppermute(x, 'head', route)]
    ppermute x2, waiting for transfers between devices: 9.29 us -> 8.43 us  [shards(): handed.append(lax.ppermute(updated, 'section', forward))]
    pallas_call x4 -> x3, Pallas kernels: 2.46 us -> 1.9 us  [the longest x1 1.7 us: project(): pl.pallas_call(functools.partial(project_kernel, chunks=chunks), in_specs...]
  transfers between devices with their start and end apart: 15 -> 12, of which waited for: 7 -> 6; matrix products, arithmetic and copies ran while one was open for 10% -> 11% of each run, Pallas kernels for 8% -> 6%
where the time goes in v6:
time: 64.9 us; the launch traced here: 63.8 us
  starting transfers between devices  23.3 us (36%)
  waiting for transfers between devices  19.9 us (31%)
  Pallas kernels  12.9 us (20%)
  local copies, waits for them, and re-layouts  6.8 us (10%)
  between operations  0.73 us (1%)
    ppermute x7, starting transfers between devices, along(): return lax.ppermute(x, 'head', route)  10.1 us
    ppermute x2, waiting for transfers between devices, shards(): handed.append(lax.ppermute(updated, 'section', forward))  8.43 us
    ppermute x7, waiting for transfers between devices, along(): return lax.ppermute(x, 'head', route)  7.97 us
    ppermute x2, starting transfers between devices, shards(): handed.append(lax.ppermute(updated, 'section', forward))  7 us
    unnamed x5, local copies, waits for them, and re-layouts  6.8 us
    pallas_call x1, Pallas kernels, attend(): pl.pallas_call(functools.partial(attend_kernel, heads=heads, chunk=keys /...  6.21 us
    all_to_all x1, starting transfers between devices, shards(): lax.all_to_all(blocked, 'head', split_axis=0, concat_axis=0, tiled=True)  6.07 us
    all_to_all x1, waiting for transfers between devices, shards(): lax.all_to_all(blocked, 'head', split_axis=0, concat_axis=0, tiled=True)  2.32 us
  transfers between devices with their start and end apart: 12, of which 6 were waited for; matrix products, arithmetic and copies ran while one was open for 11% of the time, Pallas kernels for 6%

profile of v6, /device:TPU:32, one launch (start us, length us, event | category | flops | bytes accessed | tf_op | source)
XLA Modules:
  0.0 63.8 jit_solution(4921874302771715107)
XLA Ops:
  0.0 0.0 collective-permute-start
  0.0 2.2 %pack.1 = bf16[16,54,384]{2,1,0:T(8,128)(2,1)} custom-call(bf16[1,18,3,6144]{3,2,1,0:T(4,128)(2,1)} %qkv.1), custom_call_target="tpu_custom_call" | custom-call | tf_op jit(solution)/shard_map/pack/pallas_call | solution.py:66
  2.2 6.1 %all-to-all-start = ((bf16[16,54,384]{2,1,0:T(8,128)(2,1)}), bf16[16,54,384]{2,1,0:T(8,128)(2,1)S(1)}, u32[]{:S(2)}, u32[]{:S(2)}) async-start(bf16[16,54,384]{2,1,0:T(8,128)(2,1)} %pack.1), calls=%async_computation | async-start | bytes 1376256 | tf_op jit(solution)/shard_map/all_to_all | solution.py:383
  8.3 6.8 %copy.10 = bf16[1,4608,2,384]{3,1,2,0:T(8,128)(2,1)} copy(bf16[1,4608,2,384]{3,2,1,0:T(2,128)(2,1)} %param.7) | data formatting | bytes 14155776 | tf_op args[1]
  15.1 1.6 %prefetch.1.first_in = bf16[2,4608,128]{2,1,0:T(8,128)(2,1)S(1)} custom-call(bf16[2,4608,384]{2,1,0:T(8,128)(2,1)} %bitcast.10), custom_call_target="tpu_custom_call" | custom-call | tf_op jit(solution)/shard_map/prefetch/pallas_call | solution.py:126
  17.4 0.1 pad_add_fusion.scalars
  17.5 2.3 %all-to-all-done.arrived = bf16[16,54,384]{2,1,0:T(8,128)(2,1)S(1)} async-done(((bf16[16,54,384]{2,1,0:T(8,128)(2,1)}), bf16[16,54,384]{2,1,0:T(8,128)(2,1)S(1)}, u32[]{:S(2)}, u32[]{:S(2)}) %all-to-all-start) | async-done | bytes 663584 | tf_op jit(solution)/shard_map/all_to_all | solution.py:383
  19.8 0.0 collective-permute-done.w_other
  19.8 6.2 %attend.1 = (bf16[144,384]{1,0:T(8,128)(2,1)S(1)}, bf16[144,384]{1,0:T(8,128)(2,1)S(1)}, bf16[2,384,6144]{2,1,0:T(8,128)(2,1)S(1)}, bf16[2,4608,128]{2,1,0:T(8,128)(2,1)S(1)}) custom-call(s32[2]{0:T(128)S(1)} %pad_add_fusion.scalars, bf16[16,54,384]{2,1,0:T(8,128)(2,1)S(1)} %all-to-all-done.arrived, ...), custom_call_target="tpu_custom_call", output_to_operand_aliasing={{3}: (2, {})} | custom-call | tf_op jit(solution)/shard_map/attend/pallas_call | solution.py:228
  26.0 0.2 collective-permute-start.1
  26.2 1.2 %collective-permute-done.1.other = bf16[144,384]{1,0:T(8,128)(2,1)S(1)} collective-permute-done((bf16[144,384]{1,0:T(8,128)(2,1)S(1)}, bf16[144,384]{1,0:T(8,128)(2,1)S(1)}, u32[]{:S(2)}, u32[]{:S(2)}) %collective-permute-start.1) | collective-permute-done | bytes 110624 | tf_op jit(solution)/shard_map/ppermute | solution.py:387
  27.4 0.0 copy-start
  27.4 0.0 copy-start.1
  27.4 1.7 %project.1 = (bf16[1,16,6912]{2,1,0:T(8,128)(2,1)S(1)}, bf16[1,16,6912]{2,1,0:T(8,128)(2,1)S(1)}, bf16[1,16,6912]{2,1,0:T(8,128)(2,1)S(1)}, bf16[1,16,6912]{2,1,...) custom-call(bf16[144,384]{1,0:T(8,128)(2,1)S(1)} %get-tuple-element., ...), custom_call_target="tpu_custom_call" | custom-call | tf_op jit(solution)/shard_map/project/pallas_call | solution.py:287
  29.1 0.1 collective-permute-start.4
  29.2 3.2 %collective-permute-start.5 = (bf16[1,16,6912]{2,1,0:T(8,128)(2,1)S(1)}, bf16[1,16,6912]{2,1,0:T(8,128)(2,1)S(1)}, u32[]{:S(2)}, u32[]{:S(2)}) collective-permute-start(bf16[1,16,6912]{2,1,0:T(8,128)(2,1)S(1)} %get-tuple-element.28), channel_id=1, source_target_pairs={{0,12},{1,13},{2,14},{3,15},{4,0},{5,1},{6,2},{7,3},{8,4},{9,5},{1... | collective-permute-start | bytes 663560 | tf_op jit(solution)/shard_map/ppermute | solution.py:393
  32.5 1.3 %collective-permute-start.7 = (bf16[1,16,6912]{2,1,0:T(8,128)(2,1)S(1)}, bf16[1,16,6912]{2,1,0:T(8,128)(2,1)S(1)}, u32[]{:S(2)}, u32[]{:S(2)}) collective-permute-start(bf16[1,16,6912]{2,1,0:T(8,128)(2,1)S(1)} %get-tuple-element.30), channel_id=1, source_target_pairs={{0,2},{1,3},{2,0},{3,1},{4,6},{5,7},{6,4},{7,5},{8,10},{9,11},{10,... | collective-permute-start | bytes 663560 | tf_op jit(solution)/shard_map/ppermute | solution.py:393
  33.7 0.0 collective-permute-start.2
  33.7 3.2 %collective-permute-start.3 = (bf16[1,16,6912]{2,1,0:T(8,128)(2,1)S(1)}, bf16[1,16,6912]{2,1,0:T(8,128)(2,1)S(1)}, u32[]{:S(2)}, u32[]{:S(2)}) collective-permute-start(bf16[1,16,6912]{2,1,0:T(8,128)(2,1)S(1)} %get-tuple-element.25), channel_id=1, source_target_pairs={{0,12},{1,13},{2,14},{3,15},{4,0},{5,1},{6,2},{7,3},{8,4},{9,5},{1... | collective-permute-start | bytes 663560 | tf_op jit(solution)/shard_map/ppermute | solution.py:393
  37.0 1.7 %collective-permute-done.4.refs_1_ = bf16[1,16,6912]{2,1,0:T(8,128)(2,1)S(1)} collective-permute-done((bf16[1,16,6912]{2,1,0:T(8,128)(2,1)S(1)}, bf16[1,16,6912]{2,1,0:T(8,128)(2,1)S(1)}, u32[]{:S(2)}, u32[]{:S(2)}) %collective-permute-start.4) | collective-permute-done | bytes 221216 | tf_op jit(solution)/shard_map/ppermute | solution.py:393
  38.7 0.0 collective-permute-done.5.refs_2_
  38.7 0.1 pair.1.refs_2_
  38.8 0.6 collective-permute-done.7.refs_1_
  39.4 0.1 opposite.1
  39.4 1.0 %collective-permute-start.8 = (bf16[1,16,6912]{2,1,0:T(8,128)(2,1)S(1)}, bf16[1,16,6912]{2,1,0:T(8,128)(2,1)S(1)}, u32[]{:S(2)}, u32[]{:S(2)}) collective-permute-start(bf16[1,16,6912]{2,1,0:T(8,128)(2,1)S(1)} %opposite.1), channel_id=1, source_target_pairs={{0,8},{1,9},{2,10},{3,11},{4,12},{5,13},{6,14},{7,15},{8,0},{9,1},... | collective-permute-start | bytes 663560 | tf_op jit(solution)/shard_map/ppermute | solution.py:393
  40.4 1.3 %collective-permute-start.6 = (bf16[1,16,6912]{2,1,0:T(8,128)(2,1)S(1)}, bf16[1,16,6912]{2,1,0:T(8,128)(2,1)S(1)}, u32[]{:S(2)}, u32[]{:S(2)}) collective-permute-start(bf16[1,16,6912]{2,1,0:T(8,128)(2,1)S(1)} %pair.1.refs_2_), channel_id=1, source_target_pairs={{0,2},{1,3},{2,0},{3,1},{4,6},{5,7},{6,4},{7,5},{8,10},{9,11},{10,... | collective-permute-start | bytes 663560 | tf_op jit(solution)/shard_map/ppermute | solution.py:393
  41.7 0.0 copy-done
  41.7 0.0 copy-done.1
  41.7 0.1 stream.1
  41.8 5.6 %collective-permute-done.2.refs_1_ = bf16[1,16,6912]{2,1,0:T(8,128)(2,1)S(1)} collective-permute-done((bf16[1,16,6912]{2,1,0:T(8,128)(2,1)S(1)}, bf16[1,16,6912]{2,1,0:T(8,128)(2,1)S(1)}, u32[]{:S(2)}, u32[]{:S(2)}) %collective-permute-start.2) | collective-permute-done | bytes 221216 | tf_op jit(solution)/shard_map/ppermute | solution.py:393
  47.4 0.0 collective-permute-done.3.refs_2_
  47.4 0.0 collective-permute-done.8.refs_4_
  47.4 0.0 collective-permute-done.6.refs_3_
  47.4 0.1 update_1.1
  47.5 3.3 %collective-permute-start.10 = (bf16[16,4608]{1,0:T(8,128)(2,1)S(1)}, bf16[16,4608]{1,0:T(8,128)(2,1)S(1)}, u32[]{:S(2)}, u32[]{:S(2)}) collective-permute-start(bf16[16,4608]{1,0:T(8,128)(2,1)S(1)} %update_1.1), channel_id=1, source_target_pairs={{0,16},{16,32},{32,48},{48,64},{64,80},{80,96},{96,112},{112,128},... | collective-permute-start | bytes 442376 | tf_op jit(solution)/shard_map/ppermute | solution.py:418
  50.9 0.1 update_0.1
  50.9 3.7 %collective-permute-start.9 = (bf16[16,2304]{1,0:T(8,128)(2,1)S(1)}, bf16[16,2304]{1,0:T(8,128)(2,1)S(1)}, u32[]{:S(2)}, u32[]{:S(2)}) collective-permute-start(bf16[16,2304]{1,0:T(8,128)(2,1)S(1)} %update_0.1), channel_id=1, source_target_pairs={{0,16},{16,32},{32,48},{48,64},{64,80},{80,96},{96,112},{112,128},... | collective-permute-start | bytes 221192 | tf_op jit(solution)/shard_map/ppermute | solution.py:418
  54.6 8.4 %collective-permute-done.9.refs_0_ = bf16[16,2304]{1,0:T(8,128)(2,1)S(1)} collective-permute-done((bf16[16,2304]{1,0:T(8,128)(2,1)S(1)}, bf16[16,2304]{1,0:T(8,128)(2,1)S(1)}, u32[]{:S(2)}, u32[]{:S(2)}) %collective-permute-start.9) | collective-permute-done | bytes 73760 | tf_op jit(solution)/shard_map/ppermute | solution.py:418
  63.0 0.0 collective-permute-done.10.refs_1_
  63.0 0.7 %unpack.1 = bf16[18,6144]{1,0:T(8,128)(2,1)} custom-call(bf16[16,2304]{1,0:T(8,128)(2,1)S(1)} %collective-permute-done.9.refs_0_, bf16[16,4608]{1,0:T(8,128)(2,1)S(1)} %collective-permute-done.10.refs_1_), custom_call_target="tpu_custom_call" | custom-call | tf_op jit(solution)/shard_map/unpack/pallas_call | solution.py:357
Async XLA Ops:
  0.0 19.8 %collective-permute-start = (bf16[384,6144]{1,0:T(8,128)(2,1)}, bf16[384,6144]{1,0:T(8,128)(2,1)}, u32[]{:S(2)}, u32[]{:S(2)}) collective-permute-start(bf16[384,6144]{1,0:T(8,128)(2,1)} %bitcast.12), channel_id=1, source_target_pairs={{0,1},{1,0},{2,3},{3,2},{4,5},{5,4},{6,7},{7,6},{8,9},{9,8},{10,11... | collective-permute-start | bytes 14155784 | tf_op jit(solution)/shard_map/ppermute | solution.py:381
  2.2 17.6 %all-to-all-start = ((bf16[16,54,384]{2,1,0:T(8,128)(2,1)}), bf16[16,54,384]{2,1,0:T(8,128)(2,1)S(1)}, u32[]{:S(2)}, u32[]{:S(2)}) async-start(bf16[16,54,384]{2,1,0:T(8,128)(2,1)} %pack.1), calls=%async_computation | async-start | bytes 1376256 | tf_op jit(solution)/shard_map/all_to_all | solution.py:383
  26.0 1.4 %collective-permute-start.1 = (bf16[144,384]{1,0:T(8,128)(2,1)S(1)}, bf16[144,384]{1,0:T(8,128)(2,1)S(1)}, u32[]{:S(2)}, u32[]{:S(2)}) collective-permute-start(bf16[144,384]{1,0:T(8,128)(2,1)S(1)} %get-tuple-element.21), channel_id=1, source_target_pairs={{0,1},{1,0},{2,3},{3,2},{4,5},{5,4},{6,7},{7,6},{8,9},{9,8},{10,11... | collective-permute-start | bytes 331784 | tf_op jit(solution)/shard_map/ppermute | solution.py:387
  27.4 14.3 %copy-start = (bf16[1,18,6144]{2,1,0:T(8,128)(2,1)S(1)}, bf16[1,18,6144]{2,1,0:T(8,128)(2,1)}, u32[]{:S(2)}) copy-start(bf16[1,18,6144]{2,1,0:T(8,128)(2,1)} %param.9) | copy-start | bytes 663556
  27.4 14.3 %copy-start.1 = (f32[1,6144]{1,0:T(1,128)S(1)}, f32[1,6144]{1,0:T(1,128)}, u32[]{:S(2)}) copy-start(f32[1,6144]{1,0:T(1,128)} %gate.1) | copy-start | bytes 73732
  29.1 9.6 %collective-permute-start.4 = (bf16[1,16,6912]{2,1,0:T(8,128)(2,1)S(1)}, bf16[1,16,6912]{2,1,0:T(8,128)(2,1)S(1)}, u32[]{:S(2)}, u32[]{:S(2)}) collective-permute-start(bf16[1,16,6912]{2,1,0:T(8,128)(2,1)S(1)} %get-tuple-element.27), channel_id=1, source_target_pairs={{0,4},{1,5},{2,6},{3,7},{4,8},{5,9},{6,10},{7,11},{8,12},{9,13},{1... | collective-permute-start | bytes 663560 | tf_op jit(solution)/shard_map/ppermute | solution.py:393
  29.2 9.5 %collective-permute-start.5 = (bf16[1,16,6912]{2,1,0:T(8,128)(2,1)S(1)}, bf16[1,16,6912]{2,1,0:T(8,128)(2,1)S(1)}, u32[]{:S(2)}, u32[]{:S(2)}) collective-permute-start(bf16[1,16,6912]{2,1,0:T(8,128)(2,1)S(1)} %get-tuple-element.28), channel_id=1, source_target_pairs={{0,12},{1,13},{2,14},{3,15},{4,0},{5,1},{6,2},{7,3},{8,4},{9,5},{1... | collective-permute-start | bytes 663560 | tf_op jit(solution)/shard_map/ppermute | solution.py:393
  32.5 6.9 %collective-permute-start.7 = (bf16[1,16,6912]{2,1,0:T(8,128)(2,1)S(1)}, bf16[1,16,6912]{2,1,0:T(8,128)(2,1)S(1)}, u32[]{:S(2)}, u32[]{:S(2)}) collective-permute-start(bf16[1,16,6912]{2,1,0:T(8,128)(2,1)S(1)} %get-tuple-element.30), channel_id=1, source_target_pairs={{0,2},{1,3},{2,0},{3,1},{4,6},{5,7},{6,4},{7,5},{8,10},{9,11},{10,... | collective-permute-start | bytes 663560 | tf_op jit(solution)/shard_map/ppermute | solution.py:393
  33.7 13.7 %collective-permute-start.2 = (bf16[1,16,6912]{2,1,0:T(8,128)(2,1)S(1)}, bf16[1,16,6912]{2,1,0:T(8,128)(2,1)S(1)}, u32[]{:S(2)}, u32[]{:S(2)}) collective-permute-start(bf16[1,16,6912]{2,1,0:T(8,128)(2,1)S(1)} %get-tuple-element.24), channel_id=1, source_target_pairs={{0,4},{1,5},{2,6},{3,7},{4,8},{5,9},{6,10},{7,11},{8,12},{9,13},{1... | collective-permute-start | bytes 663560 | tf_op jit(solution)/shard_map/ppermute | solution.py:393
  33.7 13.7 %collective-permute-start.3 = (bf16[1,16,6912]{2,1,0:T(8,128)(2,1)S(1)}, bf16[1,16,6912]{2,1,0:T(8,128)(2,1)S(1)}, u32[]{:S(2)}, u32[]{:S(2)}) collective-permute-start(bf16[1,16,6912]{2,1,0:T(8,128)(2,1)S(1)} %get-tuple-element.25), channel_id=1, source_target_pairs={{0,12},{1,13},{2,14},{3,15},{4,0},{5,1},{6,2},{7,3},{8,4},{9,5},{1... | collective-permute-start | bytes 663560 | tf_op jit(solution)/shard_map/ppermute | solution.py:393
  39.4 8.0 %collective-permute-start.8 = (bf16[1,16,6912]{2,1,0:T(8,128)(2,1)S(1)}, bf16[1,16,6912]{2,1,0:T(8,128)(2,1)S(1)}, u32[]{:S(2)}, u32[]{:S(2)}) collective-permute-start(bf16[1,16,6912]{2,1,0:T(8,128)(2,1)S(1)} %opposite.1), channel_id=1, source_target_pairs={{0,8},{1,9},{2,10},{3,11},{4,12},{5,13},{6,14},{7,15},{8,0},{9,1},... | collective-permute-start | bytes 663560 | tf_op jit(solution)/shard_map/ppermute | solution.py:393
  40.4 7.0 %collective-permute-start.6 = (bf16[1,16,6912]{2,1,0:T(8,128)(2,1)S(1)}, bf16[1,16,6912]{2,1,0:T(8,128)(2,1)S(1)}, u32[]{:S(2)}, u32[]{:S(2)}) collective-permute-start(bf16[1,16,6912]{2,1,0:T(8,128)(2,1)S(1)} %pair.1.refs_2_), channel_id=1, source_target_pairs={{0,2},{1,3},{2,0},{3,1},{4,6},{5,7},{6,4},{7,5},{8,10},{9,11},{10,... | collective-permute-start | bytes 663560 | tf_op jit(solution)/shard_map/ppermute | solution.py:393
  47.5 15.5 %collective-permute-start.10 = (bf16[16,4608]{1,0:T(8,128)(2,1)S(1)}, bf16[16,4608]{1,0:T(8,128)(2,1)S(1)}, u32[]{:S(2)}, u32[]{:S(2)}) collective-permute-start(bf16[16,4608]{1,0:T(8,128)(2,1)S(1)} %update_1.1), channel_id=1, source_target_pairs={{0,16},{16,32},{32,48},{48,64},{64,80},{80,96},{96,112},{112,128},... | collective-permute-start | bytes 442376 | tf_op jit(solution)/shard_map/ppermute | solution.py:418
  50.9 12.1 %collective-permute-start.9 = (bf16[16,2304]{1,0:T(8,128)(2,1)S(1)}, bf16[16,2304]{1,0:T(8,128)(2,1)S(1)}, u32[]{:S(2)}, u32[]{:S(2)}) collective-permute-start(bf16[16,2304]{1,0:T(8,128)(2,1)S(1)} %update_0.1), channel_id=1, source_target_pairs={{0,16},{16,32},{32,48},{48,64},{64,80},{80,96},{96,112},{112,128},... | collective-permute-start | bytes 221192 | tf_op jit(solution)/shard_map/ppermute | solution.py:418

commit v7 on v6

--- a/solution.py
+++ b/solution.py
@@ -55,13 +55,13 @@
 
 
 def pieces_out(groups):
-    return 4 if groups % 4 == 0 else 1
+    return 8 if groups % 8 == 0 else 1
 
 
 def pack(qkv, groups):
     _, tok, _, columns = qkv.shape
     shape = (groups, 3 * tok, columns // groups)
-    pieces = 3 if tok % 3 == 0 else 1
+    pieces = 6 if tok % 6 == 0 else 1
     anywhere = pl.BlockSpec(memory_space=pl.ANY)
     return pl.pallas_call(
         functools.partial(pack_kernel, pieces=pieces),

time: 64.9 us -> 65 us (level)
  transfers between devices with their start and end apart: 12 -> 12, of which waited for: 6 -> 6; matrix products, arithmetic and copies ran while one was open for 11% -> 11% of each run, Pallas kernels for 6% -> 7%
where the time goes in v7:
time: 65 us; the launch traced here: 63.9 us
  starting transfers between devices  23.3 us (36%)
  waiting for transfers between devices  19.9 us (31%)
  Pallas kernels  13 us (20%)
  local copies, waits for them, and re-layouts  6.8 us (10%)
  between operations  0.73 us (1%)
    ppermute x7, starting transfers between devices, along(): return lax.ppermute(x, 'head', route)  10.1 us
    ppermute x2, waiting for transfers between devices, shards(): handed.append(lax.ppermute(updated, 'section', forward))  8.43 us
    ppermute x7, waiting for transfers between devices, along(): return lax.ppermute(x, 'head', route)  7.97 us
    ppermute x2, starting transfers between devices, shards(): handed.append(lax.ppermute(updated, 'section', forward))  7.01 us
    unnamed x5, local copies, waits for them, and re-layouts  6.8 us
    pallas_call x1, Pallas kernels, attend(): pl.pallas_call(functools.partial(attend_kernel, heads=heads, chunk=keys /...  6.21 us
    all_to_all x1, starting transfers between devices, shards(): lax.all_to_all(blocked, 'head', split_axis=0, concat_axis=0, tiled=True)  6.07 us
    all_to_all x1, waiting for transfers between devices, shards(): lax.all_to_all(blocked, 'head', split_axis=0, concat_axis=0, tiled=True)  2.32 us
  transfers between devices with their start and end apart: 12, of which 6 were waited for; matrix products, arithmetic and copies ran while one was open for 11% of the time, Pallas kernels for 7%

profile of v7, /device:TPU:32, one launch (start us, length us, event | category | flops | bytes accessed | tf_op | source)
XLA Modules:
  0.0 63.9 jit_solution(17952754353594157928)
XLA Ops:
  0.0 0.0 collective-permute-start
  0.0 2.3 %pack.1 = bf16[16,54,384]{2,1,0:T(8,128)(2,1)} custom-call(bf16[1,18,3,6144]{3,2,1,0:T(4,128)(2,1)} %qkv.1), custom_call_target="tpu_custom_call" | custom-call | tf_op jit(solution)/shard_map/pack/pallas_call | solution.py:66
  2.3 6.1 %all-to-all-start = ((bf16[16,54,384]{2,1,0:T(8,128)(2,1)}), bf16[16,54,384]{2,1,0:T(8,128)(2,1)S(1)}, u32[]{:S(2)}, u32[]{:S(2)}) async-start(bf16[16,54,384]{2,1,0:T(8,128)(2,1)} %pack.1), calls=%async_computation | async-start | bytes 1376256 | tf_op jit(solution)/shard_map/all_to_all | solution.py:383
  8.4 6.8 %copy.10 = bf16[1,4608,2,384]{3,1,2,0:T(8,128)(2,1)} copy(bf16[1,4608,2,384]{3,2,1,0:T(2,128)(2,1)} %param.7) | data formatting | bytes 14155776 | tf_op args[1]
  15.2 1.6 %prefetch.1.first_in = bf16[2,4608,128]{2,1,0:T(8,128)(2,1)S(1)} custom-call(bf16[2,4608,384]{2,1,0:T(8,128)(2,1)} %bitcast.10), custom_call_target="tpu_custom_call" | custom-call | tf_op jit(solution)/shard_map/prefetch/pallas_call | solution.py:126
  17.5 0.1 pad_add_fusion.scalars
  17.6 2.3 %all-to-all-done.arrived = bf16[16,54,384]{2,1,0:T(8,128)(2,1)S(1)} async-done(((bf16[16,54,384]{2,1,0:T(8,128)(2,1)}), bf16[16,54,384]{2,1,0:T(8,128)(2,1)S(1)}, u32[]{:S(2)}, u32[]{:S(2)}) %all-to-all-start) | async-done | bytes 663584 | tf_op jit(solution)/shard_map/all_to_all | solution.py:383
  19.9 0.0 collective-permute-done.w_other
  19.9 6.2 %attend.1 = (bf16[144,384]{1,0:T(8,128)(2,1)S(1)}, bf16[144,384]{1,0:T(8,128)(2,1)S(1)}, bf16[2,384,6144]{2,1,0:T(8,128)(2,1)S(1)}, bf16[2,4608,128]{2,1,0:T(8,128)(2,1)S(1)}) custom-call(s32[2]{0:T(128)S(1)} %pad_add_fusion.scalars, bf16[16,54,384]{2,1,0:T(8,128)(2,1)S(1)} %all-to-all-done.arrived, ...), custom_call_target="tpu_custom_call", output_to_operand_aliasing={{3}: (2, {})} | custom-call | tf_op jit(solution)/shard_map/attend/pallas_call | solution.py:228
  26.1 0.2 collective-permute-start.1
  26.3 1.2 %collective-permute-done.1.other = bf16[144,384]{1,0:T(8,128)(2,1)S(1)} collective-permute-done((bf16[144,384]{1,0:T(8,128)(2,1)S(1)}, bf16[144,384]{1,0:T(8,128)(2,1)S(1)}, u32[]{:S(2)}, u32[]{:S(2)}) %collective-permute-start.1) | collective-permute-done | bytes 110624 | tf_op jit(solution)/shard_map/ppermute | solution.py:387
  27.5 0.0 copy-start
  27.5 0.0 copy-start.1
  27.5 1.7 %project.1 = (bf16[1,16,6912]{2,1,0:T(8,128)(2,1)S(1)}, bf16[1,16,6912]{2,1,0:T(8,128)(2,1)S(1)}, bf16[1,16,6912]{2,1,0:T(8,128)(2,1)S(1)}, bf16[1,16,6912]{2,1,...) custom-call(bf16[144,384]{1,0:T(8,128)(2,1)S(1)} %get-tuple-element., ...), custom_call_target="tpu_custom_call" | custom-call | tf_op jit(solution)/shard_map/project/pallas_call | solution.py:287
  29.2 0.1 collective-permute-start.4
  29.3 3.2 %collective-permute-start.5 = (bf16[1,16,6912]{2,1,0:T(8,128)(2,1)S(1)}, bf16[1,16,6912]{2,1,0:T(8,128)(2,1)S(1)}, u32[]{:S(2)}, u32[]{:S(2)}) collective-permute-start(bf16[1,16,6912]{2,1,0:T(8,128)(2,1)S(1)} %get-tuple-element.28), channel_id=1, source_target_pairs={{0,12},{1,13},{2,14},{3,15},{4,0},{5,1},{6,2},{7,3},{8,4},{9,5},{1... | collective-permute-start | bytes 663560 | tf_op jit(solution)/shard_map/ppermute | solution.py:393
  32.5 1.3 %collective-permute-start.7 = (bf16[1,16,6912]{2,1,0:T(8,128)(2,1)S(1)}, bf16[1,16,6912]{2,1,0:T(8,128)(2,1)S(1)}, u32[]{:S(2)}, u32[]{:S(2)}) collective-permute-start(bf16[1,16,6912]{2,1,0:T(8,128)(2,1)S(1)} %get-tuple-element.30), channel_id=1, source_target_pairs={{0,2},{1,3},{2,0},{3,1},{4,6},{5,7},{6,4},{7,5},{8,10},{9,11},{10,... | collective-permute-start | bytes 663560 | tf_op jit(solution)/shard_map/ppermute | solution.py:393
  33.8 0.0 collective-permute-start.2
  33.8 3.2 %collective-permute-start.3 = (bf16[1,16,6912]{2,1,0:T(8,128)(2,1)S(1)}, bf16[1,16,6912]{2,1,0:T(8,128)(2,1)S(1)}, u32[]{:S(2)}, u32[]{:S(2)}) collective-permute-start(bf16[1,16,6912]{2,1,0:T(8,128)(2,1)S(1)} %get-tuple-element.25), channel_id=1, source_target_pairs={{0,12},{1,13},{2,14},{3,15},{4,0},{5,1},{6,2},{7,3},{8,4},{9,5},{1... | collective-permute-start | bytes 663560 | tf_op jit(solution)/shard_map/ppermute | solution.py:393
  37.0 1.7 %collective-permute-done.4.refs_1_ = bf16[1,16,6912]{2,1,0:T(8,128)(2,1)S(1)} collective-permute-done((bf16[1,16,6912]{2,1,0:T(8,128)(2,1)S(1)}, bf16[1,16,6912]{2,1,0:T(8,128)(2,1)S(1)}, u32[]{:S(2)}, u32[]{:S(2)}) %collective-permute-start.4) | collective-permute-done | bytes 221216 | tf_op jit(solution)/shard_map/ppermute | solution.py:393
  38.8 0.0 collective-permute-done.5.refs_2_
  38.8 0.1 pair.1.refs_2_
  38.9 0.6 collective-permute-done.7.refs_1_
  39.5 0.1 opposite.1
  39.5 1.0 %collective-permute-start.8 = (bf16[1,16,6912]{2,1,0:T(8,128)(2,1)S(1)}, bf16[1,16,6912]{2,1,0:T(8,128)(2,1)S(1)}, u32[]{:S(2)}, u32[]{:S(2)}) collective-permute-start(bf16[1,16,6912]{2,1,0:T(8,128)(2,1)S(1)} %opposite.1), channel_id=1, source_target_pairs={{0,8},{1,9},{2,10},{3,11},{4,12},{5,13},{6,14},{7,15},{8,0},{9,1},... | collective-permute-start | bytes 663560 | tf_op jit(solution)/shard_map/ppermute | solution.py:393
  40.5 1.3 %collective-permute-start.6 = (bf16[1,16,6912]{2,1,0:T(8,128)(2,1)S(1)}, bf16[1,16,6912]{2,1,0:T(8,128)(2,1)S(1)}, u32[]{:S(2)}, u32[]{:S(2)}) collective-permute-start(bf16[1,16,6912]{2,1,0:T(8,128)(2,1)S(1)} %pair.1.refs_2_), channel_id=1, source_target_pairs={{0,2},{1,3},{2,0},{3,1},{4,6},{5,7},{6,4},{7,5},{8,10},{9,11},{10,... | collective-permute-start | bytes 663560 | tf_op jit(solution)/shard_map/ppermute | solution.py:393
  41.8 0.0 copy-done
  41.8 0.0 copy-done.1
  41.8 0.1 stream.1
  41.8 5.6 %collective-permute-done.2.refs_1_ = bf16[1,16,6912]{2,1,0:T(8,128)(2,1)S(1)} collective-permute-done((bf16[1,16,6912]{2,1,0:T(8,128)(2,1)S(1)}, bf16[1,16,6912]{2,1,0:T(8,128)(2,1)S(1)}, u32[]{:S(2)}, u32[]{:S(2)}) %collective-permute-start.2) | collective-permute-done | bytes 221216 | tf_op jit(solution)/shard_map/ppermute | solution.py:393
  47.5 0.0 collective-permute-done.3.refs_2_
  47.5 0.0 collective-permute-done.8.refs_4_
  47.5 0.0 collective-permute-done.6.refs_3_
  47.5 0.1 update_1.1
  47.6 3.4 %collective-permute-start.10 = (bf16[16,4608]{1,0:T(8,128)(2,1)S(1)}, bf16[16,4608]{1,0:T(8,128)(2,1)S(1)}, u32[]{:S(2)}, u32[]{:S(2)}) collective-permute-start(bf16[16,4608]{1,0:T(8,128)(2,1)S(1)} %update_1.1), channel_id=1, source_target_pairs={{0,16},{16,32},{32,48},{48,64},{64,80},{80,96},{96,112},{112,128},... | collective-permute-start | bytes 442376 | tf_op jit(solution)/shard_map/ppermute | solution.py:418
  51.0 0.1 update_0.1
  51.0 3.7 %collective-permute-start.9 = (bf16[16,2304]{1,0:T(8,128)(2,1)S(1)}, bf16[16,2304]{1,0:T(8,128)(2,1)S(1)}, u32[]{:S(2)}, u32[]{:S(2)}) collective-permute-start(bf16[16,2304]{1,0:T(8,128)(2,1)S(1)} %update_0.1), channel_id=1, source_target_pairs={{0,16},{16,32},{32,48},{48,64},{64,80},{80,96},{96,112},{112,128},... | collective-permute-start | bytes 221192 | tf_op jit(solution)/shard_map/ppermute | solution.py:418
  54.7 8.4 %collective-permute-done.9.refs_0_ = bf16[16,2304]{1,0:T(8,128)(2,1)S(1)} collective-permute-done((bf16[16,2304]{1,0:T(8,128)(2,1)S(1)}, bf16[16,2304]{1,0:T(8,128)(2,1)S(1)}, u32[]{:S(2)}, u32[]{:S(2)}) %collective-permute-start.9) | collective-permute-done | bytes 73760 | tf_op jit(solution)/shard_map/ppermute | solution.py:418
  63.1 0.0 collective-permute-done.10.refs_1_
  63.1 0.7 %unpack.1 = bf16[18,6144]{1,0:T(8,128)(2,1)} custom-call(bf16[16,2304]{1,0:T(8,128)(2,1)S(1)} %collective-permute-done.9.refs_0_, bf16[16,4608]{1,0:T(8,128)(2,1)S(1)} %collective-permute-done.10.refs_1_), custom_call_target="tpu_custom_call" | custom-call | tf_op jit(solution)/shard_map/unpack/pallas_call | solution.py:357
Async XLA Ops:
  0.0 19.9 %collective-permute-start = (bf16[384,6144]{1,0:T(8,128)(2,1)}, bf16[384,6144]{1,0:T(8,128)(2,1)}, u32[]{:S(2)}, u32[]{:S(2)}) collective-permute-start(bf16[384,6144]{1,0:T(8,128)(2,1)} %bitcast.12), channel_id=1, source_target_pairs={{0,1},{1,0},{2,3},{3,2},{4,5},{5,4},{6,7},{7,6},{8,9},{9,8},{10,11... | collective-permute-start | bytes 14155784 | tf_op jit(solution)/shard_map/ppermute | solution.py:381
  2.3 17.6 %all-to-all-start = ((bf16[16,54,384]{2,1,0:T(8,128)(2,1)}), bf16[16,54,384]{2,1,0:T(8,128)(2,1)S(1)}, u32[]{:S(2)}, u32[]{:S(2)}) async-start(bf16[16,54,384]{2,1,0:T(8,128)(2,1)} %pack.1), calls=%async_computation | async-start | bytes 1376256 | tf_op jit(solution)/shard_map/all_to_all | solution.py:383
  26.1 1.4 %collective-permute-start.1 = (bf16[144,384]{1,0:T(8,128)(2,1)S(1)}, bf16[144,384]{1,0:T(8,128)(2,1)S(1)}, u32[]{:S(2)}, u32[]{:S(2)}) collective-permute-start(bf16[144,384]{1,0:T(8,128)(2,1)S(1)} %get-tuple-element.21), channel_id=1, source_target_pairs={{0,1},{1,0},{2,3},{3,2},{4,5},{5,4},{6,7},{7,6},{8,9},{9,8},{10,11... | collective-permute-start | bytes 331784 | tf_op jit(solution)/shard_map/ppermute | solution.py:387
  27.5 14.3 %copy-start = (bf16[1,18,6144]{2,1,0:T(8,128)(2,1)S(1)}, bf16[1,18,6144]{2,1,0:T(8,128)(2,1)}, u32[]{:S(2)}) copy-start(bf16[1,18,6144]{2,1,0:T(8,128)(2,1)} %param.9) | copy-start | bytes 663556
  27.5 14.3 %copy-start.1 = (f32[1,6144]{1,0:T(1,128)S(1)}, f32[1,6144]{1,0:T(1,128)}, u32[]{:S(2)}) copy-start(f32[1,6144]{1,0:T(1,128)} %gate.1) | copy-start | bytes 73732
  29.2 9.6 %collective-permute-start.4 = (bf16[1,16,6912]{2,1,0:T(8,128)(2,1)S(1)}, bf16[1,16,6912]{2,1,0:T(8,128)(2,1)S(1)}, u32[]{:S(2)}, u32[]{:S(2)}) collective-permute-start(bf16[1,16,6912]{2,1,0:T(8,128)(2,1)S(1)} %get-tuple-element.27), channel_id=1, source_target_pairs={{0,4},{1,5},{2,6},{3,7},{4,8},{5,9},{6,10},{7,11},{8,12},{9,13},{1... | collective-permute-start | bytes 663560 | tf_op jit(solution)/shard_map/ppermute | solution.py:393
  29.3 9.5 %collective-permute-start.5 = (bf16[1,16,6912]{2,1,0:T(8,128)(2,1)S(1)}, bf16[1,16,6912]{2,1,0:T(8,128)(2,1)S(1)}, u32[]{:S(2)}, u32[]{:S(2)}) collective-permute-start(bf16[1,16,6912]{2,1,0:T(8,128)(2,1)S(1)} %get-tuple-element.28), channel_id=1, source_target_pairs={{0,12},{1,13},{2,14},{3,15},{4,0},{5,1},{6,2},{7,3},{8,4},{9,5},{1... | collective-permute-start | bytes 663560 | tf_op jit(solution)/shard_map/ppermute | solution.py:393
  32.5 6.9 %collective-permute-start.7 = (bf16[1,16,6912]{2,1,0:T(8,128)(2,1)S(1)}, bf16[1,16,6912]{2,1,0:T(8,128)(2,1)S(1)}, u32[]{:S(2)}, u32[]{:S(2)}) collective-permute-start(bf16[1,16,6912]{2,1,0:T(8,128)(2,1)S(1)} %get-tuple-element.30), channel_id=1, source_target_pairs={{0,2},{1,3},{2,0},{3,1},{4,6},{5,7},{6,4},{7,5},{8,10},{9,11},{10,... | collective-permute-start | bytes 663560 | tf_op jit(solution)/shard_map/ppermute | solution.py:393
  33.8 13.7 %collective-permute-start.2 = (bf16[1,16,6912]{2,1,0:T(8,128)(2,1)S(1)}, bf16[1,16,6912]{2,1,0:T(8,128)(2,1)S(1)}, u32[]{:S(2)}, u32[]{:S(2)}) collective-permute-start(bf16[1,16,6912]{2,1,0:T(8,128)(2,1)S(1)} %get-tuple-element.24), channel_id=1, source_target_pairs={{0,4},{1,5},{2,6},{3,7},{4,8},{5,9},{6,10},{7,11},{8,12},{9,13},{1... | collective-permute-start | bytes 663560 | tf_op jit(solution)/shard_map/ppermute | solution.py:393
  33.8 13.7 %collective-permute-start.3 = (bf16[1,16,6912]{2,1,0:T(8,128)(2,1)S(1)}, bf16[1,16,6912]{2,1,0:T(8,128)(2,1)S(1)}, u32[]{:S(2)}, u32[]{:S(2)}) collective-permute-start(bf16[1,16,6912]{2,1,0:T(8,128)(2,1)S(1)} %get-tuple-element.25), channel_id=1, source_target_pairs={{0,12},{1,13},{2,14},{3,15},{4,0},{5,1},{6,2},{7,3},{8,4},{9,5},{1... | collective-permute-start | bytes 663560 | tf_op jit(solution)/shard_map/ppermute | solution.py:393
  39.5 8.0 %collective-permute-start.8 = (bf16[1,16,6912]{2,1,0:T(8,128)(2,1)S(1)}, bf16[1,16,6912]{2,1,0:T(8,128)(2,1)S(1)}, u32[]{:S(2)}, u32[]{:S(2)}) collective-permute-start(bf16[1,16,6912]{2,1,0:T(8,128)(2,1)S(1)} %opposite.1), channel_id=1, source_target_pairs={{0,8},{1,9},{2,10},{3,11},{4,12},{5,13},{6,14},{7,15},{8,0},{9,1},... | collective-permute-start | bytes 663560 | tf_op jit(solution)/shard_map/ppermute | solution.py:393
  40.5 7.0 %collective-permute-start.6 = (bf16[1,16,6912]{2,1,0:T(8,128)(2,1)S(1)}, bf16[1,16,6912]{2,1,0:T(8,128)(2,1)S(1)}, u32[]{:S(2)}, u32[]{:S(2)}) collective-permute-start(bf16[1,16,6912]{2,1,0:T(8,128)(2,1)S(1)} %pair.1.refs_2_), channel_id=1, source_target_pairs={{0,2},{1,3},{2,0},{3,1},{4,6},{5,7},{6,4},{7,5},{8,10},{9,11},{10,... | collective-permute-start | bytes 663560 | tf_op jit(solution)/shard_map/ppermute | solution.py:393
  47.6 15.5 %collective-permute-start.10 = (bf16[16,4608]{1,0:T(8,128)(2,1)S(1)}, bf16[16,4608]{1,0:T(8,128)(2,1)S(1)}, u32[]{:S(2)}, u32[]{:S(2)}) collective-permute-start(bf16[16,4608]{1,0:T(8,128)(2,1)S(1)} %update_1.1), channel_id=1, source_target_pairs={{0,16},{16,32},{32,48},{48,64},{64,80},{80,96},{96,112},{112,128},... | collective-permute-start | bytes 442376 | tf_op jit(solution)/shard_map/ppermute | solution.py:418
  51.0 12.1 %collective-permute-start.9 = (bf16[16,2304]{1,0:T(8,128)(2,1)S(1)}, bf16[16,2304]{1,0:T(8,128)(2,1)S(1)}, u32[]{:S(2)}, u32[]{:S(2)}) collective-permute-start(bf16[16,2304]{1,0:T(8,128)(2,1)S(1)} %update_0.1), channel_id=1, source_target_pairs={{0,16},{16,32},{32,48},{48,64},{64,80},{80,96},{96,112},{112,128},... | collective-permute-start | bytes 221192 | tf_op jit(solution)/shard_map/ppermute | solution.py:418
